TPU v7x, 32 devices: a whole 2x2x4 slice. The times are simulated.
32 devices in a mesh: sec: 4 (over y, x), fx: 4 (over z), fy: 2 (over core).
Axes of the slice: x: 2, y: 2, z: 4, core: 2. Of those that a mesh axis runs over, the one named last changes fastest.
Arguments:
- conn: int32 [4, 4, 2, 8, 2139], P('sec', 'fx', 'fy'), may hold values from 0 to 3071, as said below
- material: int32 [4, 4, 2, 2139], P('sec', 'fx', 'fy'), may hold values from 0 to 2
- side_nodes: int32 [4, 4, 2, 2, 96], P('sec', 'fx', 'fy'), may hold values from 0 to 3071, as said below
- rim_nodes: int32 [4, 4, 2, 2, 128], P('sec', 'fx', 'fy'), may hold values from 0 to 3071, as said below
- iface_node: int32 [4, 4, 2, 1536], P('sec', 'fx', 'fy'), may hold values from 0 to 3071, as said below
- face_of_row: int32 [4, 4, 3072], P('sec', 'fx'), may hold values from 0 to 3071, each once within a row
- conductivity: float32 [3], replicated, may hold values from 0.5 to 5
- capacity: float32 [3], replicated, may hold values from 0.5 to 2
- diag_part: float32 [4, 4, 2, 3072], P('sec', 'fx', 'fy'), may hold values from 0.2 to 1
- heat_source: float32 [4, 4, 2, 3072], P('sec', 'fx', 'fy'), may hold values from -6 to 6
- air_state: float32 [4, 96, 64, 512], P(None, 'sec', 'fy', 'fx'), may hold values from -6 to 6
Outputs:
- solid_temp: float32 [4, 4, 2, 3072], P('sec', 'fx', 'fy')
- air_next: float32 [4, 96, 64, 512], P(None, 'sec', 'fy', 'fx')
Inputs may be any that keep to these rules, and one draw needn't show every extreme that they name: Each tile has a structured grid of 32 x 24 x 4 nodes (width, height, thickness) numbered by its own permutation; column e of conn lists element e's corners, corner 4 a + 2 b + c at thickness offset a, height offset b, width offset c; the columns run in order of corner 0's thickness, then height, then width position. `side_nodes`: row 0 holds the nodes at the lowest width position, row 1 at the highest, both ordered by thickness then height, so that position k of one tile's row 1 is the same physical node as position k of the next tile's row 0. `rim_nodes`: row 0 holds the nodes at the lowest height position, row 1 at the highest, both ordered by thickness then width, matching between tiles in the same way. `iface_node`: distinct nodes within a tile.
All inputs are finite; a program needn't handle non-finite values.
Results may differ from a plain program's by a relative error of at most 0.0001.
Values sent between devices are 32-bit elements; how exact they have to be, the bound alone decides.
No kernel may reach another device: no remote copies, remote signals or barrier semaphores. Data moves between devices by JAX's collectives and lax.ppermute only.
A program may use at most 64 MiB of HBM per device.

v0:
```python
import jax
import jax.numpy as jnp
import numpy as np
from jax import lax
from jax.sharding import PartitionSpec as P

NW = 32
NH = 24
NT = 4
ITERS = 4


time_step = 0.2
viscosity = 0.75


def extended_2(cells, sides, width):
    for axis, dim in sides:
        count = lax.axis_size(axis)
        ends = count - 1
        head = lax.slice_in_dim(cells, 0, width, axis=dim)
        tail = lax.slice_in_dim(cells, cells.shape[dim] - width, cells.shape[dim], axis=dim)
        cells = jnp.concatenate(
            [
                lax.ppermute(tail, axis, [(i, (i + 1) % count) for i in range(ends)]),
                cells,
                lax.ppermute(head, axis, [((i + 1) % count, i) for i in range(ends)]),
            ],
            axis=dim,
        )
    return cells


def unit_stiffness():
    table = np.zeros((8, 8), np.float32)
    for row_id in range(8):
        for col_id in range(8):
            differ = row_id ^ col_id
            bits = (differ & 1) + (differ >> 1 & 1) + (differ >> 2 & 1)
            if bits == 0:
                table[row_id, col_id] = 1.0 / 3.0
            elif bits == 1:
                table[row_id, col_id] = 0.0
            else:
                table[row_id, col_id] = -1.0 / 12.0
    return table


def advance(padded):
    centre = padded[:, 1:-1, 1:-1, 1:-1]
    vel_x = centre[1]
    vel_y = centre[2]
    vel_z = centre[3]
    fields = []
    for field_id in range(4):
        layer = padded[field_id]
        middle = centre[field_id]
        east = layer[1:-1, 1:-1, 2:]
        west = layer[1:-1, 1:-1, :-2]
        north = layer[1:-1, 2:, 1:-1]
        south = layer[1:-1, :-2, 1:-1]
        upper = layer[2:, 1:-1, 1:-1]
        lower = layer[:-2, 1:-1, 1:-1]
        transport = (
            vel_x * (east - west) * 0.5
            + vel_y * (north - south) * 0.5
            + vel_z * (upper - lower) * 0.5
        )
        spread = east + west + north + south + upper + lower - 6.0 * middle
        fields.append(middle - time_step * transport + time_step * viscosity * spread)
    return jnp.stack(fields)


def on_device(
    conn,
    material,
    side_nodes,
    rim_nodes,
    iface_node,
    face_of_row,
    conductivity,
    capacity,
    diag_part,
    heat_source,
    air_state,
):
    links = conn[0, 0, 0]
    kinds = material[0, 0, 0]
    thick_n = 2
    node_count = diag_part.shape[-1]
    width_n = NW
    height_n = NH
    thick_n = NT
    grid_shape = (thick_n, height_n, width_n)
    elem_shape = (thick_n - 1, height_n - 1, width_n - 1)
    offsets = []
    for corner in range(8):
        offsets.append((corner >> 2 & 1, corner >> 1 & 1, corner & 1))
    placed = None
    for corner in range(8):
        shift_t, shift_h, shift_w = offsets[corner]
        block = links[corner].reshape(elem_shape)
        block = jnp.pad(
            block,
            ((shift_t, 1 - shift_t), (shift_h, 1 - shift_h), (shift_w, 1 - shift_w)),
            constant_values=-1,
        )
        placed = block if placed is None else jnp.maximum(placed, block)
    grid_nodes = placed.reshape(-1)
    node_place = jnp.argsort(grid_nodes)
    material_count = conductivity.shape[0]
    onehot = (kinds[None, :] == jnp.arange(material_count, dtype=jnp.int32)[:, None]).astype(
        jnp.float32
    )
    conduct = jnp.dot(conductivity, onehot, precision=lax.Precision.HIGHEST).reshape(elem_shape)
    storage = (0.125 * jnp.dot(capacity, onehot, precision=lax.Precision.HIGHEST)).reshape(
        elem_shape
    )
    stiffness = unit_stiffness()

    def assemble(stacked):
        count = stacked.shape[0]
        cube = stacked.reshape((count,) + grid_shape)
        edge_pair = jnp.stack([cube[:, :, :, 0], cube[:, :, :, -1]], axis=1)
        extended = extended_2(edge_pair, (("fx", 1),), 1)
        low_add = extended[:, 0][:, :, :, None]
        high_add = extended[:, 3][:, :, :, None]
        cube = (
            cube
            + jnp.pad(low_add, ((0, 0), (0, 0), (0, 0), (0, width_n - 1)))
            + jnp.pad(high_add, ((0, 0), (0, 0), (0, 0), (width_n - 1, 0)))
        )
        edge_pair = jnp.stack([cube[:, :, 0, :], cube[:, :, -1, :]], axis=1)
        extended = extended_2(edge_pair, ((("sec", "fy"), 1),), 1)
        low_add = extended[:, 0][:, :, None, :]
        high_add = extended[:, 3][:, :, None, :]
        cube = (
            cube
            + jnp.pad(low_add, ((0, 0), (0, 0), (0, height_n - 1), (0, 0)))
            + jnp.pad(high_add, ((0, 0), (0, 0), (height_n - 1, 0), (0, 0)))
        )
        return cube.reshape(count, -1)

    unit_vals = jnp.ones((node_count,), jnp.float32)
    diag_grid = jnp.take(diag_part[0, 0, 0], grid_nodes, axis=0)
    source_grid = jnp.take(heat_source[0, 0, 0], grid_nodes, axis=0)
    started = assemble(jnp.stack([unit_vals, diag_grid, source_grid]))
    weight = 1.0 / started[0]
    diagonal = started[1]
    rhs = started[2]

    def inner(left_vec, right_vec):
        return jnp.sum(weight * left_vec * right_vec)

    def norm_sum(residual, scaled):
        return lax.psum(inner(residual, scaled), ("sec", "fx", "fy"))

    solution = jnp.zeros_like(rhs)
    residual = rhs
    scaled = residual / diagonal
    direction = scaled
    gamma = norm_sum(residual, scaled)
    for iteration in range(ITERS):
        apply_cube = direction.reshape(grid_shape)
        corner_vals = []
        for apply_corner in range(8):
            apply_shift_t, apply_shift_h, apply_shift_w = offsets[apply_corner]
            corner_vals.append(
                apply_cube[
                    apply_shift_t : apply_shift_t + thick_n - 1,
                    apply_shift_h : apply_shift_h + height_n - 1,
                    apply_shift_w : apply_shift_w + width_n - 1,
                ]
            )
        total = jnp.zeros(grid_shape, jnp.float32)
        for apply_corner in range(8):
            flux = None
            for other in range(8):
                coeff = float(stiffness[apply_corner, other])
                if coeff != 0.0:
                    term = coeff * corner_vals[other]
                    flux = term if flux is None else flux + term
            element_out = conduct * flux + storage * corner_vals[apply_corner]
            apply_shift_t, apply_shift_h, apply_shift_w = offsets[apply_corner]
            total = total + jnp.pad(
                element_out,
                (
                    (apply_shift_t, 1 - apply_shift_t),
                    (apply_shift_h, 1 - apply_shift_h),
                    (apply_shift_w, 1 - apply_shift_w),
                ),
            )
        image = assemble(total.reshape(-1)[None])[0]
        step_len = gamma / lax.psum(inner(direction, image), ("sec", "fx", "fy"))
        solution = solution + step_len * direction
        residual = residual - step_len * image
        if iteration + 1 < ITERS:
            scaled = residual / diagonal
            gamma_next = norm_sum(residual, scaled)
            direction = scaled + gamma_next / gamma * direction
            gamma = gamma_next
    solution_nodes = jnp.take(solution, node_place, axis=0)
    cells_z = air_state.shape[1]
    cells_x = air_state.shape[3]
    values = jnp.take(solution_nodes, iface_node[0, 0, 0], axis=0)
    gathered = lax.all_gather(values, "fy", axis=0, tiled=True)
    row_of_face = jnp.argsort(face_of_row[0, 0])
    wall_face = jnp.take(gathered, row_of_face, axis=0).reshape(cells_z, cells_x)
    at_front = lax.axis_index("fy") == 0
    padded = extended_2(air_state, (("sec", 1), ("fy", 2), ("fx", 3)), 1)
    ghost = jnp.where(at_front, wall_face, padded[0, 1:-1, 0, 1:-1])
    padded = padded.at[0, 1:-1, 0, 1:-1].set(ghost)
    air_next = advance(padded)
    return (solution_nodes[None, None, None], air_next)


def solution(mesh):
    return jax.shard_map(
        on_device,
        mesh=mesh,
        in_specs=(
            P("sec", "fx", "fy", None, None),
            P("sec", "fx", "fy", None),
            P("sec", "fx", "fy", None, None),
            P("sec", "fx", "fy", None, None),
            P("sec", "fx", "fy", None),
            P("sec", "fx", None),
            P(),
            P(),
            P("sec", "fx", "fy", None),
            P("sec", "fx", "fy", None),
            P(None, "sec", "fy", "fx"),
        ),
        out_specs=(P("sec", "fx", "fy", None), P(None, "sec", "fy", "fx")),
        check_vma=False,
    )
```

profile of v0, /device:TPU:0, one launch (start us, length us, event | category | flops | bytes accessed | tf_op | source)
XLA Modules:
  0.0 527.8 jit_solution(7872632099462877597)
XLA Ops:
  3.4 17.4 %gather_fusion.1 = f32[3072]{0:T(1024)S(1)} fusion(f32[3072]{0:T(1024)S(1)} %bitcast.197, s32[3072]{0:T(1024)S(1)} %fusion.13), kind=kCustom, calls=%fused_computation.clone | custom fusion | bytes 36864 | tf_op jit(solution)/shard_map/jit(_take)/gather | solution.py:145
  21.5 17.4 %gather_fusion.2 = f32[3072]{0:T(1024)S(1)} fusion(f32[3072]{0:T(1024)S(1)} %bitcast.199, s32[3072]{0:T(1024)S(1)} %fusion.13), kind=kCustom, calls=%fused_computation.1.clone | custom fusion | bytes 36864 | tf_op jit(solution)/shard_map/jit(_take)/gather | solution.py:146
  40.8 5.6 %collective-permute-start = (f32[3,1,4,24]{3,2,0,1:T(4,128)S(1)}, f32[3,1,4,24]{3,2,0,1:T(4,128)S(1)}, u32[]{:S(2)}, u32[]{:S(2)}) collective-permute-start(f32[3,1,4,24]{3,2,0,1:T(4,128)S(1)} %bitcast.220), channel_id=1, source_target_pairs={{0,2},{2,4},{4,6},{1,3},{3,5},{5,7},{8,10},{10,12},{12,14},{9,11},... | collective-permute-start | bytes 3464 | tf_op jit(solution)/shard_map/ppermute | solution.py:25
  55.2 4.8 collective-permute-start.4
  68.7 46.6 %all-reduce.60 = (f32[]{:T(128)}, f32[]{:T(128)}) all-reduce(f32[]{:T(128)} %get-tuple-element.24, f32[]{:T(128)} %get-tuple-element.23), channel_id=1, replica_groups=mesh['sec'=4,'fx'=4,'fy'=2] {'sec','fx','fy'}, use_global_device_ids=true, to_apply=%region_1.3 | all-reduce | flops 2 | bytes 16 | tf_op jit(solution)/shard_map/psum | solution.py:156
  117.3 40.2 %psum.58 = f32[]{:T(128)} all-reduce(f32[]{:T(128)} %get-tuple-element.52), channel_id=1, replica_groups=mesh['sec'=4,'fx'=4,'fy'=2] {'sec','fx','fy'}, use_global_device_ids=true, to_apply=%region_5.7 | all-reduce | flops 1 | bytes 8 | tf_op jit(solution)/shard_map/psum | solution.py:156
  160.7 4.5 collective-permute-start.8
  165.2 4.8 collective-permute-start.20
  170.1 5.8 %sort.31 = (s32[3072]{0:T(1024)}, s32[3072]{0:T(1024)S(1)}) sort(s32[3072]{0:T(1024)S(1)} %reshape.155, s32[3072]{0:T(1024)S(1)} %iota.11), dimensions={0}, to_apply=%region_16.18 | sort | flops 36864 | bytes 49152 | tf_op jit(solution)/shard_map/jit(argsort)/sort | solution.py:110
  182.0 5.8 %sort.32 = (s32[3072]{0:T(1024)}, s32[3072]{0:T(1024)S(1)}) sort(s32[3072]{0:T(1024)S(1)} %bitcast.201, s32[3072]{0:T(1024)S(1)} %iota.12), dimensions={0}, to_apply=%region_17.19 | sort | flops 36864 | bytes 49152 | tf_op jit(solution)/shard_map/jit(argsort)/sort | solution.py:207
  187.7 40.4 %psum.59 = f32[]{:T(128)} all-reduce(f32[]{:T(128)} %multiply_reduce_fusion.4), channel_id=1, replica_groups=mesh['sec'=4,'fx'=4,'fy'=2] {'sec','fx','fy'}, use_global_device_ids=true, to_apply=%region_7.9 | all-reduce | flops 1 | bytes 8 | tf_op jit(solution)/shard_map/psum | solution.py:194
  230.1 41.8 %psum.60 = f32[]{:T(128)} all-reduce(f32[]{:T(128)} %get-tuple-element.49), channel_id=1, replica_groups=mesh['sec'=4,'fx'=4,'fy'=2] {'sec','fx','fy'}, use_global_device_ids=true, to_apply=%region_9.11 | all-reduce | flops 1 | bytes 8 | tf_op jit(solution)/shard_map/psum | solution.py:156
  275.2 4.5 collective-permute-start.12
  287.7 43.5 %psum.61 = f32[]{:T(128)} all-reduce(f32[]{:T(128)} %get-tuple-element.47), channel_id=1, replica_groups=mesh['sec'=4,'fx'=4,'fy'=2] {'sec','fx','fy'}, use_global_device_ids=true, to_apply=%region_11.13 | all-reduce | flops 1 | bytes 8 | tf_op jit(solution)/shard_map/psum | solution.py:194
  333.3 40.8 %psum.62 = f32[]{:T(128)} all-reduce(f32[]{:T(128)} %get-tuple-element.45), channel_id=1, replica_groups=mesh['sec'=4,'fx'=4,'fy'=2] {'sec','fx','fy'}, use_global_device_ids=true, to_apply=%region_13.15 | all-reduce | flops 1 | bytes 8 | tf_op jit(solution)/shard_map/psum | solution.py:156
  377.3 5.1 collective-permute-start.16
  393.2 42.0 %psum.63 = f32[]{:T(128)} all-reduce(f32[]{:T(128)} %get-tuple-element.72), channel_id=1, replica_groups=mesh['sec'=4,'fx'=4,'fy'=2] {'sec','fx','fy'}, use_global_device_ids=true, to_apply=%region_15.17 | all-reduce | flops 1 | bytes 8 | tf_op jit(solution)/shard_map/psum | solution.py:194
  436.6 17.7 %gather_fusion.3 = f32[3072]{0:T(1024)S(1)} fusion(f32[3072]{0:T(1024)S(1)} %multiply_add_fusion.34, s32[3072]{0:T(1024)} %fusion.14), kind=kCustom, calls=%fused_computation.2.clone | custom fusion | bytes 36864 | tf_op jit(solution)/shard_map/jit(_take)/gather | solution.py:202
  454.3 8.4 %gather_fusion = f32[1536]{0:T(1024)S(1)} fusion(f32[3072]{0:T(1024)S(1)} %and_select_fusion, s32[2048]{0:T(1024)S(1)} %copy-done.10), kind=kCustom, calls=%fused_computation.4 | custom fusion | bytes 18432 | tf_op jit(solution)/shard_map/jit(_take)/gather | solution.py:205
  469.6 17.4 %gather_fusion.4 = f32[3072]{0:T(1024)S(1)} fusion(f32[3072]{0:T(1024)S(1)} %bitcast.198, s32[3072]{0:T(1024)S(1)} %copy-done.9), kind=kCustom, calls=%fused_computation.3.clone | custom fusion | bytes 36864 | tf_op jit(solution)/shard_map/jit(_take)/gather | solution.py:208
  491.2 3.3 copy.145
  495.8 3.3 copy.144
  499.1 4.8 collective-permute-start.24
  510.3 6.7 %pad_maximum_fusion = f32[4,26,34,130]{3,1,2,0:T(8,128)} fusion(f32[4,26,34,1]{3,1,2,0:T(8,128)} %copy.147, f32[4,26,1,128]{3,1,2,0:T(8,128)S(1)} %collective-permute-done.23, f32[4,1,32,128]{3,1,2,0:T(1,128)} %collective-permute-done.21, f32[4,24,32,128]{3,1,2,0:T(8,128)S(1)} %copy.143, f32[4,1,32,128]{3,1,2,0:T(1,128)} %collective-permute-done.20, ...), kind=kLoop, calls=%fused_computation.5 | loop fusion | flops 2758080 | bytes 3677440 | tf_op jit(solution)/shard_map/concatenate | solution.py:23
  (187 shorter events, 84.7 us)
Async XLA Ops:
  39.4 7.2 %collective-permute-start.1 = (f32[3,1,4,24]{3,2,0,1:T(4,128)S(1)}, f32[3,1,4,24]{3,2,0,1:T(4,128)S(1)}, u32[]{:S(2)}, u32[]{:S(2)}) collective-permute-start(f32[3,1,4,24]{3,2,0,1:T(4,128)S(1)} %bitcast.221), channel_id=1, source_target_pairs={{2,0},{4,2},{6,4},{3,1},{5,3},{7,5},{10,8},{12,10},{14,12},{11,9},... | collective-permute-start | bytes 3464 | tf_op jit(solution)/shard_map/ppermute | solution.py:27
  40.8 6.9 %collective-permute-start = (f32[3,1,4,24]{3,2,0,1:T(4,128)S(1)}, f32[3,1,4,24]{3,2,0,1:T(4,128)S(1)}, u32[]{:S(2)}, u32[]{:S(2)}) collective-permute-start(f32[3,1,4,24]{3,2,0,1:T(4,128)S(1)} %bitcast.220), channel_id=1, source_target_pairs={{0,2},{2,4},{4,6},{1,3},{3,5},{5,7},{8,10},{10,12},{12,14},{9,11},... | collective-permute-start | bytes 3464 | tf_op jit(solution)/shard_map/ppermute | solution.py:25
  48.0 4.8 collective-permute-start.3
  49.3 3.8 collective-permute-start.2
  53.9 6.1 %collective-permute-start.5 = (f32[1,1,4,24]{3,2,1,0:T(4,128)S(1)}, f32[1,1,4,24]{3,2,1,0:T(4,128)S(1)}, u32[]{:S(2)}, u32[]{:S(2)}) collective-permute-start(f32[1,1,4,24]{3,2,1,0:T(4,128)S(1)} %bitcast.237), channel_id=1, source_target_pairs={{2,0},{4,2},{6,4},{3,1},{5,3},{7,5},{10,8},{12,10},{14,12},{11,9},... | collective-permute-start | bytes 1160 | tf_op jit(solution)/shard_map/ppermute | solution.py:27
  55.2 6.1 %collective-permute-start.4 = (f32[1,1,4,24]{3,2,1,0:T(4,128)S(1)}, f32[1,1,4,24]{3,2,1,0:T(4,128)S(1)}, u32[]{:S(2)}, u32[]{:S(2)}) collective-permute-start(f32[1,1,4,24]{3,2,1,0:T(4,128)S(1)} %bitcast.230), channel_id=1, source_target_pairs={{0,2},{2,4},{4,6},{1,3},{3,5},{5,7},{8,10},{10,12},{12,14},{9,11},... | collective-permute-start | bytes 1160 | tf_op jit(solution)/shard_map/ppermute | solution.py:25
  61.6 6.4 %collective-permute-start.7 = (f32[1,1,4,32]{3,2,1,0:T(4,128)S(1)}, f32[1,1,4,32]{3,2,1,0:T(4,128)S(1)}, u32[]{:S(2)}, u32[]{:S(2)}) collective-permute-start(f32[1,1,4,32]{3,2,1,0:T(4,128)S(1)} %bitcast.242), channel_id=1, source_target_pairs={{1,0},{8,1},{9,8},{16,9},{17,16},{24,17},{25,24},{3,2},{10,3},{11,... | collective-permute-start | bytes 1544 | tf_op jit(solution)/shard_map/ppermute | solution.py:27
  62.9 5.1 collective-permute-start.6
  66.7 396.0 %collective-permute-start.21 = (f32[4,1,32,128]{3,1,2,0:T(1,128)}, f32[4,1,32,128]{3,1,2,0:T(1,128)}, u32[]{:S(2)}, u32[]{:S(2)}) collective-permute-start(f32[4,1,32,128]{3,1,2,0:T(1,128)} %bitcast.54), channel_id=1, source_target_pairs={{8,0},{16,8},{24,16},{9,1},{17,9},{25,17},{10,2},{18,10},{26,18},{... | collective-permute-start | bytes 196616 | tf_op jit(solution)/shard_map/ppermute | solution.py:27
  159.4 16.4 %collective-permute-start.9 = (f32[1,1,4,24]{3,2,1,0:T(4,128)S(1)}, f32[1,1,4,24]{3,2,1,0:T(4,128)S(1)}, u32[]{:S(2)}, u32[]{:S(2)}) collective-permute-start(f32[1,1,4,24]{3,2,1,0:T(4,128)S(1)} %bitcast.226), channel_id=1, source_target_pairs={{2,0},{4,2},{6,4},{3,1},{5,3},{7,5},{10,8},{12,10},{14,12},{11,9},... | collective-permute-start | bytes 1160 | tf_op jit(solution)/shard_map/ppermute | solution.py:27
  160.7 15.2 %collective-permute-start.8 = (f32[1,1,4,24]{3,2,1,0:T(4,128)S(1)}, f32[1,1,4,24]{3,2,1,0:T(4,128)S(1)}, u32[]{:S(2)}, u32[]{:S(2)}) collective-permute-start(f32[1,1,4,24]{3,2,1,0:T(4,128)S(1)} %bitcast.224), channel_id=1, source_target_pairs={{0,2},{2,4},{4,6},{1,3},{3,5},{5,7},{8,10},{10,12},{12,14},{9,11},... | collective-permute-start | bytes 1160 | tf_op jit(solution)/shard_map/ppermute | solution.py:25
  165.2 297.5 %collective-permute-start.20 = (f32[4,1,32,128]{3,1,2,0:T(1,128)}, f32[4,1,32,128]{3,1,2,0:T(1,128)}, u32[]{:S(2)}, u32[]{:S(2)}) collective-permute-start(f32[4,1,32,128]{3,1,2,0:T(1,128)} %bitcast.53), channel_id=1, source_target_pairs={{0,8},{8,16},{16,24},{1,9},{9,17},{17,25},{2,10},{10,18},{18,26},{... | collective-permute-start | bytes 196616 | tf_op jit(solution)/shard_map/ppermute | solution.py:25
  176.1 4.9 collective-permute-start.11
  273.9 6.5 %collective-permute-start.13 = (f32[1,1,4,24]{3,2,1,0:T(4,128)S(1)}, f32[1,1,4,24]{3,2,1,0:T(4,128)S(1)}, u32[]{:S(2)}, u32[]{:S(2)}) collective-permute-start(f32[1,1,4,24]{3,2,1,0:T(4,128)S(1)} %bitcast.234), channel_id=1, source_target_pairs={{2,0},{4,2},{6,4},{3,1},{5,3},{7,5},{10,8},{12,10},{14,12},{11,9},... | collective-permute-start | bytes 1160 | tf_op jit(solution)/shard_map/ppermute | solution.py:27
  275.2 5.8 %collective-permute-start.12 = (f32[1,1,4,24]{3,2,1,0:T(4,128)S(1)}, f32[1,1,4,24]{3,2,1,0:T(4,128)S(1)}, u32[]{:S(2)}, u32[]{:S(2)}) collective-permute-start(f32[1,1,4,24]{3,2,1,0:T(4,128)S(1)} %bitcast.229), channel_id=1, source_target_pairs={{0,2},{2,4},{4,6},{1,3},{3,5},{5,7},{8,10},{10,12},{12,14},{9,11},... | collective-permute-start | bytes 1160 | tf_op jit(solution)/shard_map/ppermute | solution.py:25
  281.2 4.4 collective-permute-start.15
  376.0 7.9 %collective-permute-start.17 = (f32[1,1,4,24]{3,2,1,0:T(4,128)S(1)}, f32[1,1,4,24]{3,2,1,0:T(4,128)S(1)}, u32[]{:S(2)}, u32[]{:S(2)}) collective-permute-start(f32[1,1,4,24]{3,2,1,0:T(4,128)S(1)} %bitcast.232), channel_id=1, source_target_pairs={{2,0},{4,2},{6,4},{3,1},{5,3},{7,5},{10,8},{12,10},{14,12},{11,9},... | collective-permute-start | bytes 1160 | tf_op jit(solution)/shard_map/ppermute | solution.py:27
  377.3 8.0 %collective-permute-start.16 = (f32[1,1,4,24]{3,2,1,0:T(4,128)S(1)}, f32[1,1,4,24]{3,2,1,0:T(4,128)}, u32[]{:S(2)}, u32[]{:S(2)}) collective-permute-start(f32[1,1,4,24]{3,2,1,0:T(4,128)S(1)} %bitcast.228), channel_id=1, source_target_pairs={{0,2},{2,4},{4,6},{1,3},{3,5},{5,7},{8,10},{10,12},{12,14},{9,11},... | collective-permute-start | bytes 1160 | tf_op jit(solution)/shard_map/ppermute | solution.py:25
  386.2 5.3 %collective-permute-start.19 = (f32[1,1,4,32]{3,2,1,0:T(4,128)S(1)}, f32[1,1,4,32]{3,2,1,0:T(4,128)S(1)}, u32[]{:S(2)}, u32[]{:S(2)}) collective-permute-start(f32[1,1,4,32]{3,2,1,0:T(4,128)S(1)} %bitcast.240), channel_id=1, source_target_pairs={{1,0},{8,1},{9,8},{16,9},{17,16},{24,17},{25,24},{3,2},{10,3},{11,... | collective-permute-start | bytes 1544 | tf_op jit(solution)/shard_map/ppermute | solution.py:27
  387.5 4.0 collective-permute-start.18
  463.4 23.6 %collective-permute-start.23 = (f32[4,26,1,128]{3,1,2,0:T(8,128)S(1)}, f32[4,26,1,128]{3,1,2,0:T(8,128)S(1)}, u32[]{:S(2)}, u32[]{:S(2)}) collective-permute-start(f32[4,26,1,128]{3,1,2,0:T(8,128)S(1)} %get-tuple-element.69), channel_id=1, source_target_pairs={{1,0},{3,2},{5,4},{7,6},{9,8},{11,10},{13,12},{15,14},{17,16},{19,... | collective-permute-start | bytes 159752 | tf_op jit(solution)/shard_map/ppermute | solution.py:27
  464.7 22.3 %collective-permute-start.22 = (f32[4,26,1,128]{3,1,2,0:T(8,128)S(1)}, f32[4,26,1,128]{3,1,2,0:T(8,128)S(1)}, u32[]{:S(2)}, u32[]{:S(2)}) collective-permute-start(f32[4,26,1,128]{3,1,2,0:T(8,128)S(1)} %get-tuple-element.68), channel_id=1, source_target_pairs={{0,1},{2,3},{4,5},{6,7},{8,9},{10,11},{12,13},{14,15},{16,17},{18,... | collective-permute-start | bytes 159752 | tf_op jit(solution)/shard_map/ppermute | solution.py:25
  494.5 9.4 %collective-permute-start.25 = (f32[4,26,34,1]{2,0,3,1:T(4,128)S(1)}, f32[4,26,34,1]{2,0,3,1:T(4,128)S(1)}, u32[]{:S(2)}, u32[]{:S(2)}) collective-permute-start(f32[4,26,34,1]{2,0,3,1:T(4,128)S(1)} %copy.145), channel_id=1, source_target_pairs={{2,0},{4,2},{6,4},{3,1},{5,3},{7,5},{10,8},{12,10},{14,12},{11,9},... | collective-permute-start | bytes 42440 | tf_op jit(solution)/shard_map/ppermute | solution.py:27
  499.1 8.0 %collective-permute-start.24 = (f32[4,26,34,1]{2,0,3,1:T(4,128)S(1)}, f32[4,26,34,1]{2,0,3,1:T(4,128)S(1)}, u32[]{:S(2)}, u32[]{:S(2)}) collective-permute-start(f32[4,26,34,1]{2,0,3,1:T(4,128)S(1)} %copy.144), channel_id=1, source_target_pairs={{0,2},{2,4},{4,6},{1,3},{3,5},{5,7},{8,10},{10,12},{12,14},{9,11},... | collective-permute-start | bytes 42440 | tf_op jit(solution)/shard_map/ppermute | solution.py:25
  (19 other events, 639.7 us)
where the time goes:
time: 530 us; the launch traced here: 528 us
  blocking collectives  297 us (56%)
  local copies, waits for them, and re-layouts  112 us (21%)
  starting transfers between devices  69.4 us (13%)
  other arithmetic  34.8 us (7%)
  between operations  10.7 us (2%)
    psum x4, blocking collectives, norm_sum(): return lax.psum(inner(residual, scaled), ('sec', 'fx', 'fy'))  169 us
    psum x3, blocking collectives, on_device(): step_len = gamma / lax.psum(inner(direction, image), ('sec', 'fx', 'fy'))  126 us
    ppermute x13, starting transfers between devices, extended_2(): lax.ppermute(tail, axis, [(i, (i + 1) % count) for i in range(ends)])  52.5 us
    gather x1, local copies, waits for them, and re-layouts, on_device(): solution_nodes = jnp.take(solution, node_place, axis=0)  17.7 us
    gather x1, local copies, waits for them, and re-layouts, on_device(): diag_grid = jnp.take(diag_part[0, 0, 0], grid_nodes, axis=0)  17.4 us
    gather x1, local copies, waits for them, and re-layouts, on_device(): jnp.take(gathered, row_of_face, axis=0).reshape(cells_z, cells_x)  17.4 us
    gather x1, local copies, waits for them, and re-layouts, on_device(): source_grid = jnp.take(heat_source[0, 0, 0], grid_nodes, axis=0)  17.4 us
    ppermute x13, starting transfers between devices, extended_2(): lax.ppermute(head, axis, [((i + 1) % count, i) for i in range(ends)])  16.9 us
  transfers between devices with their start and end apart: 26, of which 6 were waited for; matrix products, arithmetic and copies ran while one was open for 15% of the time, Pallas kernels for 0%

commit v1 on v0

v1 whole, which is shorter than its diff:
```python
import jax
import jax.numpy as jnp
import numpy as np
from jax import lax
from jax.experimental import pallas as pl
from jax.experimental.pallas import tpu as pltpu
from jax.sharding import PartitionSpec as P

NW = 32
NH = 24
NT = 4
ITERS = 4
LANES = 128
SUBS = 8

time_step = 0.2
viscosity = 0.75

VMEM = pl.BlockSpec(memory_space=pltpu.VMEM)
SMEM = pl.BlockSpec(memory_space=pltpu.SMEM)
ANY = pl.BlockSpec(memory_space=pl.ANY)
PARAMS = pltpu.CompilerParams(vmem_limit_bytes=56 * 1024 * 1024)

EW = NW - 1
EH = NH - 1
ET = NT - 1
ELEMS = ET * EH * EW
ROWS = NT * NH * NW // LANES
FIELD_ROWS = NT * NH
BAND_ROWS = 2 * FIELD_ROWS + ET * NH


def iota(shape, dim):
    return lax.broadcasted_iota(jnp.int32, shape, dim)


def lane_pick(row, idx):
    return jnp.take_along_axis(
        jnp.broadcast_to(row, idx.shape), idx, axis=1, mode="promise_in_bounds"
    )


def look_up(rows, place):
    high = place >> 7
    low = place & (LANES - 1)
    out = None
    for r, row in enumerate(rows):
        got = lane_pick(row, low)
        out = got if out is None else jnp.where(high == r, got, out)
    return out


def spread(idx, values):
    count = idx.shape[0]
    acc = None
    group = 4
    for start in range(0, count, group):
        left, right = [], []
        for r in range(start, start + group):
            row = idx[r : r + 1]
            hot_high = iota((count, LANES), 0) == (row >> 7)
            hot_low = iota((LANES, LANES), 0) == (row & (LANES - 1))
            left.append(
                jnp.concatenate(
                    [jnp.where(hot_high, v[r : r + 1], 0.0) for v in values], axis=0
                ).astype(jnp.bfloat16)
            )
            right.append(jnp.where(hot_low, 1.0, 0.0).astype(jnp.bfloat16))
        part = lax.dot_general(
            jnp.concatenate(left, axis=1),
            jnp.concatenate(right, axis=1),
            (((1,), (1,)), ((), ())),
            preferred_element_type=jnp.float32,
        )
        acc = part if acc is None else acc + part
    return [acc[i * count : (i + 1) * count] for i in range(len(values))]


def element_keys():
    h = np.arange(NH)[:, None]
    lane = np.arange(LANES)[None, :]
    t, w = lane // NW, lane % NW
    corner = 4 * (t == NT - 1) + 2 * (h == NH - 1) + (w == NW - 1)
    column = np.minimum(t, ET - 1) * EH * EW + np.minimum(h, EH - 1) * EW + np.minimum(w, EW - 1)
    return corner, column


def stage_kernel(conn_ref, material_ref, diag_ref, source_ref, pay_ref, nodes_ref):
    corner_np, column_np = element_keys()
    pieces, kinds = [], []
    for j in range(NH // SUBS):
        h = iota((SUBS, LANES), 0) + SUBS * j
        lane = iota((SUBS, LANES), 1)
        t = lane >> 5
        w = lane & (NW - 1)
        corner = (
            jnp.where(t == NT - 1, 4, 0) + jnp.where(h == NH - 1, 2, 0) + jnp.where(w == NW - 1, 1, 0)
        )
        column = (
            jnp.minimum(t, ET - 1) * (EH * EW)
            + jnp.minimum(h, EH - 1) * EW
            + jnp.minimum(w, EW - 1)
        )
        low = column & (LANES - 1)
        tile = column >> 7
        key = tile * 8 + corner
        rows = slice(SUBS * j, SUBS * (j + 1))
        wanted = sorted(set((column_np[rows] // LANES * 8 + corner_np[rows]).reshape(-1).tolist()))
        out = jnp.zeros((SUBS, LANES), jnp.int32)
        for code in wanted:
            c, k = code % 8, code // 8
            row = conn_ref[c : c + 1, LANES * k : LANES * (k + 1)]
            out = jnp.where(key == code, lane_pick(row, low), out)
        pieces.append(out)
        kind = jnp.full((SUBS, LANES), -1, jnp.int32)
        for k in sorted({code // 8 for code in wanted if code % 8 == 0}):
            row = material_ref[0:1, LANES * k : LANES * (k + 1)]
            kind = jnp.where((corner == 0) & (tile == k), lane_pick(row, low), kind)
        kinds.append(kind)
    nodes = jnp.concatenate(pieces, axis=0)
    nodes_ref[...] = nodes
    pay_ref[0:ROWS] = look_up([diag_ref[r : r + 1] for r in range(ROWS)], nodes)
    pay_ref[ROWS : 2 * ROWS] = look_up([source_ref[r : r + 1] for r in range(ROWS)], nodes)
    pay_ref[2 * ROWS : 3 * ROWS] = jnp.concatenate(kinds, axis=0).astype(jnp.float32) + 1.0


def band_kernel(tiles_x, wide, where_ref, *refs):
    parts, band_ref, held = refs[:tiles_x], refs[tiles_x], refs[tiles_x + 1]
    fx = where_ref[1]
    for k, part in enumerate(parts):
        held[fx ^ k] = part[...]
    lane = iota((NH, wide), 1)
    at = 0
    for field in range(3):
        for t in range(NT if field < 2 else ET):
            total = None
            for f in range(tiles_x):
                x = held[f, field * ROWS : (field + 1) * ROWS]
                if wide > LANES:
                    x = jnp.concatenate([x, jnp.zeros((NH, wide - LANES), jnp.float32)], axis=1)
                shift = (EW * f - NW * t) % wide
                if shift:
                    x = pltpu.roll(x, shift, 1)
                x = jnp.where((lane >= EW * f) & (lane < EW * f + NW), x, 0.0)
                total = x if total is None else total + x
            band_ref[at : at + NH] = total
            at += NH


def faces_kernel(where_ref, air_ref, x_even, x_odd, y_even, y_odd, z_even, z_odd):
    sec, fx, fy = where_ref[0], where_ref[1], where_ref[2]
    fields, cells_z, cells_y, cells_x = air_ref.shape
    z_up = (sec & 1) == 0
    z_even[...] = air_ref[:, jnp.where(z_up, cells_z - 1, 0)]
    z_odd[...] = air_ref[:, jnp.where(z_up, 0, cells_z - 1)]
    y_up = (fy & 1) == 0
    x_up = (fx & 1) == 0
    lane = iota((cells_y, LANES), 1)
    lows, highs = [], []
    for f in range(fields):
        first = air_ref[f, :, 0, :]
        last = air_ref[f, :, cells_y - 1, :]
        y_even[f] = jnp.where(y_up, last, first)
        y_odd[f] = jnp.where(y_up, first, last)
        low = jnp.zeros((cells_y, LANES), jnp.float32)
        high = jnp.zeros((cells_y, LANES), jnp.float32)
        for z in range(cells_z):
            x = pltpu.roll(air_ref[f, z], z + 1, 1)
            high = jnp.where(lane == z, x, high)
            low = jnp.where(lane == z + 1, x, low)
        lows.append(low)
        highs.append(high)
    low = pltpu.roll(jnp.concatenate(lows, axis=0), LANES - 1, 1)
    high = jnp.concatenate(highs, axis=0)
    x_even[...] = jnp.where(x_up, high, low).T[:cells_z]
    x_odd[...] = jnp.where(x_up, low, high).T[:cells_z]


def air_kernel(
    where_ref, air_ref, x_even, x_odd, y_even, y_odd, z_even, z_odd, next_ref, edge_ref, gain_ref,
    west_ref, east_ref,
):
    sec, fx, fy = where_ref[0], where_ref[1], where_ref[2]
    fields, cells_z, cells_y, cells_x = air_ref.shape
    pad = jnp.zeros((LANES - cells_z, LANES), jnp.float32)
    even = jnp.concatenate([x_even[...], pad], axis=0).T
    odd = jnp.concatenate([x_odd[...], pad], axis=0).T
    x_up = (fx & 1) == 0
    west_ref[...] = jnp.where(x_up, odd, even)
    east_ref[...] = jnp.where(x_up, even, odd)
    y_up = (fy & 1) == 0
    z_up = (sec & 1) == 0
    row = iota((cells_y, LANES), 0)
    lane = iota((cells_y, LANES), 1)
    half = 0.5 * time_step
    mix = time_step * viscosity

    def layer(z, below, above):
        u, v, w = air_ref[1, z], air_ref[2, z], air_ref[3, z]
        hu, hv, hw = half * u, half * v, half * w
        gain_ref[pl.ds(z, 1), :] = (mix + hv[0:1]) * jnp.where(fy == 0, 1.0, 0.0)
        for f in range(fields):
            x = air_ref[f, z]
            span = slice(f * cells_y, (f + 1) * cells_y)
            west = jnp.where(
                lane == 0,
                pltpu.roll(west_ref[span], (LANES - z) % LANES, 1),
                pltpu.roll(x, 1, 1),
            )
            east = jnp.where(
                lane == LANES - 1,
                pltpu.roll(east_ref[span], LANES - 1 - z, 1),
                pltpu.roll(x, LANES - 1, 1),
            )
            y_e, y_o = y_even[f, pl.ds(z, 1), :], y_odd[f, pl.ds(z, 1), :]
            south_ghost = jnp.where(y_up, y_o, y_e)
            north_ghost = jnp.where(y_up, y_e, y_o)
            south = jnp.where(row == 0, south_ghost, pltpu.roll(x, 1, 0))
            north = jnp.where(row == cells_y - 1, north_ghost, pltpu.roll(x, cells_y - 1, 0))
            lower, upper = below(f), above(f)
            out = (
                (1.0 - 6.0 * mix) * x
                + mix * (east + west + north + south + upper + lower)
                + hu * (west - east)
                + hv * (south - north)
                + hw * (lower - upper)
            )
            next_ref[f, z] = out
            if f == 0:
                edge_ref[z] = out[:SUBS]

    def ghost_low(f):
        return jnp.where(z_up, z_odd[f], z_even[f])

    def ghost_high(f):
        return jnp.where(z_up, z_even[f], z_odd[f])

    layer(0, ghost_low, lambda f: air_ref[f, 1])

    @pl.loop(1, cells_z - 1)
    def _(z):
        layer(z, lambda f: air_ref[f, z - 1], lambda f: air_ref[f, z + 1])

    layer(cells_z - 1, lambda f: air_ref[f, cells_z - 2], ghost_high)


def place_kernel(nodes_ref, iface_ref, place_ref, rows_ref):
    nodes = nodes_ref[...]
    at_row = iota(nodes.shape, 0).astype(jnp.float32)
    at_lane = iota(nodes.shape, 1).astype(jnp.float32)
    high, low = spread(nodes, [at_row, at_lane])
    place = high * LANES + low
    place_ref[...] = place.astype(jnp.int32)
    rows_ref[...] = look_up([place[r : r + 1] for r in range(ROWS)], iface_ref[...])


def face_kernel(tiles_y, where_ref, face_ref, *refs):
    parts, wall_ref, held = refs[:tiles_y], refs[tiles_y], refs[tiles_y + 1]
    fy = where_ref[2]
    for k, part in enumerate(parts):
        held[fy ^ k] = part[...] + (fy ^ k).astype(jnp.float32) * (ROWS * LANES)
    rows = jnp.concatenate([held[j] for j in range(tiles_y)], axis=0)
    row = rows.astype(jnp.int32)
    high, low = spread(
        face_ref[...],
        [(row >> 7).astype(jnp.float32), (row & (LANES - 1)).astype(jnp.float32)],
    )
    wall_ref[...] = (high * LANES + low).astype(jnp.int32)


def solve_kernel(
    tiles_s, tiles_x, tiles_y, wide, material_count,
    where_ref, conduct_ref, capacity_ref, place_ref, wall_ref, edge_ref, gain_ref, air_ref, *refs,
):
    bands = tiles_s * tiles_y
    parts = refs[:bands]
    solid_ref, next_ref = refs[bands : bands + 2]
    (held, elem, side, main, inv, res, dirn, image, sol, table, edge, sem) = refs[bands + 2 :]
    sec, fx, fy = where_ref[0], where_ref[1], where_ref[2]
    for j in range(tiles_y):
        for k in range(tiles_s):
            held[(sec ^ k) * tiles_y + (fy ^ j)] = parts[j * tiles_s + k][...]

    lane = iota((NH, wide), 1)
    first_row = iota((NH, wide), 0) == 0
    used = lane < EW * tiles_x + 1

    def right(x):
        return pltpu.roll(x, wide - 1, 1)

    def left(x):
        return pltpu.roll(x, 1, 1)

    def up(x):
        return pltpu.roll(x, NH - 1, 0)

    def down(x):
        return pltpu.roll(x, 1, 0)

    def to_nodes(x):
        x = x + left(x)
        return x + down(x)

    def seams(ref):
        for k in range(1, bands):
            for t in range(NT):
                both = ref[k - 1, t, NH - 1 : NH, :] + ref[k, t, 0:1, :]
                ref[k - 1, t, NH - 1 : NH, :] = both
                ref[k, t, 0:1, :] = both

    def each_band(body, total=None):
        return lax.fori_loop(0, bands, body, total)

    def prepare(b, _):
        cells, own = [], []
        for t in range(ET):
            kind = held[b, 2 * FIELD_ROWS + t * NH : 2 * FIELD_ROWS + (t + 1) * NH, :]
            x = jnp.zeros_like(kind)
            s = jnp.zeros_like(kind)
            for m in range(material_count):
                x = jnp.where(kind == m + 1.0, conduct_ref[m] * (1.0 / 12.0), x)
                s = jnp.where(kind == m + 1.0, capacity_ref[m] * 0.125, s)
            elem[b, t] = x
            side[b, t] = to_nodes(x)
            cells.append(x)
            own.append(5.0 * x + s)
        for t in range(NT):
            if t == 0:
                m = own[0]
            elif t == NT - 1:
                m = own[ET - 1]
            else:
                m = own[t] + own[t - 1]
            main[b, t] = to_nodes(m)
            inv[b, t] = held[b, t * NH : (t + 1) * NH, :]
            res[b, t] = held[b, FIELD_ROWS + t * NH : FIELD_ROWS + (t + 1) * NH, :]
        return _

    each_band(prepare)
    seams(inv)
    seams(res)

    zero = jnp.zeros((NH, wide), jnp.float32)

    def count_once(b, x):
        return jnp.where(first_row & (b > 0), 0.0, x)

    def total_of(x):
        return jnp.sum(jnp.sum(x, axis=0, keepdims=True), axis=1, keepdims=True)

    def begin(b, acc):
        for t in range(NT):
            d = jnp.where(used, 1.0 / inv[b, t], 0.0)
            inv[b, t] = d
            r = res[b, t]
            z = r * d
            dirn[b, t] = z
            sol[b, t] = zero
            acc = acc + count_once(b, r * z)
        return acc

    gamma = total_of(each_band(begin, zero))

    beta = None
    for iteration in range(ITERS):

        def operate(b, acc, beta=beta):
            p, cross, diag, layer = [], [], [], []
            for t in range(NT):
                x = dirn[b, t]
                if beta is not None:
                    x = res[b, t] * inv[b, t] + beta * x
                    dirn[b, t] = x
                y = right(x)
                d = x + up(y)
                c = y + up(x)
                p.append(x)
                diag.append(d)
                cross.append(c)
                layer.append(d + c)
            for t in range(NT):
                out = main[b, t] * p[t]
                if t == 0:
                    both = elem[b, 0]
                    other = both * layer[1]
                    out = out + side[b, 0] * p[1]
                elif t == NT - 1:
                    both = elem[b, ET - 1]
                    other = both * layer[ET - 1]
                    out = out + side[b, ET - 1] * p[ET - 1]
                else:
                    both = elem[b, t] + elem[b, t - 1]
                    other = elem[b, t] * layer[t + 1] + elem[b, t - 1] * layer[t - 1]
                    out = out + side[b, t] * p[t + 1] + side[b, t - 1] * p[t - 1]
                on_diag = other + both * diag[t]
                on_cross = other + both * cross[t]
                out = out - (on_diag + left(on_cross)) - down(on_cross + left(on_diag))
                image[b, t] = out
                acc = acc + p[t] * out
            return acc

        step_len = gamma / total_of(each_band(operate, zero))
        last = iteration + 1 == ITERS
        if not last:
            seams(image)

        def update(b, acc, step_len=step_len, last=last):
            for t in range(NT):
                sol[b, t] = sol[b, t] + step_len * dirn[b, t]
                if not last:
                    r = res[b, t] - step_len * image[b, t]
                    res[b, t] = r
                    acc = acc + count_once(b, r * r * inv[b, t])
            return acc

        gamma_next = total_of(each_band(update, zero))
        if not last:
            beta = gamma_next / gamma
            gamma = gamma_next

    for j in range(tiles_y):
        packed = jnp.zeros((NH, LANES), jnp.float32)
        spot = iota((NH, LANES), 1) >> 5
        for t in range(NT):
            x = sol[sec * tiles_y + j, t]
            x = pltpu.roll(x, (NW * t - EW * fx + tiles_x * wide) % wide, 1)[:, :LANES]
            packed = jnp.where(spot == t, x, packed)
        table[j] = packed
    solid_ref[...] = look_up([table[fy, r : r + 1] for r in range(ROWS)], place_ref[...])
    rows = [table[j, r : r + 1] for j in range(tiles_y) for r in range(ROWS)]
    extra = look_up(rows, wall_ref[...]) * gain_ref[...]
    cells_z = edge_ref.shape[0]
    top = iota((SUBS, LANES), 0) == 0
    for z in range(cells_z):
        edge[z] = edge_ref[z] + jnp.where(top, extra[z : z + 1], 0.0)
    copy = pltpu.make_async_copy(edge, next_ref.at[0, :, 0:SUBS, :], sem)
    copy.start()
    copy.wait()


def swap(x, axis, mask):
    count = lax.axis_size(axis)
    return lax.ppermute(x, axis, [(i, i ^ mask) for i in range(count)])


def pair_swap(x, axis, odd):
    count = lax.axis_size(axis)
    pairs = []
    for i in range(odd, count - 1, 2):
        pairs += [(i, i + 1), (i + 1, i)]
    return lax.ppermute(x, axis, pairs) if pairs else jnp.zeros_like(x)


def on_device(
    conn,
    material,
    side_nodes,
    rim_nodes,
    iface_node,
    face_of_row,
    conductivity,
    capacity,
    diag_part,
    heat_source,
    air_state,
):
    f32 = jnp.float32
    tiles_s, tiles_x, tiles_y = (lax.axis_size(axis) for axis in ("sec", "fx", "fy"))
    bands = tiles_s * tiles_y
    wide = -(-(EW * tiles_x + 1) // LANES) * LANES
    elem_lanes = -(-ELEMS // LANES) * LANES
    where = jnp.stack([lax.axis_index(axis) for axis in ("sec", "fx", "fy")]).astype(jnp.int32)
    fields, cells_z, cells_y, cells_x = air_state.shape

    def shape(*dims):
        return jax.ShapeDtypeStruct(dims, f32)

    def whole(*dims):
        return pl.BlockSpec(dims, lambda i: (0,) * len(dims))

    pay, nodes = pl.pallas_call(
        stage_kernel,
        grid=(1,),
        in_specs=[whole(8, elem_lanes), whole(1, elem_lanes), whole(ROWS, LANES), whole(ROWS, LANES)],
        out_specs=[whole(3 * ROWS, LANES), whole(ROWS, LANES)],
        out_shape=[shape(3 * ROWS, LANES), jax.ShapeDtypeStruct((ROWS, LANES), jnp.int32)],
        compiler_params=PARAMS,
    )(
        conn.reshape(conn.shape[-2:]),
        material.reshape(1, -1),
        diag_part.reshape(ROWS, LANES),
        heat_source.reshape(ROWS, LANES),
    )
    pays = [pay] + [swap(pay, "fx", k) for k in range(1, tiles_x)]

    faces = pl.pallas_call(
        faces_kernel,
        in_specs=[SMEM, VMEM],
        out_specs=[VMEM] * 6,
        out_shape=[shape(cells_z, fields * cells_y)] * 2
        + [shape(fields, cells_z, cells_x)] * 2
        + [shape(fields, cells_y, cells_x)] * 2,
        compiler_params=PARAMS,
    )(where, air_state)
    x_even, x_odd, y_even, y_odd, z_even, z_odd = faces

    band = pl.pallas_call(
        lambda *refs: band_kernel(tiles_x, wide, *refs),
        in_specs=[SMEM] + [VMEM] * tiles_x,
        out_specs=VMEM,
        out_shape=shape(BAND_ROWS, wide),
        scratch_shapes=[pltpu.VMEM((tiles_x, 3 * ROWS, LANES), f32)],
        compiler_params=PARAMS,
    )(where, *pays)

    own_bands = [band] + [swap(band, "sec", k) for k in range(1, tiles_s)]
    all_bands = own_bands + [swap(b, "fy", j) for j in range(1, tiles_y) for b in own_bands]

    place, rows = pl.pallas_call(
        place_kernel,
        in_specs=[VMEM] * 2,
        out_specs=[VMEM] * 2,
        out_shape=[
            jax.ShapeDtypeStruct((ROWS, LANES), jnp.int32),
            shape(iface_node.shape[-1] // LANES, LANES),
        ],
        compiler_params=PARAMS,
    )(nodes, iface_node.reshape(-1, LANES))
    all_rows = [rows] + [swap(rows, "fy", j) for j in range(1, tiles_y)]
    wall = pl.pallas_call(
        lambda *refs: face_kernel(tiles_y, *refs),
        in_specs=[SMEM, VMEM] + [VMEM] * tiles_y,
        out_specs=VMEM,
        out_shape=jax.ShapeDtypeStruct((cells_z, LANES), jnp.int32),
        scratch_shapes=[pltpu.VMEM((tiles_y,) + rows.shape, f32)],
        compiler_params=PARAMS,
    )(where, face_of_row.reshape(-1, LANES), *all_rows)

    ghosts = [
        pair_swap(x_even, "fx", 0),
        pair_swap(x_odd, "fx", 1),
        pair_swap(y_even, "fy", 0),
        pair_swap(y_odd, "fy", 1),
        pair_swap(z_even, "sec", 0),
        pair_swap(z_odd, "sec", 1),
    ]
    air_next, edge, gain = pl.pallas_call(
        air_kernel,
        in_specs=[SMEM] + [VMEM] * 7,
        out_specs=[VMEM] * 3,
        out_shape=[shape(*air_state.shape), shape(cells_z, SUBS, LANES), shape(cells_z, LANES)],
        scratch_shapes=[pltpu.VMEM((LANES, LANES), f32)] * 2,
        compiler_params=PARAMS,
    )(where, air_state, *ghosts)

    grid = (bands, NT, NH, wide)
    solid, air_next = pl.pallas_call(
        lambda *refs: solve_kernel(
            tiles_s, tiles_x, tiles_y, wide, conductivity.shape[0], *refs
        ),
        in_specs=[SMEM] * 3 + [VMEM] * 4 + [ANY] + [VMEM] * bands,
        out_specs=[VMEM, ANY],
        out_shape=[shape(ROWS, LANES), shape(*air_state.shape)],
        input_output_aliases={7: 1},
        scratch_shapes=[pltpu.VMEM((bands, BAND_ROWS, wide), f32)]
        + [pltpu.VMEM((bands, ET, NH, wide), f32)] * 2
        + [pltpu.VMEM(grid, f32)] * 6
        + [
            pltpu.VMEM((tiles_y, ROWS, LANES), f32),
            pltpu.VMEM((cells_z, SUBS, LANES), f32),
            pltpu.SemaphoreType.DMA,
        ],
        compiler_params=PARAMS,
    )(where, conductivity, capacity, place, wall, edge, gain, air_next, *all_bands)
    return solid.reshape(diag_part.shape), air_next


def solution(mesh):
    return jax.shard_map(
        on_device,
        mesh=mesh,
        in_specs=(
            P("sec", "fx", "fy", None, None),
            P("sec", "fx", "fy", None),
            P("sec", "fx", "fy", None, None),
            P("sec", "fx", "fy", None, None),
            P("sec", "fx", "fy", None),
            P("sec", "fx", None),
            P(),
            P(),
            P("sec", "fx", "fy", None),
            P("sec", "fx", "fy", None),
            P(None, "sec", "fy", "fx"),
        ),
        out_specs=(P("sec", "fx", "fy", None), P(None, "sec", "fy", "fx")),
        check_vma=False,
    )
```

time: 530 us -> 65.4 us (0.12)
  the two profiles are of different devices: /device:TPU:0 before, /device:TPU:20 now
where the time goes in v1:
time: 65.4 us; the launch traced here: 65 us
  Pallas kernels  27.8 us (43%)
  waiting for transfers between devices  17.4 us (27%)
  starting transfers between devices  15.8 us (24%)
  local copies, waits for them, and re-layouts  2.06 us (3%)
  other arithmetic  1.2 us (2%)
  between operations  0.8 us (1%)
    ppermute x5, waiting for transfers between devices, pair_swap(): return lax.ppermute(x, axis, pairs) if pairs else jnp.zeros_like(x)  12.7 us
    pallas_call x1, Pallas kernels, on_device(): pl.pallas_call(lambda *refs: solve_kernel(tiles_s, tiles_x, tiles_y, wide...  11.4 us
    ppermute x11, starting transfers between devices, swap(): return lax.ppermute(x, axis, [(i, i ^ mask) for i in range(count)])  8.94 us
    ppermute x5, starting transfers between devices, pair_swap(): return lax.ppermute(x, axis, pairs) if pairs else jnp.zeros_like(x)  6.87 us
    pallas_call x1, Pallas kernels, on_device(): pl.pallas_call(air_kernel, in_specs=[SMEM] + [VMEM] * 7, out_specs=[VMEM]...  6.22 us
    ppermute x11, waiting for transfers between devices, swap(): return lax.ppermute(x, axis, [(i, i ^ mask) for i in range(count)])  4.62 us
    pallas_call x1, Pallas kernels, on_device(): pl.pallas_call(faces_kernel, in_specs=[SMEM, VMEM], out_specs=[VMEM] * 6,...  2.74 us
    pallas_call x1, Pallas kernels, on_device(): pl.pallas_call(stage_kernel, grid=(1,), in_specs=[whole(8, elem_lanes), w...  2.13 us
  transfers between devices with their start and end apart: 16, of which 7 were waited for; matrix products, arithmetic and copies ran while one was open for 3% of the time, Pallas kernels for 19%

profile of v1, /device:TPU:20, one launch (start us, length us, event | category | flops | bytes accessed | tf_op | source)
XLA Modules:
  0.0 65.0 jit_solution(7717928138483009185)
XLA Ops:
  0.6 2.1 %shard_map.104 = (f32[72,128]{1,0:T(8,128)}, s32[24,128]{1,0:T(8,128)}) custom-call(s32[8,2139]{1,0:T(8,128)} %bitcast.10, s32[1,2139]{1,0:T(1,128)} %bitcast.15, f32[24,128]{1,0:T(8,128)} %bitcast.12, f32[24,128]{1,0:T(8,128)} %bitcast.13), custom_call_target="tpu_custom_call" | custom-call | tf_op jit(solution)/shard_map/pallas_call | solution.py:481
  3.2 3.5 %collective-permute-start.7 = (f32[72,128]{1,0:T(8,128)}, f32[72,128]{1,0:T(8,128)S(1)}, u32[]{:S(2)}, u32[]{:S(2)}) collective-permute-start(f32[72,128]{1,0:T(8,128)} %get-tuple-element.27.refs_1_), channel_id=1, source_target_pairs={{0,4},{2,6},{4,0},{6,2},{1,5},{3,7},{5,1},{7,3},{8,12},{10,14},{12... | collective-permute-start | bytes 110600 | tf_op jit(solution)/shard_map/ppermute | solution.py:443
  6.7 0.6 pad_add_fusion.refs_0_.where_ref
  7.3 2.0 %collective-permute-done.7.refs_3_ = f32[72,128]{1,0:T(8,128)S(1)} collective-permute-done((f32[72,128]{1,0:T(8,128)}, f32[72,128]{1,0:T(8,128)S(1)}, u32[]{:S(2)}, u32[]{:S(2)}) %collective-permute-start.7) | collective-permute-done | bytes 36896 | tf_op jit(solution)/shard_map/ppermute | solution.py:443
  9.3 1.6 %collective-permute-done.6.refs_2_ = f32[72,128]{1,0:T(8,128)S(1)} collective-permute-done((f32[72,128]{1,0:T(8,128)}, f32[72,128]{1,0:T(8,128)S(1)}, u32[]{:S(2)}, u32[]{:S(2)}) %collective-permute-start.6) | collective-permute-done | bytes 36896 | tf_op jit(solution)/shard_map/ppermute | solution.py:443
  10.9 0.6 copy-done.13
  11.5 1.7 %shard_map.109.refs_8_ = f32[264,128]{1,0:T(8,128)} custom-call(s32[3]{0:T(128)} %pad_add_fusion.refs_0_.where_ref, f32[72,128]{1,0:T(8,128)} %get-tuple-element.27.refs_1_, f32[72,128]{1,0:T(8,128)} %copy-done.13, f32[72,128]{1,0:T(8,128)} %copy-done.12, f32[72,128]{1,0:T(8,128)} %copy-done.11), custom_call_target="tpu_custom_call" | custom-call | tf_op jit(solution)/shard_map/pallas_call | solution.py:507
  13.2 1.4 %collective-permute-start.11 = (f32[264,128]{1,0:T(8,128)}, f32[264,128]{1,0:T(8,128)S(1)}, u32[]{:S(2)}, u32[]{:S(2)}) collective-permute-start(f32[264,128]{1,0:T(8,128)} %shard_map.109.refs_8_), channel_id=1, source_target_pairs={{0,24},{8,16},{16,8},{24,0},{1,25},{9,17},{17,9},{25,1},{2,26},{10... | collective-permute-start | bytes 405512 | tf_op jit(solution)/shard_map/ppermute | solution.py:443
  14.6 1.5 %collective-permute-start.10 = (f32[264,128]{1,0:T(8,128)}, f32[264,128]{1,0:T(8,128)S(1)}, u32[]{:S(2)}, u32[]{:S(2)}) collective-permute-start(f32[264,128]{1,0:T(8,128)} %shard_map.109.refs_8_), channel_id=1, source_target_pairs={{0,16},{8,24},{16,0},{24,8},{1,17},{9,25},{17,1},{25,9},{2,18},{10... | collective-permute-start | bytes 405512 | tf_op jit(solution)/shard_map/ppermute | solution.py:443
  16.7 2.7 %shard_map.107 = (f32[24,128]{1,0:T(8,128)}, f32[24,128]{1,0:T(8,128)}, f32[4,24,128]{2,1,0:T(8,128)}, f32[4,24,128]{2,1,0:T(8,128)}, f32[4,32,128]{2,1,0:T(8,128)}, /*index=5*/f32[4,32,128]{2,1,0:T(8,128)}) custom-call(s32[3]{0:T(128)} %pad_add_fusion.refs_0_.where_ref, f32[4,24,32,128]{3,2,1,0:T(8,128)} %air_ref.3), custom_call_target="tpu_custom_call" | custom-call | tf_op jit(solution)/shard_map/pallas_call | solution.py:496
  19.4 0.6 reduce
  20.0 1.8 %shard_map.105 = (s32[24,128]{1,0:T(8,128)}, f32[12,128]{1,0:T(8,128)}) custom-call(s32[24,128]{1,0:T(8,128)} %get-tuple-element.16.nodes_ref, s32[12,128]{1,0:T(8,128)} %bitcast.11), custom_call_target="tpu_custom_call" | custom-call | tf_op jit(solution)/shard_map/pallas_call | solution.py:519
  22.4 1.0 %collective-permute-done.refs_3_ = f32[12,128]{1,0:T(8,128)S(1)} collective-permute-done((f32[12,128]{1,0:T(8,128)}, f32[12,128]{1,0:T(8,128)S(1)}, u32[]{:S(2)}, u32[]{:S(2)}) %collective-permute-start) | collective-permute-done | bytes 6176 | tf_op jit(solution)/shard_map/ppermute | solution.py:443
  23.5 3.8 %collective-permute-done.1.x_even = f32[24,128]{1,0:T(8,128)S(1)} collective-permute-done((f32[24,128]{1,0:T(8,128)}, f32[24,128]{1,0:T(8,128)S(1)}, u32[]{:S(2)}, u32[]{:S(2)}) %collective-permute-start.1) | collective-permute-done | bytes 12320 | tf_op jit(solution)/shard_map/ppermute | solution.py:451
  27.3 1.9 %collective-permute-start.2 = (f32[24,128]{1,0:T(8,128)}, f32[24,128]{1,0:T(8,128)S(1)}, u32[]{:S(2)}, u32[]{:S(2)}) collective-permute-start(f32[24,128]{1,0:T(8,128)} %get-tuple-element.20), channel_id=1, source_target_pairs={{2,4},{4,2},{3,5},{5,3},{10,12},{12,10},{11,13},{13,11},{18,20},{2... | collective-permute-start | bytes 36872 | tf_op jit(solution)/shard_map/ppermute | solution.py:451
  29.3 3.8 %collective-permute-done.2.x_odd = f32[24,128]{1,0:T(8,128)S(1)} collective-permute-done((f32[24,128]{1,0:T(8,128)}, f32[24,128]{1,0:T(8,128)S(1)}, u32[]{:S(2)}, u32[]{:S(2)}) %collective-permute-start.2) | collective-permute-done | bytes 12320 | tf_op jit(solution)/shard_map/ppermute | solution.py:451
  34.2 1.5 %collective-permute-start.4 = (f32[4,32,128]{2,1,0:T(8,128)}, f32[4,32,128]{2,1,0:T(8,128)S(1)}, u32[]{:S(2)}, u32[]{:S(2)}) collective-permute-start(f32[4,32,128]{2,1,0:T(8,128)} %get-tuple-element.22), channel_id=1, source_target_pairs={{0,8},{8,0},{16,24},{24,16},{1,9},{9,1},{17,25},{25,17},{2,10},{10... | collective-permute-start | bytes 196616 | tf_op jit(solution)/shard_map/ppermute | solution.py:451
  35.6 3.0 %collective-permute-done.4.z_even = f32[4,32,128]{2,1,0:T(8,128)S(1)} collective-permute-done((f32[4,32,128]{2,1,0:T(8,128)}, f32[4,32,128]{2,1,0:T(8,128)S(1)}, u32[]{:S(2)}, u32[]{:S(2)}) %collective-permute-start.4) | collective-permute-done | bytes 65568 | tf_op jit(solution)/shard_map/ppermute | solution.py:451
  38.6 3.3 %collective-permute-start.5 = (f32[4,32,128]{2,1,0:T(8,128)}, f32[4,32,128]{2,1,0:T(8,128)S(1)}, u32[]{:S(2)}, u32[]{:S(2)}) collective-permute-start(f32[4,32,128]{2,1,0:T(8,128)} %get-tuple-element.23), channel_id=1, source_target_pairs={{8,16},{16,8},{9,17},{17,9},{10,18},{18,10},{11,19},{19,11},{12,20... | collective-permute-start | bytes 196616 | tf_op jit(solution)/shard_map/ppermute | solution.py:451
  42.0 1.8 %shard_map.106.refs_4_ = s32[24,128]{1,0:T(8,128)} custom-call(s32[3]{0:T(128)} %pad_add_fusion.refs_0_.where_ref, s32[24,128]{1,0:T(8,128)} %bitcast.14, f32[12,128]{1,0:T(8,128)} %get-tuple-element.18.refs_2_, f32[12,128]{1,0:T(8,128)} %copy-done.16), custom_call_target="tpu_custom_call" | custom-call | tf_op jit(solution)/shard_map/pallas_call | solution.py:530
  43.8 2.1 %collective-permute-done.5.z_odd = f32[4,32,128]{2,1,0:T(8,128)S(1)} collective-permute-done((f32[4,32,128]{2,1,0:T(8,128)}, f32[4,32,128]{2,1,0:T(8,128)S(1)}, u32[]{:S(2)}, u32[]{:S(2)}) %collective-permute-start.5) | collective-permute-done | bytes 65568 | tf_op jit(solution)/shard_map/ppermute | solution.py:451
  45.9 0.6 broadcast_in_dim.3.y_odd
  46.6 6.2 %shard_map.108 = (f32[4,24,32,128]{3,2,1,0:T(8,128)}, f32[24,8,128]{2,1,0:T(8,128)}, f32[24,128]{1,0:T(8,128)}) custom-call(s32[3]{0:T(128)} %pad_add_fusion.refs_0_.where_ref, f32[4,24,32,128]{3,2,1,0:T(8,128)} %air_ref.3, f32[24,128]{1,0:T(8,128)} %copy-done.14, f32[24,128]{1,0:T(8,128)} %copy-done.15, f32[4,24,128]{2,1,0:T(8,128)} %copy-done.10, ...), custom_call_target="tpu_custom_call" | custom-call | tf_op jit(solution)/shard_map/pallas_call | solution.py:547
  53.6 11.4 %shard_map.110 = (f32[24,128]{1,0:T(8,128)}, f32[4,24,32,128]{3,2,1,0:T(8,128)}) custom-call(s32[3]{0:T(128)} %pad_add_fusion.refs_0_.where_ref, f32[3]{0:T(128)} %refs_1_.1, f32[3]{0:T(128)} %refs_2_.1, s32[24,128]{1,0:T(8,128)} %get-tuple-element.17.refs_3_, s32[24,128]{1,0:T(8,128)} %shard_map.106.refs_4_, ...), custom_call_target="tpu_custom_call", output_to_operand_aliasing={{1}: (7, {})} | custom-call | tf_op jit(solution)/shard_map/pallas_call | solution.py:557
  (54 shorter events, 3.4 us)
Async XLA Ops:
  0.6 18.8 %copy-start.17 = (s32[1,1,1,1536]{3,2,1,0:T(1,128)S(1)}, s32[1,1,1,1536]{3,2,1,0:T(1,128)}, u32[]{:S(2)}) copy-start(s32[1,1,1,1536]{3,2,1,0:T(1,128)} %param.13) | copy-start | bytes 18436
  2.8 4.5 %collective-permute-start.8 = (f32[72,128]{1,0:T(8,128)}, f32[72,128]{1,0:T(8,128)S(1)}, u32[]{:S(2)}, u32[]{:S(2)}) collective-permute-start(f32[72,128]{1,0:T(8,128)} %get-tuple-element.27.refs_1_), channel_id=1, source_target_pairs={{0,6},{2,4},{4,2},{6,0},{1,7},{3,5},{5,3},{7,1},{8,14},{10,12},{12... | collective-permute-start | bytes 110600 | tf_op jit(solution)/shard_map/ppermute | solution.py:443
  3.2 6.1 %collective-permute-start.7 = (f32[72,128]{1,0:T(8,128)}, f32[72,128]{1,0:T(8,128)S(1)}, u32[]{:S(2)}, u32[]{:S(2)}) collective-permute-start(f32[72,128]{1,0:T(8,128)} %get-tuple-element.27.refs_1_), channel_id=1, source_target_pairs={{0,4},{2,6},{4,0},{6,2},{1,5},{3,7},{5,1},{7,3},{8,12},{10,14},{12... | collective-permute-start | bytes 110600 | tf_op jit(solution)/shard_map/ppermute | solution.py:443
  6.7 4.2 %collective-permute-start.6 = (f32[72,128]{1,0:T(8,128)}, f32[72,128]{1,0:T(8,128)S(1)}, u32[]{:S(2)}, u32[]{:S(2)}) collective-permute-start(f32[72,128]{1,0:T(8,128)} %get-tuple-element.27.refs_1_), channel_id=1, source_target_pairs={{0,2},{2,0},{4,6},{6,4},{1,3},{3,1},{5,7},{7,5},{8,10},{10,8},{12,... | collective-permute-start | bytes 110600 | tf_op jit(solution)/shard_map/ppermute | solution.py:443
  13.2 19.9 %copy-start = (f32[264,128]{1,0:T(8,128)S(1)}, f32[264,128]{1,0:T(8,128)}, u32[]{:S(2)}) copy-start(f32[264,128]{1,0:T(8,128)} %shard_map.109.refs_8_) | copy-start | bytes 405508
  13.2 19.9 %collective-permute-start.11 = (f32[264,128]{1,0:T(8,128)}, f32[264,128]{1,0:T(8,128)S(1)}, u32[]{:S(2)}, u32[]{:S(2)}) collective-permute-start(f32[264,128]{1,0:T(8,128)} %shard_map.109.refs_8_), channel_id=1, source_target_pairs={{0,24},{8,16},{16,8},{24,0},{1,25},{9,17},{17,9},{25,1},{2,26},{10... | collective-permute-start | bytes 405512 | tf_op jit(solution)/shard_map/ppermute | solution.py:443
  14.6 19.0 %collective-permute-start.10 = (f32[264,128]{1,0:T(8,128)}, f32[264,128]{1,0:T(8,128)S(1)}, u32[]{:S(2)}, u32[]{:S(2)}) collective-permute-start(f32[264,128]{1,0:T(8,128)} %shard_map.109.refs_8_), channel_id=1, source_target_pairs={{0,16},{8,24},{16,0},{24,8},{1,17},{9,25},{17,1},{25,9},{2,18},{10... | collective-permute-start | bytes 405512 | tf_op jit(solution)/shard_map/ppermute | solution.py:443
  16.2 17.6 %collective-permute-start.9 = (f32[264,128]{1,0:T(8,128)}, f32[264,128]{1,0:T(8,128)S(1)}, u32[]{:S(2)}, u32[]{:S(2)}) collective-permute-start(f32[264,128]{1,0:T(8,128)} %shard_map.109.refs_8_), channel_id=1, source_target_pairs={{0,8},{8,0},{16,24},{24,16},{1,9},{9,1},{17,25},{25,17},{2,10},{10... | collective-permute-start | bytes 405512 | tf_op jit(solution)/shard_map/ppermute | solution.py:443
  19.4 14.7 %collective-permute-start.3 = (f32[4,24,128]{2,1,0:T(8,128)}, f32[4,24,128]{2,1,0:T(8,128)S(1)}, u32[]{:S(2)}, u32[]{:S(2)}) collective-permute-start(f32[4,24,128]{2,1,0:T(8,128)} %get-tuple-element.21), channel_id=1, source_target_pairs={{0,1},{1,0},{2,3},{3,2},{4,5},{5,4},{6,7},{7,6},{8,9},{9,8},{10,11... | collective-permute-start | bytes 147464 | tf_op jit(solution)/shard_map/ppermute | solution.py:451
  21.9 1.5 %collective-permute-start = (f32[12,128]{1,0:T(8,128)}, f32[12,128]{1,0:T(8,128)S(1)}, u32[]{:S(2)}, u32[]{:S(2)}) collective-permute-start(f32[12,128]{1,0:T(8,128)} %get-tuple-element.18.refs_2_), channel_id=1, source_target_pairs={{0,1},{1,0},{2,3},{3,2},{4,5},{5,4},{6,7},{7,6},{8,9},{9,8},{10,11... | collective-permute-start | bytes 18440 | tf_op jit(solution)/shard_map/ppermute | solution.py:443
  23.4 18.6 %copy-start.16 = (f32[12,128]{1,0:T(8,128)}, f32[12,128]{1,0:T(8,128)S(1)}, u32[]{:S(2)}) copy-start(f32[12,128]{1,0:T(8,128)S(1)} %collective-permute-done.refs_3_) | copy-start | bytes 18436
  23.4 3.9 %collective-permute-start.1 = (f32[24,128]{1,0:T(8,128)}, f32[24,128]{1,0:T(8,128)S(1)}, u32[]{:S(2)}, u32[]{:S(2)}) collective-permute-start(f32[24,128]{1,0:T(8,128)} %get-tuple-element.19), channel_id=1, source_target_pairs={{0,2},{2,0},{4,6},{6,4},{1,3},{3,1},{5,7},{7,5},{8,10},{10,8},{12,... | collective-permute-start | bytes 36872 | tf_op jit(solution)/shard_map/ppermute | solution.py:451
  27.3 19.2 %copy-start.14 = (f32[24,128]{1,0:T(8,128)}, f32[24,128]{1,0:T(8,128)S(1)}, u32[]{:S(2)}) copy-start(f32[24,128]{1,0:T(8,128)S(1)} %collective-permute-done.1.x_even) | copy-start | bytes 36868
  27.3 5.8 %collective-permute-start.2 = (f32[24,128]{1,0:T(8,128)}, f32[24,128]{1,0:T(8,128)S(1)}, u32[]{:S(2)}, u32[]{:S(2)}) collective-permute-start(f32[24,128]{1,0:T(8,128)} %get-tuple-element.20), channel_id=1, source_target_pairs={{2,4},{4,2},{3,5},{5,3},{10,12},{12,10},{11,13},{13,11},{18,20},{2... | collective-permute-start | bytes 36872 | tf_op jit(solution)/shard_map/ppermute | solution.py:451
  33.1 13.4 %copy-start.15 = (f32[24,128]{1,0:T(8,128)}, f32[24,128]{1,0:T(8,128)S(1)}, u32[]{:S(2)}) copy-start(f32[24,128]{1,0:T(8,128)S(1)} %collective-permute-done.2.x_odd) | copy-start | bytes 36868
  33.1 19.7 %collective-permute-start.12 = (f32[264,128]{1,0:T(8,128)S(1)}, f32[264,128]{1,0:T(8,128)S(1)}, u32[]{:S(2)}, u32[]{:S(2)}) collective-permute-start(f32[264,128]{1,0:T(8,128)S(1)} %copy-done), channel_id=1, source_target_pairs={{0,1},{1,0},{2,3},{3,2},{4,5},{5,4},{6,7},{7,6},{8,9},{9,8},{10,11... | collective-permute-start | bytes 405512 | tf_op jit(solution)/shard_map/ppermute | solution.py:443
  33.1 19.7 %copy-start.1 = (f32[264,128]{1,0:T(8,128)}, f32[264,128]{1,0:T(8,128)S(1)}, u32[]{:S(2)}) copy-start(f32[264,128]{1,0:T(8,128)S(1)} %collective-permute-done.11.refs_11_) | copy-start | bytes 405508
  33.1 19.7 %collective-permute-start.15 = (f32[264,128]{1,0:T(8,128)S(1)}, f32[264,128]{1,0:T(8,128)S(1)}, u32[]{:S(2)}, u32[]{:S(2)}) collective-permute-start(f32[264,128]{1,0:T(8,128)S(1)} %collective-permute-done.11.refs_11_), channel_id=1, source_target_pairs={{0,1},{1,0},{2,3},{3,2},{4,5},{5,4},{6,7},{7,6},{8,9},{9,8},{10,11... | collective-permute-start | bytes 405512 | tf_op jit(solution)/shard_map/ppermute | solution.py:443
  33.6 19.2 %copy-start.2 = (f32[264,128]{1,0:T(8,128)}, f32[264,128]{1,0:T(8,128)S(1)}, u32[]{:S(2)}) copy-start(f32[264,128]{1,0:T(8,128)S(1)} %collective-permute-done.10.refs_10_) | copy-start | bytes 405508
  33.6 19.2 %collective-permute-start.14 = (f32[264,128]{1,0:T(8,128)S(1)}, f32[264,128]{1,0:T(8,128)S(1)}, u32[]{:S(2)}, u32[]{:S(2)}) collective-permute-start(f32[264,128]{1,0:T(8,128)S(1)} %collective-permute-done.10.refs_10_), channel_id=1, source_target_pairs={{0,1},{1,0},{2,3},{3,2},{4,5},{5,4},{6,7},{7,6},{8,9},{9,8},{10,11... | collective-permute-start | bytes 405512 | tf_op jit(solution)/shard_map/ppermute | solution.py:443
  33.7 19.2 %copy-start.3 = (f32[264,128]{1,0:T(8,128)}, f32[264,128]{1,0:T(8,128)S(1)}, u32[]{:S(2)}) copy-start(f32[264,128]{1,0:T(8,128)S(1)} %collective-permute-done.9.refs_9_) | copy-start | bytes 405508
  33.7 19.1 %collective-permute-start.13 = (f32[264,128]{1,0:T(8,128)S(1)}, f32[264,128]{1,0:T(8,128)S(1)}, u32[]{:S(2)}, u32[]{:S(2)}) collective-permute-start(f32[264,128]{1,0:T(8,128)S(1)} %collective-permute-done.9.refs_9_), channel_id=1, source_target_pairs={{0,1},{1,0},{2,3},{3,2},{4,5},{5,4},{6,7},{7,6},{8,9},{9,8},{10,11... | collective-permute-start | bytes 405512 | tf_op jit(solution)/shard_map/ppermute | solution.py:443
  34.2 4.5 %collective-permute-start.4 = (f32[4,32,128]{2,1,0:T(8,128)}, f32[4,32,128]{2,1,0:T(8,128)S(1)}, u32[]{:S(2)}, u32[]{:S(2)}) collective-permute-start(f32[4,32,128]{2,1,0:T(8,128)} %get-tuple-element.22), channel_id=1, source_target_pairs={{0,8},{8,0},{16,24},{24,16},{1,9},{9,1},{17,25},{25,17},{2,10},{10... | collective-permute-start | bytes 196616 | tf_op jit(solution)/shard_map/ppermute | solution.py:451
  38.6 7.3 %collective-permute-start.5 = (f32[4,32,128]{2,1,0:T(8,128)}, f32[4,32,128]{2,1,0:T(8,128)S(1)}, u32[]{:S(2)}, u32[]{:S(2)}) collective-permute-start(f32[4,32,128]{2,1,0:T(8,128)} %get-tuple-element.23), channel_id=1, source_target_pairs={{8,16},{16,8},{9,17},{17,9},{10,18},{18,10},{11,19},{19,11},{12,20... | collective-permute-start | bytes 196616 | tf_op jit(solution)/shard_map/ppermute | solution.py:451
  (10 other events, 29.7 us)

commit v2 on v1

--- a/solution.py
+++ b/solution.py
@@ -19,7 +19,6 @@
 VMEM = pl.BlockSpec(memory_space=pltpu.VMEM)
 SMEM = pl.BlockSpec(memory_space=pltpu.SMEM)
 ANY = pl.BlockSpec(memory_space=pl.ANY)
-PARAMS = pltpu.CompilerParams(vmem_limit_bytes=56 * 1024 * 1024)
 
 EW = NW - 1
 EH = NH - 1
@@ -85,7 +84,14 @@
     return corner, column
 
 
-def stage_kernel(conn_ref, material_ref, diag_ref, source_ref, pay_ref, nodes_ref):
+def stage_kernel(
+    conn_ref, material_ref, diag_ref, source_ref, air_hbm,
+    plain_ref, even_ref, odd_ref, nodes_ref, y_even, y_odd, z_even, z_odd, air_ref,
+    sem,
+):
+    sec, fx, fy = (lax.axis_index(axis) for axis in ("sec", "fx", "fy"))
+    load = pltpu.make_async_copy(air_hbm, air_ref, sem)
+    load.start()
     corner_np, column_np = element_keys()
     pieces, kinds = [], []
     for j in range(NH // SUBS):
@@ -119,36 +125,15 @@
         kinds.append(kind)
     nodes = jnp.concatenate(pieces, axis=0)
     nodes_ref[...] = nodes
-    pay_ref[0:ROWS] = look_up([diag_ref[r : r + 1] for r in range(ROWS)], nodes)
-    pay_ref[ROWS : 2 * ROWS] = look_up([source_ref[r : r + 1] for r in range(ROWS)], nodes)
-    pay_ref[2 * ROWS : 3 * ROWS] = jnp.concatenate(kinds, axis=0).astype(jnp.float32) + 1.0
-
-
-def band_kernel(tiles_x, wide, where_ref, *refs):
-    parts, band_ref, held = refs[:tiles_x], refs[tiles_x], refs[tiles_x + 1]
-    fx = where_ref[1]
-    for k, part in enumerate(parts):
-        held[fx ^ k] = part[...]
-    lane = iota((NH, wide), 1)
-    at = 0
-    for field in range(3):
-        for t in range(NT if field < 2 else ET):
-            total = None
-            for f in range(tiles_x):
-                x = held[f, field * ROWS : (field + 1) * ROWS]
-                if wide > LANES:
-                    x = jnp.concatenate([x, jnp.zeros((NH, wide - LANES), jnp.float32)], axis=1)
-                shift = (EW * f - NW * t) % wide
-                if shift:
-                    x = pltpu.roll(x, shift, 1)
-                x = jnp.where((lane >= EW * f) & (lane < EW * f + NW), x, 0.0)
-                total = x if total is None else total + x
-            band_ref[at : at + NH] = total
-            at += NH
-
-
-def faces_kernel(where_ref, air_ref, x_even, x_odd, y_even, y_odd, z_even, z_odd):
-    sec, fx, fy = where_ref[0], where_ref[1], where_ref[2]
+    diag = look_up([diag_ref[r : r + 1] for r in range(ROWS)], nodes)
+    source = look_up([source_ref[r : r + 1] for r in range(ROWS)], nodes)
+    kind = jnp.concatenate(kinds, axis=0).astype(jnp.float32) + 1.0
+    for ref in (plain_ref, even_ref, odd_ref):
+        ref[0:ROWS] = diag
+        ref[ROWS : 2 * ROWS] = source
+        ref[2 * ROWS : 3 * ROWS] = kind
+
+    load.wait()
     fields, cells_z, cells_y, cells_x = air_ref.shape
     z_up = (sec & 1) == 0
     z_even[...] = air_ref[:, jnp.where(z_up, cells_z - 1, 0)]
@@ -172,24 +157,53 @@
         highs.append(high)
     low = pltpu.roll(jnp.concatenate(lows, axis=0), LANES - 1, 1)
     high = jnp.concatenate(highs, axis=0)
-    x_even[...] = jnp.where(x_up, high, low).T[:cells_z]
-    x_odd[...] = jnp.where(x_up, low, high).T[:cells_z]
-
-
-def air_kernel(
-    where_ref, air_ref, x_even, x_odd, y_even, y_odd, z_even, z_odd, next_ref, edge_ref, gain_ref,
-    west_ref, east_ref,
-):
-    sec, fx, fy = where_ref[0], where_ref[1], where_ref[2]
+    even_ref[3 * ROWS :] = jnp.where(x_up, high, low).T[:cells_z]
+    odd_ref[3 * ROWS :] = jnp.where(x_up, low, high).T[:cells_z]
+
+
+def band_kernel(tiles_x, wide, *refs):
+    parts, band_ref, held = refs[:tiles_x], refs[tiles_x], refs[tiles_x + 1]
+    fx = lax.axis_index("fx")
+    for k, part in enumerate(parts):
+        held[fx ^ k] = part[0 : 3 * ROWS]
+    lane = iota((NH, wide), 1)
+    at = 0
+    for field in range(3):
+        for t in range(NT if field < 2 else ET):
+            total = None
+            for f in range(tiles_x):
+                x = held[f, field * ROWS : (field + 1) * ROWS]
+                if wide > LANES:
+                    x = jnp.concatenate([x, jnp.zeros((NH, wide - LANES), jnp.float32)], axis=1)
+                shift = (EW * f - NW * t) % wide
+                if shift:
+                    x = pltpu.roll(x, shift, 1)
+                x = jnp.where((lane >= EW * f) & (lane < EW * f + NW), x, 0.0)
+                total = x if total is None else total + x
+            band_ref[at : at + NH] = total
+            at += NH
+
+
+def air_kernel(tiles_s, tiles_x, tiles_y, air_ref, z_even, z_odd, *refs):
+    refs = list(refs)
+    y_even = refs.pop(0)
+    y_odd = refs.pop(0) if tiles_y > 2 else None
+    x_even = refs.pop(0)
+    x_odds = [(m, refs.pop(0)) for m in odd_masks(tiles_x)]
+    next_hbm, edge_ref, gain_ref, west_ref, east_ref, next_ref, sem = refs
+    sec, fx, fy = (lax.axis_index(axis) for axis in ("sec", "fx", "fy"))
     fields, cells_z, cells_y, cells_x = air_ref.shape
-    pad = jnp.zeros((LANES - cells_z, LANES), jnp.float32)
-    even = jnp.concatenate([x_even[...], pad], axis=0).T
-    odd = jnp.concatenate([x_odd[...], pad], axis=0).T
     x_up = (fx & 1) == 0
-    west_ref[...] = jnp.where(x_up, odd, even)
-    east_ref[...] = jnp.where(x_up, even, odd)
     y_up = (fy & 1) == 0
     z_up = (sec & 1) == 0
+    even = x_even[3 * ROWS :]
+    odd = jnp.zeros_like(even)
+    partner = jnp.where(x_up, fx - 1, fx + 1)
+    for m, ref in x_odds:
+        odd = jnp.where((fx ^ partner) == m, ref[3 * ROWS :], odd)
+    pad = jnp.zeros((LANES - cells_z, LANES), jnp.float32)
+    west_ref[...] = jnp.concatenate([jnp.where(x_up, odd, even), pad], axis=0).T
+    east_ref[...] = jnp.concatenate([jnp.where(x_up, even, odd), pad], axis=0).T
     row = iota((cells_y, LANES), 0)
     lane = iota((cells_y, LANES), 1)
     half = 0.5 * time_step
@@ -212,7 +226,8 @@
                 pltpu.roll(east_ref[span], LANES - 1 - z, 1),
                 pltpu.roll(x, LANES - 1, 1),
             )
-            y_e, y_o = y_even[f, pl.ds(z, 1), :], y_odd[f, pl.ds(z, 1), :]
+            y_e = y_even[f, pl.ds(z, 1), :]
+            y_o = y_odd[f, pl.ds(z, 1), :] if y_odd is not None else jnp.zeros_like(y_e)
             south_ghost = jnp.where(y_up, y_o, y_e)
             north_ghost = jnp.where(y_up, y_e, y_o)
             south = jnp.where(row == 0, south_ghost, pltpu.roll(x, 1, 0))
@@ -235,13 +250,23 @@
     def ghost_high(f):
         return jnp.where(z_up, z_even[f], z_odd[f])
 
-    layer(0, ghost_low, lambda f: air_ref[f, 1])
-
-    @pl.loop(1, cells_z - 1)
-    def _(z):
-        layer(z, lambda f: air_ref[f, z - 1], lambda f: air_ref[f, z + 1])
-
-    layer(cells_z - 1, lambda f: air_ref[f, cells_z - 2], ghost_high)
+    steps = 4
+    depth = cells_z // steps
+    for step in range(steps):
+        start, stop = step * depth, (step + 1) * depth
+        if start == 0:
+            layer(0, ghost_low, lambda f: air_ref[f, 1])
+
+        @pl.loop(max(start, 1), min(stop, cells_z - 1))
+        def _(z):
+            layer(z, lambda f: air_ref[f, z - 1], lambda f: air_ref[f, z + 1])
+
+        if stop == cells_z:
+            layer(cells_z - 1, lambda f: air_ref[f, cells_z - 2], ghost_high)
+        pltpu.make_async_copy(
+            next_ref.at[:, start:stop], next_hbm.at[:, start:stop], sem
+        ).start()
+    pltpu.make_async_copy(next_ref, next_hbm, sem).wait()
 
 
 def place_kernel(nodes_ref, iface_ref, place_ref, rows_ref):
@@ -251,12 +276,16 @@
     high, low = spread(nodes, [at_row, at_lane])
     place = high * LANES + low
     place_ref[...] = place.astype(jnp.int32)
-    rows_ref[...] = look_up([place[r : r + 1] for r in range(ROWS)], iface_ref[...])
-
-
-def face_kernel(tiles_y, where_ref, face_ref, *refs):
+    count = iface_ref.shape[-1] // LANES
+    iface = jnp.concatenate(
+        [iface_ref[0:1, LANES * r : LANES * (r + 1)] for r in range(count)], axis=0
+    )
+    rows_ref[...] = look_up([place[r : r + 1] for r in range(ROWS)], iface)
+
+
+def face_kernel(tiles_y, face_ref, *refs):
     parts, wall_ref, held = refs[:tiles_y], refs[tiles_y], refs[tiles_y + 1]
-    fy = where_ref[2]
+    fy = lax.axis_index("fy")
     for k, part in enumerate(parts):
         held[fy ^ k] = part[...] + (fy ^ k).astype(jnp.float32) * (ROWS * LANES)
     rows = jnp.concatenate([held[j] for j in range(tiles_y)], axis=0)
@@ -270,13 +299,13 @@
 
 def solve_kernel(
     tiles_s, tiles_x, tiles_y, wide, material_count,
-    where_ref, conduct_ref, capacity_ref, place_ref, wall_ref, edge_ref, gain_ref, air_ref, *refs,
+    conduct_ref, capacity_ref, place_ref, wall_ref, edge_ref, gain_ref, air_ref, *refs,
 ):
     bands = tiles_s * tiles_y
     parts = refs[:bands]
     solid_ref, next_ref = refs[bands : bands + 2]
-    (held, elem, side, main, inv, res, dirn, image, sol, table, edge, sem) = refs[bands + 2 :]
-    sec, fx, fy = where_ref[0], where_ref[1], where_ref[2]
+    (held, elem, side, main, inv, res, dirn, image, sol, table, edge, solid, sem) = refs[bands + 2 :]
+    sec, fx, fy = (lax.axis_index(axis) for axis in ("sec", "fx", "fy"))
     for j in range(tiles_y):
         for k in range(tiles_s):
             held[(sec ^ k) * tiles_y + (fy ^ j)] = parts[j * tiles_s + k][...]
@@ -309,7 +338,9 @@
                 ref[k, t, 0:1, :] = both
 
     def each_band(body, total=None):
-        return lax.fori_loop(0, bands, body, total)
+        for b in range(bands):
+            total = body(b, total)
+        return total
 
     def prepare(b, _):
         cells, own = [], []
@@ -343,7 +374,7 @@
     zero = jnp.zeros((NH, wide), jnp.float32)
 
     def count_once(b, x):
-        return jnp.where(first_row & (b > 0), 0.0, x)
+        return jnp.where(first_row, 0.0, x) if b else x
 
     def total_of(x):
         return jnp.sum(jnp.sum(x, axis=0, keepdims=True), axis=1, keepdims=True)
@@ -355,7 +386,6 @@
             r = res[b, t]
             z = r * d
             dirn[b, t] = z
-            sol[b, t] = zero
             acc = acc + count_once(b, r * z)
         return acc
 
@@ -404,17 +434,19 @@
         if not last:
             seams(image)
 
-        def update(b, acc, step_len=step_len, last=last):
+        def update(b, acc, step_len=step_len):
             for t in range(NT):
-                sol[b, t] = sol[b, t] + step_len * dirn[b, t]
-                if not last:
-                    r = res[b, t] - step_len * image[b, t]
-                    res[b, t] = r
-                    acc = acc + count_once(b, r * r * inv[b, t])
+                r = res[b, t] - step_len * image[b, t]
+                res[b, t] = r
+                acc = acc + count_once(b, r * r * inv[b, t])
             return acc
 
-        gamma_next = total_of(each_band(update, zero))
+        for j in range(tiles_y):
+            for t in range(NT):
+                x = step_len * dirn[sec * tiles_y + j, t]
+                sol[j, t] = x if iteration == 0 else sol[j, t] + x
         if not last:
+            gamma_next = total_of(each_band(update, zero))
             beta = gamma_next / gamma
             gamma = gamma_next
 
@@ -422,20 +454,27 @@
         packed = jnp.zeros((NH, LANES), jnp.float32)
         spot = iota((NH, LANES), 1) >> 5
         for t in range(NT):
-            x = sol[sec * tiles_y + j, t]
+            x = sol[j, t]
             x = pltpu.roll(x, (NW * t - EW * fx + tiles_x * wide) % wide, 1)[:, :LANES]
             packed = jnp.where(spot == t, x, packed)
         table[j] = packed
-    solid_ref[...] = look_up([table[fy, r : r + 1] for r in range(ROWS)], place_ref[...])
+    solid[...] = look_up([table[fy, r : r + 1] for r in range(ROWS)], place_ref[...])
+    first = pltpu.make_async_copy(solid, solid_ref, sem.at[0])
+    first.start()
     rows = [table[j, r : r + 1] for j in range(tiles_y) for r in range(ROWS)]
     extra = look_up(rows, wall_ref[...]) * gain_ref[...]
     cells_z = edge_ref.shape[0]
     top = iota((SUBS, LANES), 0) == 0
     for z in range(cells_z):
         edge[z] = edge_ref[z] + jnp.where(top, extra[z : z + 1], 0.0)
-    copy = pltpu.make_async_copy(edge, next_ref.at[0, :, 0:SUBS, :], sem)
-    copy.start()
-    copy.wait()
+    second = pltpu.make_async_copy(edge, next_ref.at[0, :, 0:SUBS, :], sem.at[1])
+    second.start()
+    first.wait()
+    second.wait()
+
+
+def odd_masks(count):
+    return sorted({i ^ (i + 1) for i in range(1, count - 1, 2)})
 
 
 def swap(x, axis, mask):
@@ -469,109 +508,131 @@
     bands = tiles_s * tiles_y
     wide = -(-(EW * tiles_x + 1) // LANES) * LANES
     elem_lanes = -(-ELEMS // LANES) * LANES
-    where = jnp.stack([lax.axis_index(axis) for axis in ("sec", "fx", "fy")]).astype(jnp.int32)
     fields, cells_z, cells_y, cells_x = air_state.shape
+
+    def call(kernel, args, specs, outs, out_specs, scratch=(), **more):
+        held = list(args) + list(outs) + [s for s in scratch if hasattr(s, "shape")]
+        need = sum(4 * int(np.prod(x.shape)) for x in held)
+        return pl.pallas_call(
+            kernel,
+            in_specs=specs,
+            out_specs=out_specs,
+            out_shape=outs,
+            scratch_shapes=list(scratch),
+            compiler_params=pltpu.CompilerParams(vmem_limit_bytes=need + (6 << 20)),
+            **more,
+        )(*args)
 
     def shape(*dims):
         return jax.ShapeDtypeStruct(dims, f32)
 
+    def ints(*dims):
+        return jax.ShapeDtypeStruct(dims, jnp.int32)
+
     def whole(*dims):
         return pl.BlockSpec(dims, lambda i: (0,) * len(dims))
 
-    pay, nodes = pl.pallas_call(
+    plain, even, odd, nodes, y_even, y_odd, z_even, z_odd, air = call(
         stage_kernel,
+        [
+            conn.reshape(conn.shape[-2:]),
+            material.reshape(1, -1),
+            diag_part.reshape(ROWS, LANES),
+            heat_source.reshape(ROWS, LANES),
+            air_state,
+        ],
+        [
+            whole(8, elem_lanes),
+            whole(1, elem_lanes),
+            whole(ROWS, LANES),
+            whole(ROWS, LANES),
+            ANY,
+        ],
+        [
+            shape(3 * ROWS, LANES),
+            shape(3 * ROWS + cells_z, LANES),
+            shape(3 * ROWS + cells_z, LANES),
+            ints(ROWS, LANES),
+            shape(fields, cells_z, cells_x),
+            shape(fields, cells_z, cells_x),
+            shape(fields, cells_y, cells_x),
+            shape(fields, cells_y, cells_x),
+            shape(*air_state.shape),
+        ],
+        [VMEM] * 9,
+        [pltpu.SemaphoreType.DMA],
         grid=(1,),
-        in_specs=[whole(8, elem_lanes), whole(1, elem_lanes), whole(ROWS, LANES), whole(ROWS, LANES)],
-        out_specs=[whole(3 * ROWS, LANES), whole(ROWS, LANES)],
-        out_shape=[shape(3 * ROWS, LANES), jax.ShapeDtypeStruct((ROWS, LANES), jnp.int32)],
-        compiler_params=PARAMS,
-    )(
-        conn.reshape(conn.shape[-2:]),
-        material.reshape(1, -1),
-        diag_part.reshape(ROWS, LANES),
-        heat_source.reshape(ROWS, LANES),
-    )
-    pays = [pay] + [swap(pay, "fx", k) for k in range(1, tiles_x)]
-
-    faces = pl.pallas_call(
-        faces_kernel,
-        in_specs=[SMEM, VMEM],
-        out_specs=[VMEM] * 6,
-        out_shape=[shape(cells_z, fields * cells_y)] * 2
-        + [shape(fields, cells_z, cells_x)] * 2
-        + [shape(fields, cells_y, cells_x)] * 2,
-        compiler_params=PARAMS,
-    )(where, air_state)
-    x_even, x_odd, y_even, y_odd, z_even, z_odd = faces
-
-    band = pl.pallas_call(
+    )
+    odds = odd_masks(tiles_x)
+    pays = [plain] + [
+        swap(even if k == 1 else odd if k in odds else plain, "fx", k) for k in range(1, tiles_x)
+    ]
+    z_even, z_odd = pair_swap(z_even, "sec", 0), pair_swap(z_odd, "sec", 1)
+    y_ghosts = [pair_swap(y_even, "fy", 0)]
+    if tiles_y > 2:
+        y_ghosts.append(pair_swap(y_odd, "fy", 1))
+
+    place, rows = call(
+        place_kernel,
+        [nodes, iface_node.reshape(1, -1)],
+        [VMEM] * 2,
+        [ints(ROWS, LANES), shape(iface_node.shape[-1] // LANES, LANES)],
+        [VMEM] * 2,
+    )
+
+    band = call(
         lambda *refs: band_kernel(tiles_x, wide, *refs),
-        in_specs=[SMEM] + [VMEM] * tiles_x,
-        out_specs=VMEM,
-        out_shape=shape(BAND_ROWS, wide),
-        scratch_shapes=[pltpu.VMEM((tiles_x, 3 * ROWS, LANES), f32)],
-        compiler_params=PARAMS,
-    )(where, *pays)
-
+        pays,
+        [VMEM] * tiles_x,
+        [shape(BAND_ROWS, wide)],
+        [VMEM],
+        [pltpu.VMEM((tiles_x, 3 * ROWS, LANES), f32)],
+    )[0]
     own_bands = [band] + [swap(band, "sec", k) for k in range(1, tiles_s)]
     all_bands = own_bands + [swap(b, "fy", j) for j in range(1, tiles_y) for b in own_bands]
-
-    place, rows = pl.pallas_call(
-        place_kernel,
-        in_specs=[VMEM] * 2,
-        out_specs=[VMEM] * 2,
-        out_shape=[
-            jax.ShapeDtypeStruct((ROWS, LANES), jnp.int32),
-            shape(iface_node.shape[-1] // LANES, LANES),
-        ],
-        compiler_params=PARAMS,
-    )(nodes, iface_node.reshape(-1, LANES))
     all_rows = [rows] + [swap(rows, "fy", j) for j in range(1, tiles_y)]
-    wall = pl.pallas_call(
+
+    wall = call(
         lambda *refs: face_kernel(tiles_y, *refs),
-        in_specs=[SMEM, VMEM] + [VMEM] * tiles_y,
-        out_specs=VMEM,
-        out_shape=jax.ShapeDtypeStruct((cells_z, LANES), jnp.int32),
-        scratch_shapes=[pltpu.VMEM((tiles_y,) + rows.shape, f32)],
-        compiler_params=PARAMS,
-    )(where, face_of_row.reshape(-1, LANES), *all_rows)
-
-    ghosts = [
-        pair_swap(x_even, "fx", 0),
-        pair_swap(x_odd, "fx", 1),
-        pair_swap(y_even, "fy", 0),
-        pair_swap(y_odd, "fy", 1),
-        pair_swap(z_even, "sec", 0),
-        pair_swap(z_odd, "sec", 1),
-    ]
-    air_next, edge, gain = pl.pallas_call(
-        air_kernel,
-        in_specs=[SMEM] + [VMEM] * 7,
-        out_specs=[VMEM] * 3,
-        out_shape=[shape(*air_state.shape), shape(cells_z, SUBS, LANES), shape(cells_z, LANES)],
-        scratch_shapes=[pltpu.VMEM((LANES, LANES), f32)] * 2,
-        compiler_params=PARAMS,
-    )(where, air_state, *ghosts)
+        [face_of_row.reshape(-1, LANES)] + all_rows,
+        [VMEM] * (1 + tiles_y),
+        [ints(cells_z, LANES)],
+        [VMEM],
+        [pltpu.VMEM((tiles_y,) + rows.shape, f32)],
+    )[0]
+
+    ghosts = [z_even, z_odd] + y_ghosts + [pays[1]] + [pays[m] for m in odds]
+    air_next, edge, gain = call(
+        lambda *refs: air_kernel(tiles_s, tiles_x, tiles_y, *refs),
+        [air] + ghosts,
+        [VMEM] * (1 + len(ghosts)),
+        [shape(*air_state.shape), shape(cells_z, SUBS, LANES), shape(cells_z, LANES)],
+        [ANY, VMEM, VMEM],
+        [pltpu.VMEM((LANES, LANES), f32)] * 2
+        + [pltpu.VMEM(air_state.shape, f32), pltpu.SemaphoreType.DMA],
+    )
 
     grid = (bands, NT, NH, wide)
-    solid, air_next = pl.pallas_call(
+    solid, air_next = call(
         lambda *refs: solve_kernel(
             tiles_s, tiles_x, tiles_y, wide, conductivity.shape[0], *refs
         ),
-        in_specs=[SMEM] * 3 + [VMEM] * 4 + [ANY] + [VMEM] * bands,
-        out_specs=[VMEM, ANY],
-        out_shape=[shape(ROWS, LANES), shape(*air_state.shape)],
-        input_output_aliases={7: 1},
-        scratch_shapes=[pltpu.VMEM((bands, BAND_ROWS, wide), f32)]
+        [conductivity, capacity, place, wall, edge, gain, air_next] + all_bands,
+        [SMEM] * 2 + [VMEM] * 4 + [ANY] + [VMEM] * bands,
+        [shape(ROWS, LANES), shape(*air_state.shape)],
+        [ANY, ANY],
+        [pltpu.VMEM((bands, BAND_ROWS, wide), f32)]
         + [pltpu.VMEM((bands, ET, NH, wide), f32)] * 2
-        + [pltpu.VMEM(grid, f32)] * 6
+        + [pltpu.VMEM(grid, f32)] * 5
         + [
+            pltpu.VMEM((tiles_y, NT, NH, wide), f32),
             pltpu.VMEM((tiles_y, ROWS, LANES), f32),
             pltpu.VMEM((cells_z, SUBS, LANES), f32),
-            pltpu.SemaphoreType.DMA,
+            pltpu.VMEM((ROWS, LANES), f32),
+            pltpu.SemaphoreType.DMA((2,)),
         ],
-        compiler_params=PARAMS,
-    )(where, conductivity, capacity, place, wall, edge, gain, air_next, *all_bands)
+        input_output_aliases={6: 1},
+    )
     return solid.reshape(diag_part.shape), air_next
 
 

time: 65.4 us -> 48 us (0.73)
  the two profiles are of different devices: /device:TPU:20 before, /device:TPU:2 now
where the time goes in v2:
time: 48 us; the launch traced here: 47.6 us
  waiting for transfers between devices  15.1 us (31%)
  Pallas kernels  14.1 us (29%)
  starting transfers between devices  13.2 us (28%)
  local copies, waits for them, and re-layouts  4.41 us (9%)
  between operations  0.77 us (2%)
    pallas_call x6, Pallas kernels, call(): pl.pallas_call(kernel, in_specs=specs, out_specs=out_specs, out_shape=out...  14.1 us
    ppermute x11, starting transfers between devices, swap(): return lax.ppermute(x, axis, [(i, i ^ mask) for i in range(count)])  9.12 us
    ppermute x11, waiting for transfers between devices, swap(): return lax.ppermute(x, axis, [(i, i ^ mask) for i in range(count)])  8.27 us
    ppermute x3, waiting for transfers between devices, pair_swap(): return lax.ppermute(x, axis, pairs) if pairs else jnp.zeros_like(x)  6.86 us
    unnamed x18, local copies, waits for them, and re-layouts  4.41 us
    ppermute x3, starting transfers between devices, pair_swap(): return lax.ppermute(x, axis, pairs) if pairs else jnp.zeros_like(x)  4.03 us
  transfers between devices with their start and end apart: 14, of which 7 were waited for; matrix products, arithmetic and copies ran while one was open for 0% of the time, Pallas kernels for 11%

profile of v2, /device:TPU:2, one launch (start us, length us, event | category | flops | bytes accessed | tf_op | source)
XLA Modules:
  0.0 47.6 jit_solution(10304793411125237248)
XLA Ops:
  0.7 1.4 %copy-done = f32[4,24,32,128]{3,2,1,0:T(8,128)S(1)} copy-done((f32[4,24,32,128]{3,2,1,0:T(8,128)S(1)}, f32[4,24,32,128]{3,2,1,0:T(8,128)}, u32[]{:S(2)}) %copy-start) | copy-done | bytes 1572888
  2.1 0.9 %copy-done.1 = s32[1,1,1,8,2139]{4,3,2,1,0:T(8,128)S(1)} copy-done((s32[1,1,1,8,2139]{4,3,2,1,0:T(8,128)S(1)}, s32[1,1,1,8,2139]{4,3,2,1,0:T(8,128)}, u32[]{:S(2)}) %copy-start.1) | copy-done | bytes 68472
  2.9 0.7 %copy-done.2 = f32[1,1,1,3072]{3,2,1,0:T(1,128)S(1)} copy-done((f32[1,1,1,3072]{3,2,1,0:T(1,128)S(1)}, f32[1,1,1,3072]{3,2,1,0:T(1,128)}, u32[]{:S(2)}) %copy-start.2) | copy-done | bytes 12312
  3.7 0.7 %copy-done.3 = f32[1,1,1,3072]{3,2,1,0:T(1,128)S(1)} copy-done((f32[1,1,1,3072]{3,2,1,0:T(1,128)S(1)}, f32[1,1,1,3072]{3,2,1,0:T(1,128)}, u32[]{:S(2)}) %copy-start.3) | copy-done | bytes 12312
  4.4 0.7 %copy-done.5 = s32[1,1,1,2139]{3,2,1,0:T(1,128)S(1)} copy-done((s32[1,1,1,2139]{3,2,1,0:T(1,128)S(1)}, s32[1,1,1,2139]{3,2,1,0:T(1,128)}, u32[]{:S(2)}) %copy-start.5) | copy-done | bytes 8580
  5.1 2.0 %shard_map.104 = (f32[72,128]{1,0:T(8,128)S(1)}, f32[96,128]{1,0:T(8,128)S(1)}, f32[96,128]{1,0:T(8,128)S(1)}, s32[24,128]{1,0:T(8,128)S(1)}, f32[4,24,128]{2,1,...) custom-call(s32[8,2139]{1,0:T(8,128)S(1)} %bitcast.7, ...), custom_call_target="tpu_custom_call" | custom-call | tf_op jit(solution)/shard_map/pallas_call | solution.py:516
  7.1 1.6 %collective-permute-start.4 = (f32[96,128]{1,0:T(8,128)S(1)}, f32[96,128]{1,0:T(8,128)S(1)}, u32[]{:S(2)}, u32[]{:S(2)}) collective-permute-start(f32[96,128]{1,0:T(8,128)S(1)} %get-tuple-element.24), channel_id=1, source_target_pairs={{0,2},{2,0},{4,6},{6,4},{1,3},{3,1},{5,7},{7,5},{8,10},{10,8},{12,... | collective-permute-start | bytes 147464 | tf_op jit(solution)/shard_map/ppermute | solution.py:482
  8.7 2.5 %collective-permute-start.5 = (f32[96,128]{1,0:T(8,128)S(1)}, f32[96,128]{1,0:T(8,128)S(1)}, u32[]{:S(2)}, u32[]{:S(2)}) collective-permute-start(f32[96,128]{1,0:T(8,128)S(1)} %get-tuple-element.25), channel_id=1, source_target_pairs={{0,6},{2,4},{4,2},{6,0},{1,7},{3,5},{5,3},{7,1},{8,14},{10,12},{12... | collective-permute-start | bytes 147464 | tf_op jit(solution)/shard_map/ppermute | solution.py:482
  11.3 5.1 %collective-permute-done.6.refs_2_ = f32[72,128]{1,0:T(8,128)S(1)} collective-permute-done((f32[72,128]{1,0:T(8,128)S(1)}, f32[72,128]{1,0:T(8,128)S(1)}, u32[]{:S(2)}, u32[]{:S(2)}) %collective-permute-start.6) | collective-permute-done | bytes 36896 | tf_op jit(solution)/shard_map/ppermute | solution.py:482
  16.7 1.6 %collective-permute-start.9 = (f32[264,128]{1,0:T(8,128)S(1)}, f32[264,128]{1,0:T(8,128)S(1)}, u32[]{:S(2)}, u32[]{:S(2)}) collective-permute-start(f32[264,128]{1,0:T(8,128)S(1)} %shard_map.108.refs_7_), channel_id=1, source_target_pairs={{0,24},{8,16},{16,8},{24,0},{1,25},{9,17},{17,9},{25,1},{2,26},{10... | collective-permute-start | bytes 405512 | tf_op jit(solution)/shard_map/ppermute | solution.py:482
  18.2 0.5 %collective-permute-start.8 = (f32[264,128]{1,0:T(8,128)S(1)}, f32[264,128]{1,0:T(8,128)S(1)}, u32[]{:S(2)}, u32[]{:S(2)}) collective-permute-start(f32[264,128]{1,0:T(8,128)S(1)} %shard_map.108.refs_7_), channel_id=1, source_target_pairs={{0,16},{8,24},{16,0},{24,8},{1,17},{9,25},{17,1},{25,9},{2,18},{10... | collective-permute-start | bytes 405512 | tf_op jit(solution)/shard_map/ppermute | solution.py:482
  18.7 1.5 %collective-permute-start.7 = (f32[264,128]{1,0:T(8,128)S(1)}, f32[264,128]{1,0:T(8,128)S(1)}, u32[]{:S(2)}, u32[]{:S(2)}) collective-permute-start(f32[264,128]{1,0:T(8,128)S(1)} %shard_map.108.refs_7_), channel_id=1, source_target_pairs={{0,8},{8,0},{16,24},{24,16},{1,9},{9,1},{17,25},{25,17},{2,10},{10... | collective-permute-start | bytes 405512 | tf_op jit(solution)/shard_map/ppermute | solution.py:482
  20.2 0.5 %shard_map.105 = (s32[24,128]{1,0:T(8,128)S(1)}, f32[12,128]{1,0:T(8,128)S(1)}) custom-call(s32[24,128]{1,0:T(8,128)S(1)} %get-tuple-element.17.nodes_ref, s32[1,1536]{1,0:T(1,128)S(1)} %bitcast.12), custom_call_target="tpu_custom_call" | custom-call | tf_op jit(solution)/shard_map/pallas_call | solution.py:516
  20.7 0.6 %collective-permute-start = (f32[12,128]{1,0:T(8,128)S(1)}, f32[12,128]{1,0:T(8,128)S(1)}, u32[]{:S(2)}, u32[]{:S(2)}) collective-permute-start(f32[12,128]{1,0:T(8,128)S(1)} %get-tuple-element.19.refs_1_), channel_id=1, source_target_pairs={{0,1},{1,0},{2,3},{3,2},{4,5},{5,4},{6,7},{7,6},{8,9},{9,8},{10,11... | collective-permute-start | bytes 18440 | tf_op jit(solution)/shard_map/ppermute | solution.py:482
  21.3 0.8 %collective-permute-done.refs_2_ = f32[12,128]{1,0:T(8,128)S(1)} collective-permute-done((f32[12,128]{1,0:T(8,128)S(1)}, f32[12,128]{1,0:T(8,128)S(1)}, u32[]{:S(2)}, u32[]{:S(2)}) %collective-permute-start) | collective-permute-done | bytes 6176 | tf_op jit(solution)/shard_map/ppermute | solution.py:482
  22.5 0.8 %collective-permute-done.9.refs_10_ = f32[264,128]{1,0:T(8,128)S(1)} collective-permute-done((f32[264,128]{1,0:T(8,128)S(1)}, f32[264,128]{1,0:T(8,128)S(1)}, u32[]{:S(2)}, u32[]{:S(2)}) %collective-permute-start.9) | collective-permute-done | bytes 135200 | tf_op jit(solution)/shard_map/ppermute | solution.py:482
  23.3 1.3 %collective-permute-done.8.refs_9_ = f32[264,128]{1,0:T(8,128)S(1)} collective-permute-done((f32[264,128]{1,0:T(8,128)S(1)}, f32[264,128]{1,0:T(8,128)S(1)}, u32[]{:S(2)}, u32[]{:S(2)}) %collective-permute-start.8) | collective-permute-done | bytes 135200 | tf_op jit(solution)/shard_map/ppermute | solution.py:482
  24.8 0.4 collective-permute-start.11
  25.2 0.6 %collective-permute-start.1 = (f32[4,32,128]{2,1,0:T(8,128)S(1)}, f32[4,32,128]{2,1,0:T(8,128)S(1)}, u32[]{:S(2)}, u32[]{:S(2)}) collective-permute-start(f32[4,32,128]{2,1,0:T(8,128)S(1)} %get-tuple-element.21), channel_id=1, source_target_pairs={{0,8},{8,0},{16,24},{24,16},{1,9},{9,1},{17,25},{25,17},{2,10},{10... | collective-permute-start | bytes 196616 | tf_op jit(solution)/shard_map/ppermute | solution.py:490
  25.9 3.6 %collective-permute-done.1.refs_1_ = f32[4,32,128]{2,1,0:T(8,128)S(1)} collective-permute-done((f32[4,32,128]{2,1,0:T(8,128)S(1)}, f32[4,32,128]{2,1,0:T(8,128)S(1)}, u32[]{:S(2)}, u32[]{:S(2)}) %collective-permute-start.1) | collective-permute-done | bytes 65568 | tf_op jit(solution)/shard_map/ppermute | solution.py:490
  29.5 3.4 %collective-permute-start.2 = (f32[4,32,128]{2,1,0:T(8,128)S(1)}, f32[4,32,128]{2,1,0:T(8,128)S(1)}, u32[]{:S(2)}, u32[]{:S(2)}) collective-permute-start(f32[4,32,128]{2,1,0:T(8,128)S(1)} %get-tuple-element.22), channel_id=1, source_target_pairs={{8,16},{16,8},{9,17},{17,9},{10,18},{18,10},{11,19},{19,11},{12,20... | collective-permute-start | bytes 196616 | tf_op jit(solution)/shard_map/ppermute | solution.py:490
  33.3 3.2 %collective-permute-done.2.refs_2_ = f32[4,32,128]{2,1,0:T(8,128)S(1)} collective-permute-done((f32[4,32,128]{2,1,0:T(8,128)S(1)}, f32[4,32,128]{2,1,0:T(8,128)S(1)}, u32[]{:S(2)}, u32[]{:S(2)}) %collective-permute-start.2) | collective-permute-done | bytes 65568 | tf_op jit(solution)/shard_map/ppermute | solution.py:490
  36.5 4.3 %shard_map.107 = (f32[4,24,32,128]{3,2,1,0:T(8,128)}, f32[24,8,128]{2,1,0:T(8,128)S(1)}, f32[24,128]{1,0:T(8,128)S(1)}) custom-call(f32[4,24,32,128]{3,2,1,0:T(8,128)S(1)} %get-tuple-element.20.refs_0_, f32[4,32,128]{2,1,0:T(8,128)S(1)} %collective-permute-done.1.refs_1_, f32[4,32,128]{2,1,0:T(8,128)S(1)} %collective-permute-done.2.refs_2_, ...), custom_call_target="tpu_custom_call" | custom-call | tf_op jit(solution)/shard_map/pallas_call | solution.py:516
  40.9 6.7 %shard_map.109 = (f32[24,128]{1,0:T(8,128)}, f32[4,24,32,128]{3,2,1,0:T(8,128)}) custom-call(f32[3]{0:T(128)S(1)} %copy-done.7, f32[3]{0:T(128)S(1)} %copy-done.8, s32[24,128]{1,0:T(8,128)S(1)} %get-tuple-element.18.refs_2_, s32[24,128]{1,0:T(8,128)S(1)} %shard_map.106.refs_3_, ...), custom_call_target="tpu_custom_call", output_to_operand_aliasing={{1}: (6, {})} | custom-call | tf_op jit(solution)/shard_map/pallas_call | solution.py:516
  (28 shorter events, 1.2 us)
Async XLA Ops:
  0.6 19.6 %copy-start.6 = (s32[1,1,1,1536]{3,2,1,0:T(1,128)S(1)}, s32[1,1,1,1536]{3,2,1,0:T(1,128)}, u32[]{:S(2)}) copy-start(s32[1,1,1,1536]{3,2,1,0:T(1,128)} %param.13) | copy-start | bytes 18436
  0.6 1.4 %copy-start = (f32[4,24,32,128]{3,2,1,0:T(8,128)S(1)}, f32[4,24,32,128]{3,2,1,0:T(8,128)}, u32[]{:S(2)}) copy-start(f32[4,24,32,128]{3,2,1,0:T(8,128)} %air_hbm.1) | copy-start | bytes 4718596
  2.1 0.9 %copy-start.1 = (s32[1,1,1,8,2139]{4,3,2,1,0:T(8,128)S(1)}, s32[1,1,1,8,2139]{4,3,2,1,0:T(8,128)}, u32[]{:S(2)}) copy-start(s32[1,1,1,8,2139]{4,3,2,1,0:T(8,128)} %param.11) | copy-start | bytes 205348
  2.9 0.7 %copy-start.2 = (f32[1,1,1,3072]{3,2,1,0:T(1,128)S(1)}, f32[1,1,1,3072]{3,2,1,0:T(1,128)}, u32[]{:S(2)}) copy-start(f32[1,1,1,3072]{3,2,1,0:T(1,128)} %param.17) | copy-start | bytes 36868
  3.6 0.7 %copy-start.3 = (f32[1,1,1,3072]{3,2,1,0:T(1,128)S(1)}, f32[1,1,1,3072]{3,2,1,0:T(1,128)}, u32[]{:S(2)}) copy-start(f32[1,1,1,3072]{3,2,1,0:T(1,128)} %param.18) | copy-start | bytes 36868
  4.4 0.7 %copy-start.5 = (s32[1,1,1,2139]{3,2,1,0:T(1,128)S(1)}, s32[1,1,1,2139]{3,2,1,0:T(1,128)}, u32[]{:S(2)}) copy-start(s32[1,1,1,2139]{3,2,1,0:T(1,128)} %param.12) | copy-start | bytes 25672
  5.1 27.8 %copy-start.4 = (s32[1,1,3072]{2,1,0:T(1,128)S(1)}, s32[1,1,3072]{2,1,0:T(1,128)}, u32[]{:S(2)}) copy-start(s32[1,1,3072]{2,1,0:T(1,128)} %param.14) | copy-start | bytes 36868
  5.1 35.8 %copy-start.7 = (f32[3]{0:T(128)S(1)}, f32[3]{0:T(128)}, u32[]{:S(2)}) copy-start(f32[3]{0:T(128)} %refs_0_.1) | copy-start | bytes 40
  5.1 35.8 %copy-start.8 = (f32[3]{0:T(128)S(1)}, f32[3]{0:T(128)}, u32[]{:S(2)}) copy-start(f32[3]{0:T(128)} %refs_1_.1) | copy-start | bytes 40
  7.1 9.4 %collective-permute-start.4 = (f32[96,128]{1,0:T(8,128)S(1)}, f32[96,128]{1,0:T(8,128)S(1)}, u32[]{:S(2)}, u32[]{:S(2)}) collective-permute-start(f32[96,128]{1,0:T(8,128)S(1)} %get-tuple-element.24), channel_id=1, source_target_pairs={{0,2},{2,0},{4,6},{6,4},{1,3},{3,1},{5,7},{7,5},{8,10},{10,8},{12,... | collective-permute-start | bytes 147464 | tf_op jit(solution)/shard_map/ppermute | solution.py:482
  8.7 7.7 %collective-permute-start.5 = (f32[96,128]{1,0:T(8,128)S(1)}, f32[96,128]{1,0:T(8,128)S(1)}, u32[]{:S(2)}, u32[]{:S(2)}) collective-permute-start(f32[96,128]{1,0:T(8,128)S(1)} %get-tuple-element.25), channel_id=1, source_target_pairs={{0,6},{2,4},{4,2},{6,0},{1,7},{3,5},{5,3},{7,1},{8,14},{10,12},{12... | collective-permute-start | bytes 147464 | tf_op jit(solution)/shard_map/ppermute | solution.py:482
  11.2 5.3 %collective-permute-start.6 = (f32[72,128]{1,0:T(8,128)S(1)}, f32[72,128]{1,0:T(8,128)S(1)}, u32[]{:S(2)}, u32[]{:S(2)}) collective-permute-start(f32[72,128]{1,0:T(8,128)S(1)} %get-tuple-element.29.refs_0_), channel_id=1, source_target_pairs={{0,4},{2,6},{4,0},{6,2},{1,5},{3,7},{5,1},{7,3},{8,12},{10,14},{12... | collective-permute-start | bytes 110600 | tf_op jit(solution)/shard_map/ppermute | solution.py:482
  16.7 6.7 %collective-permute-start.9 = (f32[264,128]{1,0:T(8,128)S(1)}, f32[264,128]{1,0:T(8,128)S(1)}, u32[]{:S(2)}, u32[]{:S(2)}) collective-permute-start(f32[264,128]{1,0:T(8,128)S(1)} %shard_map.108.refs_7_), channel_id=1, source_target_pairs={{0,24},{8,16},{16,8},{24,0},{1,25},{9,17},{17,9},{25,1},{2,26},{10... | collective-permute-start | bytes 405512 | tf_op jit(solution)/shard_map/ppermute | solution.py:482
  18.2 6.5 %collective-permute-start.8 = (f32[264,128]{1,0:T(8,128)S(1)}, f32[264,128]{1,0:T(8,128)S(1)}, u32[]{:S(2)}, u32[]{:S(2)}) collective-permute-start(f32[264,128]{1,0:T(8,128)S(1)} %shard_map.108.refs_7_), channel_id=1, source_target_pairs={{0,16},{8,24},{16,0},{24,8},{1,17},{9,25},{17,1},{25,9},{2,18},{10... | collective-permute-start | bytes 405512 | tf_op jit(solution)/shard_map/ppermute | solution.py:482
  18.7 6.1 %collective-permute-start.7 = (f32[264,128]{1,0:T(8,128)S(1)}, f32[264,128]{1,0:T(8,128)S(1)}, u32[]{:S(2)}, u32[]{:S(2)}) collective-permute-start(f32[264,128]{1,0:T(8,128)S(1)} %shard_map.108.refs_7_), channel_id=1, source_target_pairs={{0,8},{8,0},{16,24},{24,16},{1,9},{9,1},{17,25},{25,17},{2,10},{10... | collective-permute-start | bytes 405512 | tf_op jit(solution)/shard_map/ppermute | solution.py:482
  20.2 5.0 %collective-permute-start.3 = (f32[4,24,128]{2,1,0:T(8,128)S(1)}, f32[4,24,128]{2,1,0:T(8,128)S(1)}, u32[]{:S(2)}, u32[]{:S(2)}) collective-permute-start(f32[4,24,128]{2,1,0:T(8,128)S(1)} %get-tuple-element.23), channel_id=1, source_target_pairs={{0,1},{1,0},{2,3},{3,2},{4,5},{5,4},{6,7},{7,6},{8,9},{9,8},{10,11... | collective-permute-start | bytes 147464 | tf_op jit(solution)/shard_map/ppermute | solution.py:490
  20.7 1.4 %collective-permute-start = (f32[12,128]{1,0:T(8,128)S(1)}, f32[12,128]{1,0:T(8,128)S(1)}, u32[]{:S(2)}, u32[]{:S(2)}) collective-permute-start(f32[12,128]{1,0:T(8,128)S(1)} %get-tuple-element.19.refs_1_), channel_id=1, source_target_pairs={{0,1},{1,0},{2,3},{3,2},{4,5},{5,4},{6,7},{7,6},{8,9},{9,8},{10,11... | collective-permute-start | bytes 18440 | tf_op jit(solution)/shard_map/ppermute | solution.py:482
  22.2 18.7 %collective-permute-start.10 = (f32[264,128]{1,0:T(8,128)S(1)}, f32[264,128]{1,0:T(8,128)S(1)}, u32[]{:S(2)}, u32[]{:S(2)}) collective-permute-start(f32[264,128]{1,0:T(8,128)S(1)} %shard_map.108.refs_7_), channel_id=1, source_target_pairs={{0,1},{1,0},{2,3},{3,2},{4,5},{5,4},{6,7},{7,6},{8,9},{9,8},{10,11... | collective-permute-start | bytes 405512 | tf_op jit(solution)/shard_map/ppermute | solution.py:482
  23.3 17.5 %collective-permute-start.13 = (f32[264,128]{1,0:T(8,128)S(1)}, f32[264,128]{1,0:T(8,128)S(1)}, u32[]{:S(2)}, u32[]{:S(2)}) collective-permute-start(f32[264,128]{1,0:T(8,128)S(1)} %collective-permute-done.9.refs_10_), channel_id=1, source_target_pairs={{0,1},{1,0},{2,3},{3,2},{4,5},{5,4},{6,7},{7,6},{8,9},{9,8},{10,11... | collective-permute-start | bytes 405512 | tf_op jit(solution)/shard_map/ppermute | solution.py:482
  24.7 16.2 %collective-permute-start.12 = (f32[264,128]{1,0:T(8,128)S(1)}, f32[264,128]{1,0:T(8,128)S(1)}, u32[]{:S(2)}, u32[]{:S(2)}) collective-permute-start(f32[264,128]{1,0:T(8,128)S(1)} %collective-permute-done.8.refs_9_), channel_id=1, source_target_pairs={{0,1},{1,0},{2,3},{3,2},{4,5},{5,4},{6,7},{7,6},{8,9},{9,8},{10,11... | collective-permute-start | bytes 405512 | tf_op jit(solution)/shard_map/ppermute | solution.py:482
  24.8 16.1 %collective-permute-start.11 = (f32[264,128]{1,0:T(8,128)S(1)}, f32[264,128]{1,0:T(8,128)S(1)}, u32[]{:S(2)}, u32[]{:S(2)}) collective-permute-start(f32[264,128]{1,0:T(8,128)S(1)} %collective-permute-done.7.refs_8_), channel_id=1, source_target_pairs={{0,1},{1,0},{2,3},{3,2},{4,5},{5,4},{6,7},{7,6},{8,9},{9,8},{10,11... | collective-permute-start | bytes 405512 | tf_op jit(solution)/shard_map/ppermute | solution.py:482
  25.2 4.3 %collective-permute-start.1 = (f32[4,32,128]{2,1,0:T(8,128)S(1)}, f32[4,32,128]{2,1,0:T(8,128)S(1)}, u32[]{:S(2)}, u32[]{:S(2)}) collective-permute-start(f32[4,32,128]{2,1,0:T(8,128)S(1)} %get-tuple-element.21), channel_id=1, source_target_pairs={{0,8},{8,0},{16,24},{24,16},{1,9},{9,1},{17,25},{25,17},{2,10},{10... | collective-permute-start | bytes 196616 | tf_op jit(solution)/shard_map/ppermute | solution.py:490
  29.5 7.0 %collective-permute-start.2 = (f32[4,32,128]{2,1,0:T(8,128)S(1)}, f32[4,32,128]{2,1,0:T(8,128)S(1)}, u32[]{:S(2)}, u32[]{:S(2)}) collective-permute-start(f32[4,32,128]{2,1,0:T(8,128)S(1)} %get-tuple-element.22), channel_id=1, source_target_pairs={{8,16},{16,8},{9,17},{17,9},{10,18},{18,10},{11,19},{19,11},{12,20... | collective-permute-start | bytes 196616 | tf_op jit(solution)/shard_map/ppermute | solution.py:490

commit v3 on v2

v3 whole, which is shorter than its diff:
```python
import jax
import jax.numpy as jnp
import numpy as np
from jax import lax
from jax.experimental import pallas as pl
from jax.experimental.pallas import tpu as pltpu
from jax.sharding import PartitionSpec as P

NW = 32
NH = 24
NT = 4
ITERS = 4
LANES = 128
SUBS = 8

time_step = 0.2
viscosity = 0.75

VMEM = pl.BlockSpec(memory_space=pltpu.VMEM)
SMEM = pl.BlockSpec(memory_space=pltpu.SMEM)
ANY = pl.BlockSpec(memory_space=pl.ANY)
HBM = pl.BlockSpec(memory_space=pltpu.HBM)

EW = NW - 1
EH = NH - 1
ET = NT - 1
ELEMS = ET * EH * EW
ROWS = NT * NH * NW // LANES
FIELD_ROWS = NT * NH
BAND_ROWS = 2 * FIELD_ROWS + ET * NH


def iota(shape, dim):
    return lax.broadcasted_iota(jnp.int32, shape, dim)


def lane_pick(row, idx):
    return jnp.take_along_axis(
        jnp.broadcast_to(row, idx.shape), idx, axis=1, mode="promise_in_bounds"
    )


def look_up(load, count, place):
    outs = []
    for start in range(0, place.shape[0], SUBS):
        part = place[start : start + SUBS]
        high = part >> 7
        low = part & (LANES - 1)
        out = None
        for r in range(count):
            got = lane_pick(load(r), low)
            out = got if out is None else jnp.where(high == r, got, out)
        outs.append(out)
    return jnp.concatenate(outs, axis=0) if len(outs) > 1 else outs[0]


def spread(idx, values):
    count = idx.shape[0]
    acc = None
    group = 4
    for start in range(0, count, group):
        left, right = [], []
        for r in range(start, start + group):
            row = idx[r : r + 1]
            hot_high = iota((count, LANES), 0) == (row >> 7)
            hot_low = iota((LANES, LANES), 0) == (row & (LANES - 1))
            left.append(
                jnp.concatenate(
                    [jnp.where(hot_high, v[r : r + 1], 0.0) for v in values], axis=0
                ).astype(jnp.bfloat16)
            )
            right.append(jnp.where(hot_low, 1.0, 0.0).astype(jnp.bfloat16))
        part = lax.dot_general(
            jnp.concatenate(left, axis=1),
            jnp.concatenate(right, axis=1),
            (((1,), (1,)), ((), ())),
            preferred_element_type=jnp.float32,
        )
        acc = part if acc is None else acc + part
    return [acc[i * count : (i + 1) * count] for i in range(len(values))]


def element_keys():
    h = np.arange(NH)[:, None]
    lane = np.arange(LANES)[None, :]
    t, w = lane // NW, lane % NW
    corner = 4 * (t == NT - 1) + 2 * (h == NH - 1) + (w == NW - 1)
    column = np.minimum(t, ET - 1) * EH * EW + np.minimum(h, EH - 1) * EW + np.minimum(w, EW - 1)
    return corner, column


def stage_kernel(
    conn_hbm, material_hbm, diag_hbm, source_hbm, air_hbm,
    plain_ref, even_ref, odd_ref, nodes_ref, y_even, y_odd, z_even, z_odd, air_ref,
    conn_ref, material_ref, diag_ref, source_ref, sem,
):
    sec, fx, fy = (lax.axis_index(axis) for axis in ("sec", "fx", "fy"))
    loads = [
        pltpu.make_async_copy(a, b, sem.at[i])
        for i, (a, b) in enumerate(
            [
                (conn_hbm, conn_ref),
                (diag_hbm, diag_ref),
                (source_hbm, source_ref),
                (material_hbm, material_ref),
                (air_hbm, air_ref),
            ]
        )
    ]
    for load in loads:
        load.start()
    corner_np, column_np = element_keys()
    last = ELEMS // LANES

    def column_tile(ref, c, k):
        start = ELEMS - LANES if k == last else LANES * k
        return ref[c : c + 1, start : start + LANES]

    loads[0].wait()
    loads[3].wait()
    pieces, kinds = [], []
    for j in range(NH // SUBS):
        h = iota((SUBS, LANES), 0) + SUBS * j
        lane = iota((SUBS, LANES), 1)
        t = lane >> 5
        w = lane & (NW - 1)
        corner = (
            jnp.where(t == NT - 1, 4, 0) + jnp.where(h == NH - 1, 2, 0) + jnp.where(w == NW - 1, 1, 0)
        )
        column = (
            jnp.minimum(t, ET - 1) * (EH * EW)
            + jnp.minimum(h, EH - 1) * EW
            + jnp.minimum(w, EW - 1)
        )
        tile = column >> 7
        low = jnp.where(tile == last, column - (ELEMS - LANES), column & (LANES - 1))
        key = tile * 8 + corner
        rows = slice(SUBS * j, SUBS * (j + 1))
        wanted = sorted(set((column_np[rows] // LANES * 8 + corner_np[rows]).reshape(-1).tolist()))
        out = jnp.zeros((SUBS, LANES), jnp.int32)
        for code in wanted:
            c, k = code % 8, code // 8
            out = jnp.where(key == code, lane_pick(column_tile(conn_ref, c, k), low), out)
        pieces.append(out)
        kind = jnp.full((SUBS, LANES), -1, jnp.int32)
        for k in sorted({code // 8 for code in wanted if code % 8 == 0}):
            row = column_tile(material_ref, 0, k)
            kind = jnp.where((corner == 0) & (tile == k), lane_pick(row, low), kind)
        kinds.append(kind)
    nodes = jnp.concatenate(pieces, axis=0)
    nodes_ref[...] = nodes
    loads[1].wait()
    loads[2].wait()
    diag = look_up(lambda r: diag_ref[r : r + 1], ROWS, nodes)
    source = look_up(lambda r: source_ref[r : r + 1], ROWS, nodes)
    kind = jnp.concatenate(kinds, axis=0).astype(jnp.float32) + 1.0
    for ref in (plain_ref, even_ref, odd_ref):
        ref[0:ROWS] = diag
        ref[ROWS : 2 * ROWS] = source
        ref[2 * ROWS : 3 * ROWS] = kind

    loads[4].wait()
    fields, cells_z, cells_y, cells_x = air_ref.shape
    z_up = (sec & 1) == 0
    z_even[...] = air_ref[:, jnp.where(z_up, cells_z - 1, 0)]
    z_odd[...] = air_ref[:, jnp.where(z_up, 0, cells_z - 1)]
    y_up = (fy & 1) == 0
    x_up = (fx & 1) == 0
    lane = iota((cells_y, LANES), 1)
    lows, highs = [], []
    for f in range(fields):
        first = air_ref[f, :, 0, :]
        last = air_ref[f, :, cells_y - 1, :]
        y_even[f] = jnp.where(y_up, last, first)
        y_odd[f] = jnp.where(y_up, first, last)
        low = jnp.zeros((cells_y, LANES), jnp.float32)
        high = jnp.zeros((cells_y, LANES), jnp.float32)
        for z in range(cells_z):
            x = pltpu.roll(air_ref[f, z], z + 1, 1)
            high = jnp.where(lane == z, x, high)
            low = jnp.where(lane == z + 1, x, low)
        lows.append(low)
        highs.append(high)
    low = pltpu.roll(jnp.concatenate(lows, axis=0), LANES - 1, 1)
    high = jnp.concatenate(highs, axis=0)
    even_ref[3 * ROWS :] = jnp.where(x_up, high, low).T[:cells_z]
    odd_ref[3 * ROWS :] = jnp.where(x_up, low, high).T[:cells_z]


def band_kernel(tiles_x, wide, *refs):
    parts, (rows_ref, z_even, z_odd) = refs[:tiles_x], refs[tiles_x : tiles_x + 3]
    plain_ref, even_ref, odd_ref, both_ref, held = refs[-5:]
    both_ref[BAND_ROWS : BAND_ROWS + rows_ref.shape[0], :LANES] = rows_ref[...]
    fields, cells_y = z_even.shape[:2]
    for f in range(fields):
        span = slice(BAND_ROWS + f * cells_y, BAND_ROWS + (f + 1) * cells_y)
        even_ref[span, :LANES] = z_even[f]
        odd_ref[span, :LANES] = z_odd[f]
    fx = lax.axis_index("fx")
    for k, part in enumerate(parts):
        held[fx ^ k] = part[0 : 3 * ROWS]
    lane = iota((NH, wide), 1)
    at = 0
    for field in range(3):
        for t in range(NT if field < 2 else ET):
            total = None
            for f in range(tiles_x):
                x = held[f, field * ROWS : (field + 1) * ROWS]
                if wide > LANES:
                    x = jnp.concatenate([x, jnp.zeros((NH, wide - LANES), jnp.float32)], axis=1)
                shift = (EW * f - NW * t) % wide
                if shift:
                    x = pltpu.roll(x, shift, 1)
                x = jnp.where((lane >= EW * f) & (lane < EW * f + NW), x, 0.0)
                total = x if total is None else total + x
            for ref in (plain_ref, even_ref, odd_ref, both_ref):
                ref[at : at + NH] = total
            at += NH


def air_kernel(tiles_x, tiles_y, air_ref, *refs):
    refs = list(refs)
    y_even = refs.pop(0)
    y_odd = refs.pop(0) if tiles_y > 2 else None
    x_even = refs.pop(0)
    x_odds = [(m, refs.pop(0)) for m in odd_masks(tiles_x)]
    next_hbm, edge_ref, gain_ref, ends_ref, weight_ref, west_ref, east_ref, next_ref, sem = refs
    fx, fy = lax.axis_index("fx"), lax.axis_index("fy")
    fields, cells_z, cells_y, cells_x = air_ref.shape
    x_up = (fx & 1) == 0
    y_up = (fy & 1) == 0
    even = x_even[3 * ROWS :]
    odd = jnp.zeros_like(even)
    partner = jnp.where(x_up, fx - 1, fx + 1)
    for m, ref in x_odds:
        odd = jnp.where((fx ^ partner) == m, ref[3 * ROWS :], odd)
    pad = jnp.zeros((LANES - cells_z, LANES), jnp.float32)
    west_ref[...] = jnp.concatenate([jnp.where(x_up, odd, even), pad], axis=0).T
    east_ref[...] = jnp.concatenate([jnp.where(x_up, even, odd), pad], axis=0).T
    row = iota((cells_y, LANES), 0)
    lane = iota((cells_y, LANES), 1)
    half = 0.5 * time_step
    mix = time_step * viscosity

    def layer(z, below, above):
        u, v, w = air_ref[1, z], air_ref[2, z], air_ref[3, z]
        hu, hv, hw = half * u, half * v, half * w
        gain_ref[pl.ds(z, 1), :] = (mix + hv[0:1]) * jnp.where(fy == 0, 1.0, 0.0)
        for f in range(fields):
            x = air_ref[f, z]
            span = slice(f * cells_y, (f + 1) * cells_y)
            west = jnp.where(
                lane == 0,
                pltpu.roll(west_ref[span], (LANES - z) % LANES, 1),
                pltpu.roll(x, 1, 1),
            )
            east = jnp.where(
                lane == LANES - 1,
                pltpu.roll(east_ref[span], LANES - 1 - z, 1),
                pltpu.roll(x, LANES - 1, 1),
            )
            y_e = y_even[f, pl.ds(z, 1), :]
            y_o = y_odd[f, pl.ds(z, 1), :] if y_odd is not None else jnp.zeros_like(y_e)
            south_ghost = jnp.where(y_up, y_o, y_e)
            north_ghost = jnp.where(y_up, y_e, y_o)
            south = jnp.where(row == 0, south_ghost, pltpu.roll(x, 1, 0))
            north = jnp.where(row == cells_y - 1, north_ghost, pltpu.roll(x, cells_y - 1, 0))
            lower, upper = below(f), above(f)
            out = (
                (1.0 - 6.0 * mix) * x
                + mix * (east + west + north + south + upper + lower)
                + hu * (west - east)
                + hv * (south - north)
                + hw * (lower - upper)
            )
            next_ref[f, z] = out
            if f == 0:
                edge_ref[z] = out[:SUBS]

    def outside(f):
        return jnp.zeros((cells_y, LANES), jnp.float32)

    steps = 4
    depth = cells_z // steps
    for step in range(steps):
        start, stop = step * depth, (step + 1) * depth
        if start == 0:
            layer(0, outside, lambda f: air_ref[f, 1])

        @pl.loop(max(start, 1), min(stop, cells_z - 1))
        def _(z):
            layer(z, lambda f: air_ref[f, z - 1], lambda f: air_ref[f, z + 1])

        if stop == cells_z:
            layer(cells_z - 1, lambda f: air_ref[f, cells_z - 2], outside)
        pltpu.make_async_copy(
            next_ref.at[:, start:stop], next_hbm.at[:, start:stop], sem
        ).start()
    for i, z in enumerate((0, cells_z - 1)):
        hw = half * air_ref[3, z]
        weight_ref[i] = mix - hw if i else mix + hw
        ends_ref[i] = next_ref[:, z]
    pltpu.make_async_copy(next_ref, next_hbm, sem).wait()


def place_kernel(nodes_ref, iface_ref, place_ref, rows_ref):
    nodes = nodes_ref[...]
    at_row = iota(nodes.shape, 0).astype(jnp.float32)
    at_lane = iota(nodes.shape, 1).astype(jnp.float32)
    high, low = spread(nodes, [at_row, at_lane])
    place = high * LANES + low
    place_ref[...] = place.astype(jnp.int32)
    count = iface_ref.shape[-1] // LANES
    iface = jnp.concatenate(
        [iface_ref[0:1, LANES * r : LANES * (r + 1)] for r in range(count)], axis=0
    )
    rows_ref[...] = look_up(lambda r: place[r : r + 1], ROWS, iface)


def face_kernel(tiles_y, face_ref, *refs):
    parts, wall_ref, held = refs[:tiles_y], refs[tiles_y], refs[tiles_y + 1]
    fy = lax.axis_index("fy")
    for k, part in enumerate(parts):
        count = held.shape[1]
        rows = part[BAND_ROWS : BAND_ROWS + count, :LANES]
        held[fy ^ k] = rows + (fy ^ k).astype(jnp.float32) * (ROWS * LANES)
    rows = jnp.concatenate([held[j] for j in range(tiles_y)], axis=0)
    row = rows.astype(jnp.int32)
    high, low = spread(
        face_ref[...],
        [(row >> 7).astype(jnp.float32), (row & (LANES - 1)).astype(jnp.float32)],
    )
    wall_ref[...] = (high * LANES + low).astype(jnp.int32)


def solve_kernel(
    tiles_s, tiles_x, tiles_y, wide, material_count,
    conduct_ref, capacity_ref, place_ref, wall_ref, edge_ref, gain_ref, ends_ref, weight_ref, air_ref,
    *refs,
):
    bands = tiles_s * tiles_y
    parts = refs[:bands]
    solid_ref, next_ref = refs[bands : bands + 2]
    (held, elem, side, main, inv, res, dirn, image, sol, table, last_table, edge, solid, ends, sem) = refs[
        bands + 2 :
    ]
    sec, fx, fy = (lax.axis_index(axis) for axis in ("sec", "fx", "fy"))
    z_up = (sec & 1) == 0
    fields, cells_z, cells_y = air_ref.shape[:3]
    z_odds = [(m, parts[m]) for m in odd_masks(tiles_s)]
    across = sec ^ jnp.where(z_up, sec - 1, sec + 1)
    outer = [
        pltpu.make_async_copy(ends.at[i], next_ref.at[:, z], sem.at[2 + i])
        for i, z in enumerate((0, cells_z - 1))
    ]
    lane_tiles = [slice(i, i + LANES) for i in range(0, wide, LANES)]

    @pl.when(fy >= 0)
    def _():
        for i, copy in enumerate(outer):
            for f in range(fields):
                span = slice(BAND_ROWS + f * cells_y, BAND_ROWS + (f + 1) * cells_y)
                even = parts[1][span, :LANES]
                odd = jnp.zeros_like(even)
                for m, part in z_odds:
                    odd = jnp.where(across == m, part[span, :LANES], odd)
                here, there = (odd, even) if i == 0 else (even, odd)
                ends[i, f] = ends_ref[i, f] + weight_ref[i] * jnp.where(z_up, here, there)
            copy.start()

    @pl.when(fy >= 0)
    def _():
        for j in range(tiles_y):
            for k in range(tiles_s):
                band = (sec ^ k) * tiles_y + (fy ^ j)
                for i, cut in enumerate(lane_tiles):
                    held[i, pl.ds(band, BAND_ROWS, stride=bands), :] = parts[j * tiles_s + k][
                        0:BAND_ROWS, cut
                    ]

    def loop(start, stop, body, carry):
        if bands * wide > SUBS * LANES:
            return lax.fori_loop(start, stop, body, carry)
        for h in range(start, stop):
            carry = body(h, carry)
        return carry

    def span_of(r):
        return pl.ds(r * bands if isinstance(r, int) else pl.multiple_of(r * bands, bands), bands)

    def join(tiles):
        return tiles[0] if len(tiles) == 1 else jnp.concatenate(tiles, axis=1)

    def row_of(ref, r):
        return join([ref[i, span_of(r), :] for i in range(len(lane_tiles))])

    def put(ref, r, x):
        for i, cut in enumerate(lane_tiles):
            ref[i, span_of(r), :] = x[:, cut]

    lane = iota((bands, wide), 1)
    band = iota((bands, wide), 0)
    used = lane < EW * tiles_x + 1

    def right(x):
        return pltpu.roll(x, wide - 1, 1)

    def left(x):
        return pltpu.roll(x, 1, 1)

    def plus(*terms):
        terms = [x for x in terms if x is not None]
        total = terms[0] if terms else None
        for x in terms[1:]:
            total = total + x
        return total

    def seam(low, high):
        below = jnp.where(band > 0, pltpu.roll(high, 1, 0), 0.0)
        above = jnp.where(band < bands - 1, pltpu.roll(low, bands - 1, 0), 0.0)
        return low + below, high + above

    def total_of(parts):
        x = plus(*parts)
        return jnp.sum(jnp.sum(x, axis=0, keepdims=True), axis=1, keepdims=True)

    def first_row(ref, x, n):
        return seam(x, row_of(ref, n + NH - 1))[0]

    def last_row(ref, x, n):
        return seam(row_of(ref, n - NH + 1), x)[1]

    def once(x):
        return jnp.where(band > 0, 0.0, x)

    zero = jnp.zeros((bands, wide), jnp.float32)

    @pl.when(fy >= 0)
    def _():
        def prepare(h, before):
            now = []
            for t in range(ET):
                kind = row_of(held, 2 * FIELD_ROWS + t * NH + h)
                x = jnp.zeros_like(kind)
                s = jnp.zeros_like(kind)
                for m in range(material_count):
                    x = jnp.where(kind == m + 1.0, conduct_ref[m] * (1.0 / 12.0), x)
                    s = jnp.where(kind == m + 1.0, capacity_ref[m] * 0.125, s)
                put(elem, t * NH + h, x)
                now += [x, 5.0 * x + s]
            both = [a + b for a, b in zip(now, before)]
            for t in range(NT):
                if t < ET:
                    x = both[2 * t]
                    put(side, t * NH + h, x + left(x))
                x = plus(both[2 * t + 1] if t < ET else None, both[2 * t - 1] if t else None)
                put(main, t * NH + h, x + left(x))
            return tuple(now)

        loop(0, NH, prepare, (zero,) * (2 * ET))

    def begin(h, acc, fix=None):
        out = []
        for t in range(NT):
            n = t * NH + h
            d, r = row_of(held, n), row_of(held, FIELD_ROWS + n)
            if fix is not None:
                d, r = fix(held, d, n), fix(held, r, FIELD_ROWS + n)
            v = jnp.where(used, 1.0 / d, 0.0)
            z = r * v
            put(inv, n, v)
            put(res, n, r)
            put(dirn, n, z)
            out.append(acc[t] + (once(r * z) if fix is first_row else r * z))
        return tuple(out)

    acc = begin(0, (zero,) * NT, first_row)
    acc = begin(NH - 1, acc, last_row)
    acc = loop(1, NH - 1, begin, acc)
    gamma = total_of(acc)

    def operate(iteration, beta, step_len):
        last = iteration + 1 == ITERS

        def fetch(h):
            p, y = [], []
            for t in range(NT):
                n = t * NH + h
                x = row_of(dirn, n)
                if beta is not None:
                    put(sol, n, plus(step_len * x, row_of(sol, n) if iteration > 1 else None))
                    x = row_of(res, n) * row_of(inv, n) + beta * x
                    put(dirn, n, x)
                p.append(x)
                y.append(right(x))
            return p, y

        def finish(h, p, diag_now, cross_now, on_diag, on_cross, acc):
            out_acc = []
            for t in range(NT):
                n = t * NH + h
                out = row_of(main, n) * p[t]
                if t < ET:
                    out = out + row_of(side, n) * p[t + 1]
                if t > 0:
                    out = out + row_of(side, n - NH) * p[t - 1]
                out = out - plus(
                    diag_now[t], on_cross[t], left(plus(cross_now[t], on_diag[t]))
                )
                if not last:
                    put(image, n, out)
                out_acc.append(acc[t] + p[t] * out)
            return out_acc

        def body(h, carry):
            p, y, on_diag, on_cross, acc = (carry[i * NT : (i + 1) * NT] for i in range(5))
            p_next, y_next = fetch(h + 1)
            diag = [p[t] + y_next[t] for t in range(NT)]
            cross = [y[t] + p_next[t] for t in range(NT)]
            layer = [a + b for a, b in zip(diag, cross)]
            x = [row_of(elem, t * NH + h) for t in range(ET)]
            diag_now, cross_now = [], []
            for t in range(NT):
                upper = x[t] if t < ET else None
                lower = x[t - 1] if t > 0 else None
                both = plus(upper, lower)
                other = plus(
                    upper * layer[t + 1] if t < ET else None,
                    lower * layer[t - 1] if t > 0 else None,
                )
                diag_now.append(other + both * diag[t])
                cross_now.append(other + both * cross[t])
            acc = finish(h, p, diag_now, cross_now, on_diag, on_cross, acc)
            return (*p_next, *y_next, *diag_now, *cross_now, *acc)

        p, y = fetch(0)
        carry = loop(0, EH, body, (*p, *y) + (zero,) * (3 * NT))
        p, y, on_diag, on_cross, acc = (carry[i * NT : (i + 1) * NT] for i in range(5))
        none = [None] * NT
        acc = finish(EH, p, none, none, on_diag, on_cross, acc)
        if last:
            for j in range(tiles_y):
                table[j] = pack(sol, j)
                last_table[j] = pack(dirn, j)
        return total_of(acc)

    spot = iota((NH, LANES), 1) >> 5

    def pack(ref, j):
        packed = None
        for t in range(NT):
            start = t * NH * bands + sec * tiles_y + j
            x = join(
                [ref[i, pl.ds(start, NH, stride=bands), :] for i in range(len(lane_tiles))]
            )
            x = pltpu.roll(x, (NW * t - EW * fx + tiles_x * wide) % wide, 1)[:, :LANES]
            packed = x if packed is None else jnp.where(spot == t, x, packed)
        return packed

    beta = step_len = None
    for iteration in range(ITERS):
        step_len = gamma / operate(iteration, beta, step_len)
        if iteration + 1 == ITERS:
            break

        def update(h, acc, fix=None, step_len=step_len):
            out = []
            for t in range(NT):
                n = t * NH + h
                q = row_of(image, n)
                if fix is not None:
                    q = fix(image, q, n)
                r = row_of(res, n) - step_len * q
                put(res, n, r)
                part = r * r * row_of(inv, n)
                out.append(acc[t] + (once(part) if fix is first_row else part))
            return tuple(out)

        acc = update(0, (zero,) * NT, first_row)
        acc = update(NH - 1, acc, last_row)
        gamma_next = total_of(loop(1, NH - 1, update, acc))
        beta = gamma_next / gamma
        gamma = gamma_next

    for j in range(tiles_y):
        table[j] = table[j] + step_len * last_table[j]
    last_table[0] = table[fy]
    first = pltpu.make_async_copy(solid, solid_ref, sem.at[0])
    second = pltpu.make_async_copy(edge, next_ref.at[0, :, 0:SUBS, :], sem.at[1])

    @pl.when(fy >= 0)
    def _():
        solid[...] = look_up(lambda r: last_table[0, r : r + 1], ROWS, place_ref[...])
        first.start()

    for copy in outer:
        copy.wait()

    @pl.when(fy == 0)
    def _():
        extra = look_up(
            lambda r: table[r // ROWS, r % ROWS : r % ROWS + 1], tiles_y * ROWS, wall_ref[...]
        )
        extra = extra * gain_ref[...]
        top = iota((SUBS, LANES), 0) == 0
        for z in range(cells_z):
            base = ends[z // (cells_z - 1), 0, :SUBS] if z in (0, cells_z - 1) else edge_ref[z]
            edge[z] = base + jnp.where(top, extra[z : z + 1], 0.0)
        second.start()
        second.wait()

    first.wait()


def odd_masks(count):
    return sorted({i ^ (i + 1) for i in range(1, count - 1, 2)})


def swap(x, axis, mask):
    count = lax.axis_size(axis)
    return lax.ppermute(x, axis, [(i, i ^ mask) for i in range(count)])


def pair_swap(x, axis, odd):
    count = lax.axis_size(axis)
    pairs = []
    for i in range(odd, count - 1, 2):
        pairs += [(i, i + 1), (i + 1, i)]
    return lax.ppermute(x, axis, pairs) if pairs else jnp.zeros_like(x)


def on_device(
    conn,
    material,
    side_nodes,
    rim_nodes,
    iface_node,
    face_of_row,
    conductivity,
    capacity,
    diag_part,
    heat_source,
    air_state,
):
    f32 = jnp.float32
    tiles_s, tiles_x, tiles_y = (lax.axis_size(axis) for axis in ("sec", "fx", "fy"))
    bands = tiles_s * tiles_y
    wide = -(-(EW * tiles_x + 1) // LANES) * LANES
    fields, cells_z, cells_y, cells_x = air_state.shape

    def call(kernel, args, specs, outs, out_specs, scratch=(), **more):
        held = list(args) + list(outs) + [s for s in scratch if hasattr(s, "shape")]
        need = sum(4 * int(np.prod(x.shape)) for x in held)
        return pl.pallas_call(
            kernel,
            in_specs=specs,
            out_specs=out_specs,
            out_shape=outs,
            scratch_shapes=list(scratch),
            compiler_params=pltpu.CompilerParams(vmem_limit_bytes=need + (6 << 20)),
            **more,
        )(*args)

    def cost(microseconds):
        return pl.CostEstimate(
            flops=0, bytes_accessed=int(3.7e6 * microseconds), transcendentals=0
        )

    def shape(*dims):
        return jax.ShapeDtypeStruct(dims, f32)

    def ints(*dims):
        return jax.ShapeDtypeStruct(dims, jnp.int32)

    plain, even, odd, nodes, y_even, y_odd, z_even, z_odd, air = call(
        stage_kernel,
        [
            pltpu.with_memory_space_constraint(x, pltpu.HBM)
            for x in (
                conn.reshape(conn.shape[-2:]),
                material.reshape(1, -1),
                diag_part.reshape(ROWS, LANES),
                heat_source.reshape(ROWS, LANES),
                air_state,
            )
        ],
        [HBM] * 5,
        [
            shape(3 * ROWS, LANES),
            shape(3 * ROWS + cells_z, LANES),
            shape(3 * ROWS + cells_z, LANES),
            ints(ROWS, LANES),
            shape(fields, cells_z, cells_x),
            shape(fields, cells_z, cells_x),
            shape(fields, cells_y, cells_x),
            shape(fields, cells_y, cells_x),
            shape(*air_state.shape),
        ],
        [VMEM] * 9,
        [
            pltpu.VMEM(conn.shape[-2:], jnp.int32),
            pltpu.VMEM((1, material.shape[-1]), jnp.int32),
            pltpu.VMEM((ROWS, LANES), f32),
            pltpu.VMEM((ROWS, LANES), f32),
            pltpu.SemaphoreType.DMA((5,)),
        ],
    )
    odds = odd_masks(tiles_x)
    pays = [plain] + [
        swap(even if k == 1 else odd if k in odds else plain, "fx", k) for k in range(1, tiles_x)
    ]
    y_ghosts = [pair_swap(y_even, "fy", 0)]
    if tiles_y > 2:
        y_ghosts.append(pair_swap(y_odd, "fy", 1))

    place, rows = call(
        place_kernel,
        [nodes, iface_node.reshape(1, -1)],
        [VMEM] * 2,
        [ints(ROWS, LANES), shape(iface_node.shape[-1] // LANES, LANES)],
        [VMEM] * 2,
        cost_estimate=cost(0.6),
    )

    ghosts = list(y_ghosts)
    plain, even, odd, both = call(
        lambda *refs: band_kernel(tiles_x, wide, *refs),
        pays + [rows, z_even, z_odd] + ghosts,
        [VMEM] * (tiles_x + 3) + [ANY] * len(ghosts),
        [shape(BAND_ROWS, wide)]
        + [shape(BAND_ROWS + fields * cells_y, wide)] * 2
        + [shape(BAND_ROWS + 2 * SUBS, wide)],
        [VMEM] * 4,
        [pltpu.VMEM((tiles_x, 3 * ROWS, LANES), f32)],
        cost_estimate=cost(0.3),
    )
    z_odds = odd_masks(tiles_s)
    own_bands = [plain] + [
        swap(even if k == 1 else odd if k in z_odds else plain, "sec", k) for k in range(1, tiles_s)
    ]
    boths = [both] + [swap(both, "fy", j) for j in range(1, tiles_y)]
    wall = call(
        lambda *refs: face_kernel(tiles_y, *refs),
        [face_of_row.reshape(-1, LANES)] + boths,
        [VMEM] * (1 + tiles_y),
        [ints(cells_z, LANES)],
        [VMEM],
        [pltpu.VMEM((tiles_y,) + rows.shape, f32)],
        cost_estimate=cost(0.5),
    )[0]

    ghosts += [pays[1]] + [pays[m] for m in odds]
    air_next, edge, gain, ends, weight = call(
        lambda *refs: air_kernel(tiles_x, tiles_y, *refs),
        [air] + ghosts,
        [VMEM] * (1 + len(ghosts)),
        [
            shape(*air_state.shape),
            shape(cells_z, SUBS, LANES),
            shape(cells_z, LANES),
            shape(2, fields, cells_y, cells_x),
            shape(2, cells_y, cells_x),
        ],
        [ANY] + [VMEM] * 4,
        [pltpu.VMEM((LANES, LANES), f32)] * 2
        + [pltpu.VMEM(air_state.shape, f32), pltpu.SemaphoreType.DMA],
        cost_estimate=cost(4.0),
    )

    marks = [edge, gain, ends]
    for k in range(1, tiles_s):
        i = (k - 1) % len(marks)
        own_bands[k], marks[i] = lax.optimization_barrier((own_bands[k], marks[i]))
    edge, gain, ends = marks
    all_bands = list(own_bands)
    for j in range(1, tiles_y):
        all_bands += [boths[j]] + [swap(b, "fy", j) for b in own_bands[1:]]

    grid = (wide // LANES, NT * NH * bands, LANES)
    solid, air_next = call(
        lambda *refs: solve_kernel(
            tiles_s, tiles_x, tiles_y, wide, conductivity.shape[0], *refs
        ),
        [conductivity, capacity, place, wall, edge, gain, ends, weight, air_next]
        + all_bands,
        [SMEM] * 2 + [VMEM] * 6 + [ANY] + [VMEM] * bands,
        [shape(ROWS, LANES), shape(*air_state.shape)],
        [ANY, ANY],
        [pltpu.VMEM((wide // LANES, BAND_ROWS * bands, LANES), f32)]
        + [pltpu.VMEM(grid, f32)] * 8
        + [
            pltpu.VMEM((tiles_y, ROWS, LANES), f32),
            pltpu.VMEM((tiles_y, ROWS, LANES), f32),
            pltpu.VMEM((cells_z, SUBS, LANES), f32),
            pltpu.VMEM((ROWS, LANES), f32),
            pltpu.VMEM((2, fields, cells_y, cells_x), f32),
            pltpu.SemaphoreType.DMA((4,)),
        ],
        input_output_aliases={8: 1},
    )
    return solid.reshape(diag_part.shape), air_next


def solution(mesh):
    return jax.shard_map(
        on_device,
        mesh=mesh,
        in_specs=(
            P("sec", "fx", "fy", None, None),
            P("sec", "fx", "fy", None),
            P("sec", "fx", "fy", None, None),
            P("sec", "fx", "fy", None, None),
            P("sec", "fx", "fy", None),
            P("sec", "fx", None),
            P(),
            P(),
            P("sec", "fx", "fy", None),
            P("sec", "fx", "fy", None),
            P(None, "sec", "fy", "fx"),
        ),
        out_specs=(P("sec", "fx", "fy", None), P(None, "sec", "fy", "fx")),
        check_vma=False,
    )
```

time: 48 us -> 34.3 us (0.71)
  the two profiles are of different devices: /device:TPU:2 before, /device:TPU:0 now
where the time goes in v3:
time: 34.3 us; the launch traced here: 34.2 us
  Pallas kernels  13.2 us (38%)
  waiting for transfers between devices  10.3 us (30%)
  starting transfers between devices  9.82 us (29%)
  between operations  0.76 us (2%)
    pallas_call x6, Pallas kernels, call(): pl.pallas_call(kernel, in_specs=specs, out_specs=out_specs, out_shape=out...  13.2 us
    ppermute x10, waiting for transfers between devices, swap(): return lax.ppermute(x, axis, [(i, i ^ mask) for i in range(count)])  10.3 us
    ppermute x10, starting transfers between devices, swap(): return lax.ppermute(x, axis, [(i, i ^ mask) for i in range(count)])  9.81 us
  transfers between devices with their start and end apart: 11, of which 3 were waited for; matrix products, arithmetic and copies ran while one was open for 0% of the time, Pallas kernels for 15%

profile of v3, /device:TPU:0, one launch (start us, length us, event | category | flops | bytes accessed | tf_op | source)
XLA Modules:
  0.0 34.2 jit_solution(4374781703205027385)
XLA Ops:
  0.7 2.9 %shard_map.104 = (f32[72,128]{1,0:T(8,128)S(1)}, f32[96,128]{1,0:T(8,128)S(1)}, f32[96,128]{1,0:T(8,128)S(1)}, s32[24,128]{1,0:T(8,128)S(1)}, f32[4,24,128]{2,1,...) custom-call(s32[8,2139]{1,0:T(8,128)} %bitcast.9, ...), custom_call_target="tpu_custom_call" | custom-call | tf_op jit(solution)/shard_map/pallas_call | solution.py:654
  3.5 0.0 copy-start.2
  3.5 0.0 copy-start.3
  3.5 3.1 %collective-permute-start = (f32[96,128]{1,0:T(8,128)S(1)}, f32[96,128]{1,0:T(8,128)S(1)}, u32[]{:S(2)}, u32[]{:S(2)}) collective-permute-start(f32[96,128]{1,0:T(8,128)S(1)} %get-tuple-element.32), channel_id=1, source_target_pairs={{0,2},{2,0},{4,6},{6,4},{1,3},{3,1},{5,7},{7,5},{8,10},{10,8},{12,... | collective-permute-start | bytes 147464 | tf_op jit(solution)/shard_map/ppermute | solution.py:621
  6.6 2.5 %collective-permute-start.2 = (f32[96,128]{1,0:T(8,128)S(1)}, f32[96,128]{1,0:T(8,128)S(1)}, u32[]{:S(2)}, u32[]{:S(2)}) collective-permute-start(f32[96,128]{1,0:T(8,128)S(1)} %get-tuple-element.33), channel_id=1, source_target_pairs={{0,6},{2,4},{4,2},{6,0},{1,7},{3,5},{5,3},{7,1},{8,14},{10,12},{12... | collective-permute-start | bytes 147464 | tf_op jit(solution)/shard_map/ppermute | solution.py:621
  9.1 0.0 collective-permute-start.3
  9.1 0.1 collective-permute-start.1
  9.2 0.5 %shard_map.105 = (s32[24,128]{1,0:T(8,128)S(1)}, f32[12,128]{1,0:T(8,128)S(1)}) custom-call(s32[24,128]{1,0:T(8,128)S(1)} %get-tuple-element.29.nodes_ref, s32[1,1536]{1,0:T(1,128)S(1)} %bitcast.8), custom_call_target="tpu_custom_call" | custom-call | bytes 2220000 | tf_op jit(solution)/shard_map/pallas_call | solution.py:654
  9.7 4.9 %collective-permute-done.1.refs_2_ = f32[72,128]{1,0:T(8,128)S(1)} collective-permute-done((f32[72,128]{1,0:T(8,128)S(1)}, f32[72,128]{1,0:T(8,128)S(1)}, u32[]{:S(2)}, u32[]{:S(2)}) %collective-permute-start.1) | collective-permute-done | bytes 36896 | tf_op jit(solution)/shard_map/ppermute | solution.py:621
  14.7 0.0 collective-permute-done.refs_1_.refs_2_
  14.7 0.0 collective-permute-done.2.refs_3_
  14.7 0.2 shard_map.106
  14.9 1.6 %collective-permute-start.5 = (f32[392,128]{1,0:T(8,128)S(1)}, f32[392,128]{1,0:T(8,128)S(1)}, u32[]{:S(2)}, u32[]{:S(2)}) collective-permute-start(f32[392,128]{1,0:T(8,128)S(1)} %get-tuple-element.39), channel_id=1, source_target_pairs={{0,8},{8,0},{16,24},{24,16},{1,9},{9,1},{17,25},{25,17},{2,10},{10... | collective-permute-start | bytes 602120 | tf_op jit(solution)/shard_map/ppermute | solution.py:621
  16.5 1.5 %collective-permute-start.7 = (f32[392,128]{1,0:T(8,128)S(1)}, f32[392,128]{1,0:T(8,128)S(1)}, u32[]{:S(2)}, u32[]{:S(2)}) collective-permute-start(f32[392,128]{1,0:T(8,128)S(1)} %get-tuple-element.46), channel_id=1, source_target_pairs={{0,24},{8,16},{16,8},{24,0},{1,25},{9,17},{17,9},{25,1},{2,26},{10... | collective-permute-start | bytes 602120 | tf_op jit(solution)/shard_map/ppermute | solution.py:621
  18.0 0.5 %collective-permute-start.6 = (f32[264,128]{1,0:T(8,128)S(1)}, f32[264,128]{1,0:T(8,128)S(1)}, u32[]{:S(2)}, u32[]{:S(2)}) collective-permute-start(f32[264,128]{1,0:T(8,128)S(1)} %get-tuple-element.43.refs_9_), channel_id=1, source_target_pairs={{0,16},{8,24},{16,0},{24,8},{1,17},{9,25},{17,1},{25,9},{2,18},{10... | collective-permute-start | bytes 405512 | tf_op jit(solution)/shard_map/ppermute | solution.py:621
  18.5 4.4 %shard_map.108 = (f32[4,24,32,128]{3,2,1,0:T(8,128)}, f32[24,8,128]{2,1,0:T(8,128)S(1)}, f32[24,128]{1,0:T(8,128)S(1)}, f32[2,4,32,128]{3,2,1,0:T(8,128)S(1)}, f32[2,32,128]{2,1,0:T(8,128)S(1)}) custom-call(f32[4,24,32,128]{3,2,1,0:T(8,128)S(1)} %get-tuple-element.40.refs_0_, f32[4,24,128]{2,1,0:T(8,128)S(1)} %collective-permute-done.3.refs_7_.refs_1_, ...), custom_call_target="tpu_custom_call" | custom-call | bytes 14800000 | tf_op jit(solution)/shard_map/pallas_call | solution.py:654
  22.8 0.0 collective-permute-done.5.refs_10_
  22.9 0.1 collective-permute-start.8
  22.9 4.2 %collective-permute-done.7.refs_12_ = f32[392,128]{1,0:T(8,128)S(1)} collective-permute-done((f32[392,128]{1,0:T(8,128)S(1)}, f32[392,128]{1,0:T(8,128)S(1)}, u32[]{:S(2)}, u32[]{:S(2)}) %collective-permute-start.7) | collective-permute-done | bytes 200736 | tf_op jit(solution)/shard_map/ppermute | solution.py:621
  27.2 0.5 %collective-permute-start.4 = (f32[280,128]{1,0:T(8,128)S(1)}, f32[280,128]{1,0:T(8,128)S(1)}, u32[]{:S(2)}, u32[]{:S(2)}) collective-permute-start(f32[280,128]{1,0:T(8,128)S(1)} %get-tuple-element.38.refs_1_), channel_id=1, source_target_pairs={{0,1},{1,0},{2,3},{3,2},{4,5},{5,4},{6,7},{7,6},{8,9},{9,8},{10,11... | collective-permute-start | bytes 430088 | tf_op jit(solution)/shard_map/ppermute | solution.py:621
  27.7 0.0 collective-permute-start.9
  27.7 1.1 %collective-permute-done.4.refs_2_.refs_13_ = f32[280,128]{1,0:T(8,128)S(1)} collective-permute-done((f32[280,128]{1,0:T(8,128)S(1)}, f32[280,128]{1,0:T(8,128)S(1)}, u32[]{:S(2)}, u32[]{:S(2)}) %collective-permute-start.4) | collective-permute-done | bytes 143392 | tf_op jit(solution)/shard_map/ppermute | solution.py:621
  28.8 0.4 %shard_map.107.refs_3_ = s32[24,128]{1,0:T(8,128)S(1)} custom-call(s32[24,128]{1,0:T(8,128)S(1)} %bitcast.7, f32[280,128]{1,0:T(8,128)S(1)} %get-tuple-element.38.refs_1_, f32[280,128]{1,0:T(8,128)S(1)} %collective-permute-done.4.refs_2_.refs_13_), custom_call_target="tpu_custom_call" | custom-call | bytes 1850000 | tf_op jit(solution)/shard_map/pallas_call | solution.py:654
  29.3 4.9 %shard_map.109 = (f32[24,128]{1,0:T(8,128)}, f32[4,24,32,128]{3,2,1,0:T(8,128)}) custom-call(f32[3]{0:T(128)S(1)} %copy-done.2, f32[3]{0:T(128)S(1)} %copy-done.3, s32[24,128]{1,0:T(8,128)S(1)} %get-tuple-element.30.refs_2_, s32[24,128]{1,0:T(8,128)S(1)} %shard_map.107.refs_3_, ...), custom_call_target="tpu_custom_call", output_to_operand_aliasing={{1}: (8, {})} | custom-call | tf_op jit(solution)/shard_map/pallas_call | solution.py:654
  (12 shorter events, 0.0 us)
Async XLA Ops:
  0.6 8.6 %copy-start.1 = (s32[1,1,1,1536]{3,2,1,0:T(1,128)S(1)}, s32[1,1,1,1536]{3,2,1,0:T(1,128)}, u32[]{:S(2)}) copy-start(s32[1,1,1,1536]{3,2,1,0:T(1,128)} %param.13) | copy-start | bytes 18436
  0.6 28.2 %copy-start = (s32[1,1,3072]{2,1,0:T(1,128)S(1)}, s32[1,1,3072]{2,1,0:T(1,128)}, u32[]{:S(2)}) copy-start(s32[1,1,3072]{2,1,0:T(1,128)} %param.14) | copy-start | bytes 36868
  3.5 25.7 %copy-start.2 = (f32[3]{0:T(128)S(1)}, f32[3]{0:T(128)}, u32[]{:S(2)}) copy-start(f32[3]{0:T(128)} %refs_0_.1) | copy-start | bytes 40
  3.5 25.7 %copy-start.3 = (f32[3]{0:T(128)S(1)}, f32[3]{0:T(128)}, u32[]{:S(2)}) copy-start(f32[3]{0:T(128)} %refs_1_.1) | copy-start | bytes 40
  3.5 11.2 %collective-permute-start = (f32[96,128]{1,0:T(8,128)S(1)}, f32[96,128]{1,0:T(8,128)S(1)}, u32[]{:S(2)}, u32[]{:S(2)}) collective-permute-start(f32[96,128]{1,0:T(8,128)S(1)} %get-tuple-element.32), channel_id=1, source_target_pairs={{0,2},{2,0},{4,6},{6,4},{1,3},{3,1},{5,7},{7,5},{8,10},{10,8},{12,... | collective-permute-start | bytes 147464 | tf_op jit(solution)/shard_map/ppermute | solution.py:621
  6.6 8.1 %collective-permute-start.2 = (f32[96,128]{1,0:T(8,128)S(1)}, f32[96,128]{1,0:T(8,128)S(1)}, u32[]{:S(2)}, u32[]{:S(2)}) collective-permute-start(f32[96,128]{1,0:T(8,128)S(1)} %get-tuple-element.33), channel_id=1, source_target_pairs={{0,6},{2,4},{4,2},{6,0},{1,7},{3,5},{5,3},{7,1},{8,14},{10,12},{12... | collective-permute-start | bytes 147464 | tf_op jit(solution)/shard_map/ppermute | solution.py:621
  9.1 5.6 %collective-permute-start.3 = (f32[4,24,128]{2,1,0:T(8,128)S(1)}, f32[4,24,128]{2,1,0:T(8,128)S(1)}, u32[]{:S(2)}, u32[]{:S(2)}) collective-permute-start(f32[4,24,128]{2,1,0:T(8,128)S(1)} %get-tuple-element.37), channel_id=1, source_target_pairs={{0,1},{1,0},{2,3},{3,2},{4,5},{5,4},{6,7},{7,6},{8,9},{9,8},{10,11... | collective-permute-start | bytes 147464 | tf_op jit(solution)/shard_map/ppermute | solution.py:629
  9.1 5.6 %collective-permute-start.1 = (f32[72,128]{1,0:T(8,128)S(1)}, f32[72,128]{1,0:T(8,128)S(1)}, u32[]{:S(2)}, u32[]{:S(2)}) collective-permute-start(f32[72,128]{1,0:T(8,128)S(1)} %get-tuple-element.31.refs_0_), channel_id=1, source_target_pairs={{0,4},{2,6},{4,0},{6,2},{1,5},{3,7},{5,1},{7,3},{8,12},{10,14},{12... | collective-permute-start | bytes 110600 | tf_op jit(solution)/shard_map/ppermute | solution.py:621
  14.9 7.9 %collective-permute-start.5 = (f32[392,128]{1,0:T(8,128)S(1)}, f32[392,128]{1,0:T(8,128)S(1)}, u32[]{:S(2)}, u32[]{:S(2)}) collective-permute-start(f32[392,128]{1,0:T(8,128)S(1)} %get-tuple-element.39), channel_id=1, source_target_pairs={{0,8},{8,0},{16,24},{24,16},{1,9},{9,1},{17,25},{25,17},{2,10},{10... | collective-permute-start | bytes 602120 | tf_op jit(solution)/shard_map/ppermute | solution.py:621
  16.5 10.7 %collective-permute-start.7 = (f32[392,128]{1,0:T(8,128)S(1)}, f32[392,128]{1,0:T(8,128)S(1)}, u32[]{:S(2)}, u32[]{:S(2)}) collective-permute-start(f32[392,128]{1,0:T(8,128)S(1)} %get-tuple-element.46), channel_id=1, source_target_pairs={{0,24},{8,16},{16,8},{24,0},{1,25},{9,17},{17,9},{25,1},{2,26},{10... | collective-permute-start | bytes 602120 | tf_op jit(solution)/shard_map/ppermute | solution.py:621
  18.0 9.7 %collective-permute-start.6 = (f32[264,128]{1,0:T(8,128)S(1)}, f32[264,128]{1,0:T(8,128)S(1)}, u32[]{:S(2)}, u32[]{:S(2)}) collective-permute-start(f32[264,128]{1,0:T(8,128)S(1)} %get-tuple-element.43.refs_9_), channel_id=1, source_target_pairs={{0,16},{8,24},{16,0},{24,8},{1,17},{9,25},{17,1},{25,9},{2,18},{10... | collective-permute-start | bytes 405512 | tf_op jit(solution)/shard_map/ppermute | solution.py:621
  22.9 6.4 %collective-permute-start.8 = (f32[392,128]{1,0:T(8,128)S(1)}, f32[392,128]{1,0:T(8,128)S(1)}, u32[]{:S(2)}, u32[]{:S(2)}) collective-permute-start(f32[392,128]{1,0:T(8,128)S(1)} %collective-permute-done.5.refs_10_), channel_id=1, source_target_pairs={{0,1},{1,0},{2,3},{3,2},{4,5},{5,4},{6,7},{7,6},{8,9},{9,8},{10,11... | collective-permute-start | bytes 602120 | tf_op jit(solution)/shard_map/ppermute | solution.py:621
  27.1 2.1 %collective-permute-start.10 = (f32[392,128]{1,0:T(8,128)S(1)}, f32[392,128]{1,0:T(8,128)S(1)}, u32[]{:S(2)}, u32[]{:S(2)}) collective-permute-start(f32[392,128]{1,0:T(8,128)S(1)} %collective-permute-done.7.refs_12_), channel_id=1, source_target_pairs={{0,1},{1,0},{2,3},{3,2},{4,5},{5,4},{6,7},{7,6},{8,9},{9,8},{10,11... | collective-permute-start | bytes 602120 | tf_op jit(solution)/shard_map/ppermute | solution.py:621
  27.2 1.6 %collective-permute-start.4 = (f32[280,128]{1,0:T(8,128)S(1)}, f32[280,128]{1,0:T(8,128)S(1)}, u32[]{:S(2)}, u32[]{:S(2)}) collective-permute-start(f32[280,128]{1,0:T(8,128)S(1)} %get-tuple-element.38.refs_1_), channel_id=1, source_target_pairs={{0,1},{1,0},{2,3},{3,2},{4,5},{5,4},{6,7},{7,6},{8,9},{9,8},{10,11... | collective-permute-start | bytes 430088 | tf_op jit(solution)/shard_map/ppermute | solution.py:621
  27.7 1.5 %collective-permute-start.9 = (f32[264,128]{1,0:T(8,128)S(1)}, f32[264,128]{1,0:T(8,128)S(1)}, u32[]{:S(2)}, u32[]{:S(2)}) collective-permute-start(f32[264,128]{1,0:T(8,128)S(1)} %collective-permute-done.6.refs_11_), channel_id=1, source_target_pairs={{0,1},{1,0},{2,3},{3,2},{4,5},{5,4},{6,7},{7,6},{8,9},{9,8},{10,11... | collective-permute-start | bytes 405512 | tf_op jit(solution)/shard_map/ppermute | solution.py:621

commit v4 on v3

--- a/solution.py
+++ b/solution.py
@@ -91,10 +91,10 @@
 
 def stage_kernel(
     conn_hbm, material_hbm, diag_hbm, source_hbm, air_hbm,
-    plain_ref, even_ref, odd_ref, nodes_ref, y_even, y_odd, z_even, z_odd, air_ref,
+    even_ref, odd_ref, nodes_ref, air_ref,
     conn_ref, material_ref, diag_ref, source_ref, sem,
 ):
-    sec, fx, fy = (lax.axis_index(axis) for axis in ("sec", "fx", "fy"))
+    fx = lax.axis_index("fx")
     loads = [
         pltpu.make_async_copy(a, b, sem.at[i])
         for i, (a, b) in enumerate(
@@ -154,25 +154,17 @@
     diag = look_up(lambda r: diag_ref[r : r + 1], ROWS, nodes)
     source = look_up(lambda r: source_ref[r : r + 1], ROWS, nodes)
     kind = jnp.concatenate(kinds, axis=0).astype(jnp.float32) + 1.0
-    for ref in (plain_ref, even_ref, odd_ref):
+    for ref in (even_ref, odd_ref):
         ref[0:ROWS] = diag
         ref[ROWS : 2 * ROWS] = source
         ref[2 * ROWS : 3 * ROWS] = kind
 
     loads[4].wait()
     fields, cells_z, cells_y, cells_x = air_ref.shape
-    z_up = (sec & 1) == 0
-    z_even[...] = air_ref[:, jnp.where(z_up, cells_z - 1, 0)]
-    z_odd[...] = air_ref[:, jnp.where(z_up, 0, cells_z - 1)]
-    y_up = (fy & 1) == 0
     x_up = (fx & 1) == 0
     lane = iota((cells_y, LANES), 1)
     lows, highs = [], []
     for f in range(fields):
-        first = air_ref[f, :, 0, :]
-        last = air_ref[f, :, cells_y - 1, :]
-        y_even[f] = jnp.where(y_up, last, first)
-        y_odd[f] = jnp.where(y_up, first, last)
         low = jnp.zeros((cells_y, LANES), jnp.float32)
         high = jnp.zeros((cells_y, LANES), jnp.float32)
         for z in range(cells_z):
@@ -189,7 +181,7 @@
 
 def band_kernel(tiles_x, wide, *refs):
     parts, (rows_ref, z_even, z_odd) = refs[:tiles_x], refs[tiles_x : tiles_x + 3]
-    plain_ref, even_ref, odd_ref, both_ref, held = refs[-5:]
+    even_ref, odd_ref, both_ref, held = refs[-4:]
     both_ref[BAND_ROWS : BAND_ROWS + rows_ref.shape[0], :LANES] = rows_ref[...]
     fields, cells_y = z_even.shape[:2]
     for f in range(fields):
@@ -213,17 +205,18 @@
                     x = pltpu.roll(x, shift, 1)
                 x = jnp.where((lane >= EW * f) & (lane < EW * f + NW), x, 0.0)
                 total = x if total is None else total + x
-            for ref in (plain_ref, even_ref, odd_ref, both_ref):
+            for ref in (even_ref, odd_ref, both_ref):
                 ref[at : at + NH] = total
             at += NH
 
 
-def air_kernel(tiles_x, tiles_y, air_ref, *refs):
+def air_kernel(tiles_x, tiles_y, others, air_ref, *refs):
     refs = list(refs)
     y_even = refs.pop(0)
     y_odd = refs.pop(0) if tiles_y > 2 else None
     x_even = refs.pop(0)
     x_odds = [(m, refs.pop(0)) for m in odd_masks(tiles_x)]
+    refs = refs[others:]
     next_hbm, edge_ref, gain_ref, ends_ref, weight_ref, west_ref, east_ref, next_ref, sem = refs
     fx, fy = lax.axis_index("fx"), lax.axis_index("fy")
     fields, cells_z, cells_y, cells_x = air_ref.shape
@@ -303,7 +296,20 @@
     pltpu.make_async_copy(next_ref, next_hbm, sem).wait()
 
 
-def place_kernel(nodes_ref, iface_ref, place_ref, rows_ref):
+def place_kernel(
+    nodes_ref, iface_ref, air_ref, place_ref, rows_ref, y_even, y_odd, z_even, z_odd
+):
+    sec, fy = lax.axis_index("sec"), lax.axis_index("fy")
+    fields, cells_z, cells_y, cells_x = air_ref.shape
+    z_up = (sec & 1) == 0
+    z_even[...] = air_ref[:, jnp.where(z_up, cells_z - 1, 0)]
+    z_odd[...] = air_ref[:, jnp.where(z_up, 0, cells_z - 1)]
+    y_up = (fy & 1) == 0
+    for f in range(fields):
+        first = air_ref[f, :, 0, :]
+        last = air_ref[f, :, cells_y - 1, :]
+        y_even[f] = jnp.where(y_up, last, first)
+        y_odd[f] = jnp.where(y_up, first, last)
     nodes = nodes_ref[...]
     at_row = iota(nodes.shape, 0).astype(jnp.float32)
     at_lane = iota(nodes.shape, 1).astype(jnp.float32)
@@ -354,6 +360,22 @@
         for i, z in enumerate((0, cells_z - 1))
     ]
     lane_tiles = [slice(i, i + LANES) for i in range(0, wide, LANES)]
+    small = bands * wide <= SUBS * LANES
+
+    def take(part, band):
+        count = BAND_ROWS if small else SUBS
+
+        def body(n, carry):
+            for i, cut in enumerate(lane_tiles):
+                held[i, pl.ds(band + n * (count * bands), count, stride=bands), :] = part[
+                    pl.ds(n * count, count), cut
+                ]
+            return carry
+
+        if small:
+            body(0, 0)
+        else:
+            lax.fori_loop(0, BAND_ROWS // count, body, 0)
 
     @pl.when(fy >= 0)
     def _():
@@ -373,13 +395,10 @@
         for j in range(tiles_y):
             for k in range(tiles_s):
                 band = (sec ^ k) * tiles_y + (fy ^ j)
-                for i, cut in enumerate(lane_tiles):
-                    held[i, pl.ds(band, BAND_ROWS, stride=bands), :] = parts[j * tiles_s + k][
-                        0:BAND_ROWS, cut
-                    ]
+                take(parts[j * tiles_s + k], band)
 
     def loop(start, stop, body, carry):
-        if bands * wide > SUBS * LANES:
+        if not small:
             return lax.fori_loop(start, stop, body, carry)
         for h in range(start, stop):
             carry = body(h, carry)
@@ -672,7 +691,7 @@
     def ints(*dims):
         return jax.ShapeDtypeStruct(dims, jnp.int32)
 
-    plain, even, odd, nodes, y_even, y_odd, z_even, z_odd, air = call(
+    even, odd, nodes, air = call(
         stage_kernel,
         [
             pltpu.with_memory_space_constraint(x, pltpu.HBM)
@@ -686,17 +705,12 @@
         ],
         [HBM] * 5,
         [
-            shape(3 * ROWS, LANES),
             shape(3 * ROWS + cells_z, LANES),
             shape(3 * ROWS + cells_z, LANES),
             ints(ROWS, LANES),
-            shape(fields, cells_z, cells_x),
-            shape(fields, cells_z, cells_x),
-            shape(fields, cells_y, cells_x),
-            shape(fields, cells_y, cells_x),
             shape(*air_state.shape),
         ],
-        [VMEM] * 9,
+        [VMEM] * 4,
         [
             pltpu.VMEM(conn.shape[-2:], jnp.int32),
             pltpu.VMEM((1, material.shape[-1]), jnp.int32),
@@ -706,37 +720,38 @@
         ],
     )
     odds = odd_masks(tiles_x)
-    pays = [plain] + [
-        swap(even if k == 1 else odd if k in odds else plain, "fx", k) for k in range(1, tiles_x)
+    pays = [even] + [
+        swap(odd if k in odds else even, "fx", k) for k in range(1, tiles_x)
     ]
+    place, rows, y_even, y_odd, z_even, z_odd = call(
+        place_kernel,
+        [nodes, iface_node.reshape(1, -1), air],
+        [VMEM] * 3,
+        [ints(ROWS, LANES), shape(iface_node.shape[-1] // LANES, LANES)]
+        + [shape(fields, cells_z, cells_x)] * 2
+        + [shape(fields, cells_y, cells_x)] * 2,
+        [VMEM] * 6,
+        cost_estimate=cost(0.6),
+    )
+
     y_ghosts = [pair_swap(y_even, "fy", 0)]
     if tiles_y > 2:
         y_ghosts.append(pair_swap(y_odd, "fy", 1))
 
-    place, rows = call(
-        place_kernel,
-        [nodes, iface_node.reshape(1, -1)],
-        [VMEM] * 2,
-        [ints(ROWS, LANES), shape(iface_node.shape[-1] // LANES, LANES)],
-        [VMEM] * 2,
-        cost_estimate=cost(0.6),
-    )
-
     ghosts = list(y_ghosts)
-    plain, even, odd, both = call(
+    even, odd, both = call(
         lambda *refs: band_kernel(tiles_x, wide, *refs),
         pays + [rows, z_even, z_odd] + ghosts,
         [VMEM] * (tiles_x + 3) + [ANY] * len(ghosts),
-        [shape(BAND_ROWS, wide)]
-        + [shape(BAND_ROWS + fields * cells_y, wide)] * 2
+        [shape(BAND_ROWS + fields * cells_y, wide)] * 2
         + [shape(BAND_ROWS + 2 * SUBS, wide)],
-        [VMEM] * 4,
+        [VMEM] * 3,
         [pltpu.VMEM((tiles_x, 3 * ROWS, LANES), f32)],
         cost_estimate=cost(0.3),
     )
     z_odds = odd_masks(tiles_s)
-    own_bands = [plain] + [
-        swap(even if k == 1 else odd if k in z_odds else plain, "sec", k) for k in range(1, tiles_s)
+    own_bands = [even] + [
+        swap(odd if k in z_odds else even, "sec", k) for k in range(1, tiles_s)
     ]
     boths = [both] + [swap(both, "fy", j) for j in range(1, tiles_y)]
     wall = call(
@@ -750,10 +765,11 @@
     )[0]
 
     ghosts += [pays[1]] + [pays[m] for m in odds]
+    others = [wall] + [pays[k] for k in range(2, tiles_x) if k not in odds]
     air_next, edge, gain, ends, weight = call(
-        lambda *refs: air_kernel(tiles_x, tiles_y, *refs),
-        [air] + ghosts,
-        [VMEM] * (1 + len(ghosts)),
+        lambda *refs: air_kernel(tiles_x, tiles_y, len(others), *refs),
+        [air] + ghosts + others,
+        [VMEM] * (1 + len(ghosts)) + [ANY] * len(others),
         [
             shape(*air_state.shape),
             shape(cells_z, SUBS, LANES),

time: 34.3 us -> 31.8 us (0.927)
  waiting for transfers between devices: 10.3 us -> 7.91 us
    ppermute x10, waiting for transfers between devices: 10.3 us -> 7.91 us  [swap(): return lax.ppermute(x, axis, [(i, i ^ mask) for i in range(count)])]
  transfers between devices with their start and end apart: 11 -> 11, of which waited for: 3 -> 7; matrix products, arithmetic and copies ran while one was open for 0% -> 0% of each run, Pallas kernels for 15% -> 19%
where the time goes in v4:
time: 31.8 us; the launch traced here: 31.7 us
  Pallas kernels  13.2 us (42%)
  starting transfers between devices  9.87 us (31%)
  waiting for transfers between devices  7.91 us (25%)
  between operations  0.7 us (2%)
    pallas_call x6, Pallas kernels, call(): pl.pallas_call(kernel, in_specs=specs, out_specs=out_specs, out_shape=out...  13.2 us
    ppermute x10, starting transfers between devices, swap(): return lax.ppermute(x, axis, [(i, i ^ mask) for i in range(count)])  9.86 us
    ppermute x10, waiting for transfers between devices, swap(): return lax.ppermute(x, axis, [(i, i ^ mask) for i in range(count)])  7.91 us
  transfers between devices with their start and end apart: 11, of which 7 were waited for; matrix products, arithmetic and copies ran while one was open for 0% of the time, Pallas kernels for 19%

profile of v4, /device:TPU:0, one launch (start us, length us, event | category | flops | bytes accessed | tf_op | source)
XLA Modules:
  0.0 31.7 jit_solution(1159773584627711335)
XLA Ops:
  0.7 2.2 %shard_map.104 = (f32[96,128]{1,0:T(8,128)S(1)}, f32[96,128]{1,0:T(8,128)S(1)}, s32[24,128]{1,0:T(8,128)S(1)}, f32[4,24,32,128]{3,2,1,0:T(8,128)S(1)}) custom-call(s32[8,2139]{1,0:T(8,128)} %bitcast.9, s32[1,2139]{1,0:T(1,128)} %bitcast.12, f32[24,128]{1,0:T(8,128)} %bitcast.10, f32[24,128]{1,0:T(8,128)} %bitcast.11, f32[4,24,32,128]{3,2,1,0:T(8,128)} %air_hbm.1), custom_call_target="tpu_custom_call" | custom-call | tf_op jit(solution)/shard_map/pallas_call | solution.py:673
  2.8 4.1 %collective-permute-start.1 = (f32[96,128]{1,0:T(8,128)S(1)}, f32[96,128]{1,0:T(8,128)S(1)}, u32[]{:S(2)}, u32[]{:S(2)}) collective-permute-start(f32[96,128]{1,0:T(8,128)S(1)} %get-tuple-element.30.refs_0_), channel_id=1, source_target_pairs={{0,4},{2,6},{4,0},{6,2},{1,5},{3,7},{5,1},{7,3},{8,12},{10,14},{12... | collective-permute-start | bytes 147464 | tf_op jit(solution)/shard_map/ppermute | solution.py:640
  6.9 1.6 %collective-permute-start = (f32[96,128]{1,0:T(8,128)S(1)}, f32[96,128]{1,0:T(8,128)S(1)}, u32[]{:S(2)}, u32[]{:S(2)}) collective-permute-start(f32[96,128]{1,0:T(8,128)S(1)} %get-tuple-element.30.refs_0_), channel_id=1, source_target_pairs={{0,2},{2,0},{4,6},{6,4},{1,3},{3,1},{5,7},{7,5},{8,10},{10,8},{12,... | collective-permute-start | bytes 147464 | tf_op jit(solution)/shard_map/ppermute | solution.py:640
  8.5 0.0 collective-permute-start.2
  8.5 1.2 %shard_map.105 = (s32[24,128]{1,0:T(8,128)S(1)}, f32[12,128]{1,0:T(8,128)S(1)}, f32[4,24,128]{2,1,0:T(8,128)S(1)}, f32[4,24,128]{2,1,0:T(8,128)}, f32[4,32,128]{2,1,0:T(8,128)S(1)}, /*index=5*/f32[4,32,128]{2,1,0:T(8,128)S(1)}) custom-call(s32[24,128]{1,0:T(8,128)S(1)} %get-tuple-element.27.nodes_ref, s32[1,1536]{1,0:T(1,128)S(1)} %bitcast.8, ...), custom_call_target="tpu_custom_call" | custom-call | bytes 2220000 | tf_op jit(solution)/shard_map/pallas_call | solution.py:673
  9.7 0.0 collective-permute-start.3
  9.7 4.7 %collective-permute-done.2.refs_3_ = f32[96,128]{1,0:T(8,128)S(1)} collective-permute-done((f32[96,128]{1,0:T(8,128)S(1)}, f32[96,128]{1,0:T(8,128)S(1)}, u32[]{:S(2)}, u32[]{:S(2)}) %collective-permute-start.2) | collective-permute-done | bytes 49184 | tf_op jit(solution)/shard_map/ppermute | solution.py:640
  14.4 0.0 collective-permute-done.1.refs_2_.refs_5_
  14.4 0.0 collective-permute-done.refs_1_.refs_2_
  14.4 0.2 shard_map.106
  14.6 2.5 %collective-permute-start.7 = (f32[392,128]{1,0:T(8,128)S(1)}, f32[392,128]{1,0:T(8,128)S(1)}, u32[]{:S(2)}, u32[]{:S(2)}) collective-permute-start(f32[392,128]{1,0:T(8,128)S(1)} %get-tuple-element.42), channel_id=1, source_target_pairs={{0,24},{8,16},{16,8},{24,0},{1,25},{9,17},{17,9},{25,1},{2,26},{10... | collective-permute-start | bytes 602120 | tf_op jit(solution)/shard_map/ppermute | solution.py:640
  17.2 0.5 %collective-permute-start.6 = (f32[392,128]{1,0:T(8,128)S(1)}, f32[392,128]{1,0:T(8,128)S(1)}, u32[]{:S(2)}, u32[]{:S(2)}) collective-permute-start(f32[392,128]{1,0:T(8,128)S(1)} %get-tuple-element.37.refs_9_), channel_id=1, source_target_pairs={{0,16},{8,24},{16,0},{24,8},{1,17},{9,25},{17,1},{25,9},{2,18},{10... | collective-permute-start | bytes 602120 | tf_op jit(solution)/shard_map/ppermute | solution.py:640
  17.7 0.5 %collective-permute-start.5 = (f32[392,128]{1,0:T(8,128)S(1)}, f32[392,128]{1,0:T(8,128)S(1)}, u32[]{:S(2)}, u32[]{:S(2)}) collective-permute-start(f32[392,128]{1,0:T(8,128)S(1)} %get-tuple-element.37.refs_9_), channel_id=1, source_target_pairs={{0,8},{8,0},{16,24},{24,16},{1,9},{9,1},{17,25},{25,17},{2,10},{10... | collective-permute-start | bytes 602120 | tf_op jit(solution)/shard_map/ppermute | solution.py:640
  18.2 1.4 %collective-permute-done.4.refs_2_.refs_13_ = f32[280,128]{1,0:T(8,128)S(1)} collective-permute-done((f32[280,128]{1,0:T(8,128)S(1)}, f32[280,128]{1,0:T(8,128)S(1)}, u32[]{:S(2)}, u32[]{:S(2)}) %collective-permute-start.4) | collective-permute-done | bytes 143392 | tf_op jit(solution)/shard_map/ppermute | solution.py:640
  19.6 0.4 %shard_map.107.refs_4_.refs_3_ = s32[24,128]{1,0:T(8,128)S(1)} custom-call(s32[24,128]{1,0:T(8,128)S(1)} %bitcast.7, f32[280,128]{1,0:T(8,128)S(1)} %get-tuple-element.36.refs_1_, f32[280,128]{1,0:T(8,128)S(1)} %collective-permute-done.4.refs_2_.refs_13_), custom_call_target="tpu_custom_call" | custom-call | bytes 1850000 | tf_op jit(solution)/shard_map/pallas_call | solution.py:673
  20.0 4.3 %shard_map.108 = (f32[4,24,32,128]{3,2,1,0:T(8,128)}, f32[24,8,128]{2,1,0:T(8,128)S(1)}, f32[24,128]{1,0:T(8,128)S(1)}, f32[2,4,32,128]{3,2,1,0:T(8,128)S(1)}, f32[2,32,128]{2,1,0:T(8,128)S(1)}) custom-call(f32[4,24,32,128]{3,2,1,0:T(8,128)S(1)} %get-tuple-element.28.air_ref.refs_0_, f32[4,24,128]{2,1,0:T(8,128)S(1)} %collective-permute-done.3.refs_7_.refs_1_, ...), custom_call_target="tpu_custom_call" | custom-call | bytes 14800000 | tf_op jit(solution)/shard_map/pallas_call | solution.py:673
  24.3 0.2 collective-permute-start.10
  24.5 0.5 %collective-permute-done.6.refs_11_ = f32[392,128]{1,0:T(8,128)S(1)} collective-permute-done((f32[392,128]{1,0:T(8,128)S(1)}, f32[392,128]{1,0:T(8,128)S(1)}, u32[]{:S(2)}, u32[]{:S(2)}) %collective-permute-start.6) | collective-permute-done | bytes 200736 | tf_op jit(solution)/shard_map/ppermute | solution.py:640
  25.0 0.1 collective-permute-done.5.refs_10_
  25.1 0.4 %collective-permute-start.8 = (f32[392,128]{1,0:T(8,128)S(1)}, f32[392,128]{1,0:T(8,128)S(1)}, u32[]{:S(2)}, u32[]{:S(2)}) collective-permute-start(f32[392,128]{1,0:T(8,128)S(1)} %collective-permute-done.5.refs_10_), channel_id=1, source_target_pairs={{0,1},{1,0},{2,3},{3,2},{4,5},{5,4},{6,7},{7,6},{8,9},{9,8},{10,11... | collective-permute-start | bytes 602120 | tf_op jit(solution)/shard_map/ppermute | solution.py:640
  25.6 0.3 collective-permute-done.10.refs_16_
  25.8 0.7 %collective-permute-done.9.refs_15_ = f32[392,128]{1,0:T(8,128)S(1)} collective-permute-done((f32[392,128]{1,0:T(8,128)S(1)}, f32[392,128]{1,0:T(8,128)S(1)}, u32[]{:S(2)}, u32[]{:S(2)}) %collective-permute-start.9) | collective-permute-done | bytes 200736 | tf_op jit(solution)/shard_map/ppermute | solution.py:640
  26.5 0.3 collective-permute-done.8.refs_14_
  26.8 4.9 %shard_map.109 = (f32[24,128]{1,0:T(8,128)}, f32[4,24,32,128]{3,2,1,0:T(8,128)}) custom-call(f32[3]{0:T(128)S(1)} %copy-done.2, f32[3]{0:T(128)S(1)} %copy-done.3, s32[24,128]{1,0:T(8,128)S(1)} %get-tuple-element.29.refs_2_, s32[24,128]{1,0:T(8,128)S(1)} %shard_map.107.refs_4_.refs_3_, ...), custom_call_target="tpu_custom_call", output_to_operand_aliasing={{1}: (8, {})} | custom-call | tf_op jit(solution)/shard_map/pallas_call | solution.py:673
  (12 shorter events, 0.0 us)
Async XLA Ops:
  0.6 7.9 %copy-start.1 = (s32[1,1,1,1536]{3,2,1,0:T(1,128)S(1)}, s32[1,1,1,1536]{3,2,1,0:T(1,128)}, u32[]{:S(2)}) copy-start(s32[1,1,1,1536]{3,2,1,0:T(1,128)} %param.13) | copy-start | bytes 18436
  0.6 18.9 %copy-start = (s32[1,1,3072]{2,1,0:T(1,128)S(1)}, s32[1,1,3072]{2,1,0:T(1,128)}, u32[]{:S(2)}) copy-start(s32[1,1,3072]{2,1,0:T(1,128)} %param.14) | copy-start | bytes 36868
  2.8 11.6 %collective-permute-start.1 = (f32[96,128]{1,0:T(8,128)S(1)}, f32[96,128]{1,0:T(8,128)S(1)}, u32[]{:S(2)}, u32[]{:S(2)}) collective-permute-start(f32[96,128]{1,0:T(8,128)S(1)} %get-tuple-element.30.refs_0_), channel_id=1, source_target_pairs={{0,4},{2,6},{4,0},{6,2},{1,5},{3,7},{5,1},{7,3},{8,12},{10,14},{12... | collective-permute-start | bytes 147464 | tf_op jit(solution)/shard_map/ppermute | solution.py:640
  6.9 7.5 %collective-permute-start = (f32[96,128]{1,0:T(8,128)S(1)}, f32[96,128]{1,0:T(8,128)S(1)}, u32[]{:S(2)}, u32[]{:S(2)}) collective-permute-start(f32[96,128]{1,0:T(8,128)S(1)} %get-tuple-element.30.refs_0_), channel_id=1, source_target_pairs={{0,2},{2,0},{4,6},{6,4},{1,3},{3,1},{5,7},{7,5},{8,10},{10,8},{12,... | collective-permute-start | bytes 147464 | tf_op jit(solution)/shard_map/ppermute | solution.py:640
  8.5 5.9 %collective-permute-start.2 = (f32[96,128]{1,0:T(8,128)S(1)}, f32[96,128]{1,0:T(8,128)S(1)}, u32[]{:S(2)}, u32[]{:S(2)}) collective-permute-start(f32[96,128]{1,0:T(8,128)S(1)} %get-tuple-element.31), channel_id=1, source_target_pairs={{0,6},{2,4},{4,2},{6,0},{1,7},{3,5},{5,3},{7,1},{8,14},{10,12},{12... | collective-permute-start | bytes 147464 | tf_op jit(solution)/shard_map/ppermute | solution.py:640
  9.7 17.1 %copy-start.2 = (f32[3]{0:T(128)S(1)}, f32[3]{0:T(128)}, u32[]{:S(2)}) copy-start(f32[3]{0:T(128)} %refs_0_.1) | copy-start | bytes 40
  9.7 17.1 %copy-start.3 = (f32[3]{0:T(128)S(1)}, f32[3]{0:T(128)}, u32[]{:S(2)}) copy-start(f32[3]{0:T(128)} %refs_1_.1) | copy-start | bytes 40
  9.7 4.7 %collective-permute-start.3 = (f32[4,24,128]{2,1,0:T(8,128)S(1)}, f32[4,24,128]{2,1,0:T(8,128)S(1)}, u32[]{:S(2)}, u32[]{:S(2)}) collective-permute-start(f32[4,24,128]{2,1,0:T(8,128)S(1)} %get-tuple-element.35), channel_id=1, source_target_pairs={{0,1},{1,0},{2,3},{3,2},{4,5},{5,4},{6,7},{7,6},{8,9},{9,8},{10,11... | collective-permute-start | bytes 147464 | tf_op jit(solution)/shard_map/ppermute | solution.py:648
  14.6 9.7 %collective-permute-start.7 = (f32[392,128]{1,0:T(8,128)S(1)}, f32[392,128]{1,0:T(8,128)S(1)}, u32[]{:S(2)}, u32[]{:S(2)}) collective-permute-start(f32[392,128]{1,0:T(8,128)S(1)} %get-tuple-element.42), channel_id=1, source_target_pairs={{0,24},{8,16},{16,8},{24,0},{1,25},{9,17},{17,9},{25,1},{2,26},{10... | collective-permute-start | bytes 602120 | tf_op jit(solution)/shard_map/ppermute | solution.py:640
  17.2 7.9 %collective-permute-start.6 = (f32[392,128]{1,0:T(8,128)S(1)}, f32[392,128]{1,0:T(8,128)S(1)}, u32[]{:S(2)}, u32[]{:S(2)}) collective-permute-start(f32[392,128]{1,0:T(8,128)S(1)} %get-tuple-element.37.refs_9_), channel_id=1, source_target_pairs={{0,16},{8,24},{16,0},{24,8},{1,17},{9,25},{17,1},{25,9},{2,18},{10... | collective-permute-start | bytes 602120 | tf_op jit(solution)/shard_map/ppermute | solution.py:640
  17.7 7.5 %collective-permute-start.5 = (f32[392,128]{1,0:T(8,128)S(1)}, f32[392,128]{1,0:T(8,128)S(1)}, u32[]{:S(2)}, u32[]{:S(2)}) collective-permute-start(f32[392,128]{1,0:T(8,128)S(1)} %get-tuple-element.37.refs_9_), channel_id=1, source_target_pairs={{0,8},{8,0},{16,24},{24,16},{1,9},{9,1},{17,25},{25,17},{2,10},{10... | collective-permute-start | bytes 602120 | tf_op jit(solution)/shard_map/ppermute | solution.py:640
  18.2 1.4 %collective-permute-start.4 = (f32[280,128]{1,0:T(8,128)S(1)}, f32[280,128]{1,0:T(8,128)S(1)}, u32[]{:S(2)}, u32[]{:S(2)}) collective-permute-start(f32[280,128]{1,0:T(8,128)S(1)} %get-tuple-element.36.refs_1_), channel_id=1, source_target_pairs={{0,1},{1,0},{2,3},{3,2},{4,5},{5,4},{6,7},{7,6},{8,9},{9,8},{10,11... | collective-permute-start | bytes 430088 | tf_op jit(solution)/shard_map/ppermute | solution.py:640
  24.3 1.5 %collective-permute-start.10 = (f32[392,128]{1,0:T(8,128)S(1)}, f32[392,128]{1,0:T(8,128)S(1)}, u32[]{:S(2)}, u32[]{:S(2)}) collective-permute-start(f32[392,128]{1,0:T(8,128)S(1)} %collective-permute-done.7.refs_12_), channel_id=1, source_target_pairs={{0,1},{1,0},{2,3},{3,2},{4,5},{5,4},{6,7},{7,6},{8,9},{9,8},{10,11... | collective-permute-start | bytes 602120 | tf_op jit(solution)/shard_map/ppermute | solution.py:640
  25.0 1.4 %collective-permute-start.9 = (f32[392,128]{1,0:T(8,128)S(1)}, f32[392,128]{1,0:T(8,128)S(1)}, u32[]{:S(2)}, u32[]{:S(2)}) collective-permute-start(f32[392,128]{1,0:T(8,128)S(1)} %collective-permute-done.6.refs_11_), channel_id=1, source_target_pairs={{0,1},{1,0},{2,3},{3,2},{4,5},{5,4},{6,7},{7,6},{8,9},{9,8},{10,11... | collective-permute-start | bytes 602120 | tf_op jit(solution)/shard_map/ppermute | solution.py:640
  25.1 1.6 %collective-permute-start.8 = (f32[392,128]{1,0:T(8,128)S(1)}, f32[392,128]{1,0:T(8,128)S(1)}, u32[]{:S(2)}, u32[]{:S(2)}) collective-permute-start(f32[392,128]{1,0:T(8,128)S(1)} %collective-permute-done.5.refs_10_), channel_id=1, source_target_pairs={{0,1},{1,0},{2,3},{3,2},{4,5},{5,4},{6,7},{7,6},{8,9},{9,8},{10,11... | collective-permute-start | bytes 602120 | tf_op jit(solution)/shard_map/ppermute | solution.py:640

commit v5 on v4

--- a/solution.py
+++ b/solution.py
@@ -280,7 +280,7 @@
         if start == 0:
             layer(0, outside, lambda f: air_ref[f, 1])
 
-        @pl.loop(max(start, 1), min(stop, cells_z - 1))
+        @pl.loop(max(start, 1), min(stop, cells_z - 1), unroll=True)
         def _(z):
             layer(z, lambda f: air_ref[f, z - 1], lambda f: air_ref[f, z + 1])
 
@@ -607,11 +607,6 @@
     first = pltpu.make_async_copy(solid, solid_ref, sem.at[0])
     second = pltpu.make_async_copy(edge, next_ref.at[0, :, 0:SUBS, :], sem.at[1])
 
-    @pl.when(fy >= 0)
-    def _():
-        solid[...] = look_up(lambda r: last_table[0, r : r + 1], ROWS, place_ref[...])
-        first.start()
-
     for copy in outer:
         copy.wait()
 
@@ -626,6 +621,14 @@
             base = ends[z // (cells_z - 1), 0, :SUBS] if z in (0, cells_z - 1) else edge_ref[z]
             edge[z] = base + jnp.where(top, extra[z : z + 1], 0.0)
         second.start()
+
+    @pl.when(fy >= 0)
+    def _():
+        solid[...] = look_up(lambda r: last_table[0, r : r + 1], ROWS, place_ref[...])
+        first.start()
+
+    @pl.when(fy == 0)
+    def _():
         second.wait()
 
     first.wait()

time: 31.8 us -> 31.8 us (level)
  waiting for transfers between devices: 7.91 us -> 9.9 us
  Pallas kernels: 13.2 us -> 11.3 us
    ppermute x10, waiting for transfers between devices: 7.91 us -> 9.9 us  [swap(): return lax.ppermute(x, axis, [(i, i ^ mask) for i in range(count)])]
    pallas_call x6, Pallas kernels: 13.2 us -> 11.3 us  [call(): pl.pallas_call(kernel, in_specs=specs, out_specs=out_specs, out_shape=out...]
  transfers between devices with their start and end apart: 11 -> 11, of which waited for: 7 -> 7; matrix products, arithmetic and copies ran while one was open for 0% -> 0% of each run, Pallas kernels for 19% -> 13%
where the time goes in v5:
time: 31.8 us; the launch traced here: 31.6 us
  Pallas kernels  11.3 us (36%)
  waiting for transfers between devices  9.9 us (31%)
  starting transfers between devices  9.66 us (30%)
  between operations  0.7 us (2%)
    pallas_call x6, Pallas kernels, call(): pl.pallas_call(kernel, in_specs=specs, out_specs=out_specs, out_shape=out...  11.3 us
    ppermute x10, waiting for transfers between devices, swap(): return lax.ppermute(x, axis, [(i, i ^ mask) for i in range(count)])  9.9 us
    ppermute x10, starting transfers between devices, swap(): return lax.ppermute(x, axis, [(i, i ^ mask) for i in range(count)])  9.66 us
  transfers between devices with their start and end apart: 11, of which 7 were waited for; matrix products, arithmetic and copies ran while one was open for 0% of the time, Pallas kernels for 13%

profile of v5, /device:TPU:0, one launch (start us, length us, event | category | flops | bytes accessed | tf_op | source)
XLA Modules:
  0.0 31.6 jit_solution(10624202946361161393)
XLA Ops:
  0.7 2.2 %shard_map.104 = (f32[96,128]{1,0:T(8,128)S(1)}, f32[96,128]{1,0:T(8,128)S(1)}, s32[24,128]{1,0:T(8,128)S(1)}, f32[4,24,32,128]{3,2,1,0:T(8,128)S(1)}) custom-call(s32[8,2139]{1,0:T(8,128)} %bitcast.9, s32[1,2139]{1,0:T(1,128)} %bitcast.12, f32[24,128]{1,0:T(8,128)} %bitcast.10, f32[24,128]{1,0:T(8,128)} %bitcast.11, f32[4,24,32,128]{3,2,1,0:T(8,128)} %air_hbm.1), custom_call_target="tpu_custom_call" | custom-call | tf_op jit(solution)/shard_map/pallas_call | solution.py:676
  2.8 4.1 %collective-permute-start.1 = (f32[96,128]{1,0:T(8,128)S(1)}, f32[96,128]{1,0:T(8,128)S(1)}, u32[]{:S(2)}, u32[]{:S(2)}) collective-permute-start(f32[96,128]{1,0:T(8,128)S(1)} %get-tuple-element.30.refs_0_), channel_id=1, source_target_pairs={{0,4},{2,6},{4,0},{6,2},{1,5},{3,7},{5,1},{7,3},{8,12},{10,14},{12... | collective-permute-start | bytes 147464 | tf_op jit(solution)/shard_map/ppermute | solution.py:643
  6.9 1.6 %collective-permute-start = (f32[96,128]{1,0:T(8,128)S(1)}, f32[96,128]{1,0:T(8,128)S(1)}, u32[]{:S(2)}, u32[]{:S(2)}) collective-permute-start(f32[96,128]{1,0:T(8,128)S(1)} %get-tuple-element.30.refs_0_), channel_id=1, source_target_pairs={{0,2},{2,0},{4,6},{6,4},{1,3},{3,1},{5,7},{7,5},{8,10},{10,8},{12,... | collective-permute-start | bytes 147464 | tf_op jit(solution)/shard_map/ppermute | solution.py:643
  8.5 0.0 collective-permute-start.2
  8.5 1.2 %shard_map.105 = (s32[24,128]{1,0:T(8,128)S(1)}, f32[12,128]{1,0:T(8,128)S(1)}, f32[4,24,128]{2,1,0:T(8,128)S(1)}, f32[4,24,128]{2,1,0:T(8,128)}, f32[4,32,128]{2,1,0:T(8,128)S(1)}, /*index=5*/f32[4,32,128]{2,1,0:T(8,128)S(1)}) custom-call(s32[24,128]{1,0:T(8,128)S(1)} %get-tuple-element.27.nodes_ref, s32[1,1536]{1,0:T(1,128)S(1)} %bitcast.8, ...), custom_call_target="tpu_custom_call" | custom-call | bytes 2220000 | tf_op jit(solution)/shard_map/pallas_call | solution.py:676
  9.7 0.0 collective-permute-start.3
  9.7 4.7 %collective-permute-done.2.refs_3_ = f32[96,128]{1,0:T(8,128)S(1)} collective-permute-done((f32[96,128]{1,0:T(8,128)S(1)}, f32[96,128]{1,0:T(8,128)S(1)}, u32[]{:S(2)}, u32[]{:S(2)}) %collective-permute-start.2) | collective-permute-done | bytes 49184 | tf_op jit(solution)/shard_map/ppermute | solution.py:643
  14.4 0.0 collective-permute-done.1.refs_2_.refs_5_
  14.4 0.0 collective-permute-done.refs_1_.refs_2_
  14.4 0.2 shard_map.106
  14.6 2.5 %collective-permute-start.7 = (f32[392,128]{1,0:T(8,128)S(1)}, f32[392,128]{1,0:T(8,128)S(1)}, u32[]{:S(2)}, u32[]{:S(2)}) collective-permute-start(f32[392,128]{1,0:T(8,128)S(1)} %get-tuple-element.42), channel_id=1, source_target_pairs={{0,24},{8,16},{16,8},{24,0},{1,25},{9,17},{17,9},{25,1},{2,26},{10... | collective-permute-start | bytes 602120 | tf_op jit(solution)/shard_map/ppermute | solution.py:643
  17.2 0.5 %collective-permute-start.6 = (f32[392,128]{1,0:T(8,128)S(1)}, f32[392,128]{1,0:T(8,128)S(1)}, u32[]{:S(2)}, u32[]{:S(2)}) collective-permute-start(f32[392,128]{1,0:T(8,128)S(1)} %get-tuple-element.37.refs_9_), channel_id=1, source_target_pairs={{0,16},{8,24},{16,0},{24,8},{1,17},{9,25},{17,1},{25,9},{2,18},{10... | collective-permute-start | bytes 602120 | tf_op jit(solution)/shard_map/ppermute | solution.py:643
  17.7 0.5 %collective-permute-start.5 = (f32[392,128]{1,0:T(8,128)S(1)}, f32[392,128]{1,0:T(8,128)S(1)}, u32[]{:S(2)}, u32[]{:S(2)}) collective-permute-start(f32[392,128]{1,0:T(8,128)S(1)} %get-tuple-element.37.refs_9_), channel_id=1, source_target_pairs={{0,8},{8,0},{16,24},{24,16},{1,9},{9,1},{17,25},{25,17},{2,10},{10... | collective-permute-start | bytes 602120 | tf_op jit(solution)/shard_map/ppermute | solution.py:643
  18.2 1.4 %collective-permute-done.4.refs_2_.refs_13_ = f32[280,128]{1,0:T(8,128)S(1)} collective-permute-done((f32[280,128]{1,0:T(8,128)S(1)}, f32[280,128]{1,0:T(8,128)S(1)}, u32[]{:S(2)}, u32[]{:S(2)}) %collective-permute-start.4) | collective-permute-done | bytes 143392 | tf_op jit(solution)/shard_map/ppermute | solution.py:643
  19.6 0.4 %shard_map.107.refs_4_.refs_3_ = s32[24,128]{1,0:T(8,128)S(1)} custom-call(s32[24,128]{1,0:T(8,128)S(1)} %bitcast.7, f32[280,128]{1,0:T(8,128)S(1)} %get-tuple-element.36.refs_1_, f32[280,128]{1,0:T(8,128)S(1)} %collective-permute-done.4.refs_2_.refs_13_), custom_call_target="tpu_custom_call" | custom-call | bytes 1850000 | tf_op jit(solution)/shard_map/pallas_call | solution.py:676
  20.0 2.5 %shard_map.108 = (f32[4,24,32,128]{3,2,1,0:T(8,128)}, f32[24,8,128]{2,1,0:T(8,128)S(1)}, f32[24,128]{1,0:T(8,128)S(1)}, f32[2,4,32,128]{3,2,1,0:T(8,128)S(1)}, f32[2,32,128]{2,1,0:T(8,128)S(1)}) custom-call(f32[4,24,32,128]{3,2,1,0:T(8,128)S(1)} %get-tuple-element.28.air_ref.refs_0_, f32[4,24,128]{2,1,0:T(8,128)S(1)} %collective-permute-done.3.refs_7_.refs_1_, ...), custom_call_target="tpu_custom_call" | custom-call | bytes 14800000 | tf_op jit(solution)/shard_map/pallas_call | solution.py:676
  22.5 0.8 %collective-permute-done.7.refs_12_ = f32[392,128]{1,0:T(8,128)S(1)} collective-permute-done((f32[392,128]{1,0:T(8,128)S(1)}, f32[392,128]{1,0:T(8,128)S(1)}, u32[]{:S(2)}, u32[]{:S(2)}) %collective-permute-start.7) | collective-permute-done | bytes 200736 | tf_op jit(solution)/shard_map/ppermute | solution.py:643
  23.3 0.0 collective-permute-start.10
  23.3 1.7 %collective-permute-done.6.refs_11_ = f32[392,128]{1,0:T(8,128)S(1)} collective-permute-done((f32[392,128]{1,0:T(8,128)S(1)}, f32[392,128]{1,0:T(8,128)S(1)}, u32[]{:S(2)}, u32[]{:S(2)}) %collective-permute-start.6) | collective-permute-done | bytes 200736 | tf_op jit(solution)/shard_map/ppermute | solution.py:643
  25.0 0.1 collective-permute-done.5.refs_10_
  25.1 0.4 %collective-permute-start.8 = (f32[392,128]{1,0:T(8,128)S(1)}, f32[392,128]{1,0:T(8,128)S(1)}, u32[]{:S(2)}, u32[]{:S(2)}) collective-permute-start(f32[392,128]{1,0:T(8,128)S(1)} %collective-permute-done.5.refs_10_), channel_id=1, source_target_pairs={{0,1},{1,0},{2,3},{3,2},{4,5},{5,4},{6,7},{7,6},{8,9},{9,8},{10,11... | collective-permute-start | bytes 602120 | tf_op jit(solution)/shard_map/ppermute | solution.py:643
  25.6 0.9 %collective-permute-done.9.refs_15_ = f32[392,128]{1,0:T(8,128)S(1)} collective-permute-done((f32[392,128]{1,0:T(8,128)S(1)}, f32[392,128]{1,0:T(8,128)S(1)}, u32[]{:S(2)}, u32[]{:S(2)}) %collective-permute-start.9) | collective-permute-done | bytes 200736 | tf_op jit(solution)/shard_map/ppermute | solution.py:643
  26.5 0.3 collective-permute-done.8.refs_14_
  26.8 4.8 %shard_map.109 = (f32[24,128]{1,0:T(8,128)}, f32[4,24,32,128]{3,2,1,0:T(8,128)}) custom-call(f32[3]{0:T(128)S(1)} %copy-done.2, f32[3]{0:T(128)S(1)} %copy-done.3, s32[24,128]{1,0:T(8,128)S(1)} %get-tuple-element.29.refs_2_, s32[24,128]{1,0:T(8,128)S(1)} %shard_map.107.refs_4_.refs_3_, ...), custom_call_target="tpu_custom_call", output_to_operand_aliasing={{1}: (8, {})} | custom-call | tf_op jit(solution)/shard_map/pallas_call | solution.py:676
  (12 shorter events, 0.0 us)
Async XLA Ops:
  0.6 7.9 %copy-start.1 = (s32[1,1,1,1536]{3,2,1,0:T(1,128)S(1)}, s32[1,1,1,1536]{3,2,1,0:T(1,128)}, u32[]{:S(2)}) copy-start(s32[1,1,1,1536]{3,2,1,0:T(1,128)} %param.13) | copy-start | bytes 18436
  0.6 18.9 %copy-start = (s32[1,1,3072]{2,1,0:T(1,128)S(1)}, s32[1,1,3072]{2,1,0:T(1,128)}, u32[]{:S(2)}) copy-start(s32[1,1,3072]{2,1,0:T(1,128)} %param.14) | copy-start | bytes 36868
  2.8 11.6 %collective-permute-start.1 = (f32[96,128]{1,0:T(8,128)S(1)}, f32[96,128]{1,0:T(8,128)S(1)}, u32[]{:S(2)}, u32[]{:S(2)}) collective-permute-start(f32[96,128]{1,0:T(8,128)S(1)} %get-tuple-element.30.refs_0_), channel_id=1, source_target_pairs={{0,4},{2,6},{4,0},{6,2},{1,5},{3,7},{5,1},{7,3},{8,12},{10,14},{12... | collective-permute-start | bytes 147464 | tf_op jit(solution)/shard_map/ppermute | solution.py:643
  6.9 7.5 %collective-permute-start = (f32[96,128]{1,0:T(8,128)S(1)}, f32[96,128]{1,0:T(8,128)S(1)}, u32[]{:S(2)}, u32[]{:S(2)}) collective-permute-start(f32[96,128]{1,0:T(8,128)S(1)} %get-tuple-element.30.refs_0_), channel_id=1, source_target_pairs={{0,2},{2,0},{4,6},{6,4},{1,3},{3,1},{5,7},{7,5},{8,10},{10,8},{12,... | collective-permute-start | bytes 147464 | tf_op jit(solution)/shard_map/ppermute | solution.py:643
  8.5 5.9 %collective-permute-start.2 = (f32[96,128]{1,0:T(8,128)S(1)}, f32[96,128]{1,0:T(8,128)S(1)}, u32[]{:S(2)}, u32[]{:S(2)}) collective-permute-start(f32[96,128]{1,0:T(8,128)S(1)} %get-tuple-element.31), channel_id=1, source_target_pairs={{0,6},{2,4},{4,2},{6,0},{1,7},{3,5},{5,3},{7,1},{8,14},{10,12},{12... | collective-permute-start | bytes 147464 | tf_op jit(solution)/shard_map/ppermute | solution.py:643
  9.7 17.1 %copy-start.2 = (f32[3]{0:T(128)S(1)}, f32[3]{0:T(128)}, u32[]{:S(2)}) copy-start(f32[3]{0:T(128)} %refs_0_.1) | copy-start | bytes 40
  9.7 17.1 %copy-start.3 = (f32[3]{0:T(128)S(1)}, f32[3]{0:T(128)}, u32[]{:S(2)}) copy-start(f32[3]{0:T(128)} %refs_1_.1) | copy-start | bytes 40
  9.7 4.7 %collective-permute-start.3 = (f32[4,24,128]{2,1,0:T(8,128)S(1)}, f32[4,24,128]{2,1,0:T(8,128)S(1)}, u32[]{:S(2)}, u32[]{:S(2)}) collective-permute-start(f32[4,24,128]{2,1,0:T(8,128)S(1)} %get-tuple-element.35), channel_id=1, source_target_pairs={{0,1},{1,0},{2,3},{3,2},{4,5},{5,4},{6,7},{7,6},{8,9},{9,8},{10,11... | collective-permute-start | bytes 147464 | tf_op jit(solution)/shard_map/ppermute | solution.py:651
  14.6 8.6 %collective-permute-start.7 = (f32[392,128]{1,0:T(8,128)S(1)}, f32[392,128]{1,0:T(8,128)S(1)}, u32[]{:S(2)}, u32[]{:S(2)}) collective-permute-start(f32[392,128]{1,0:T(8,128)S(1)} %get-tuple-element.42), channel_id=1, source_target_pairs={{0,24},{8,16},{16,8},{24,0},{1,25},{9,17},{17,9},{25,1},{2,26},{10... | collective-permute-start | bytes 602120 | tf_op jit(solution)/shard_map/ppermute | solution.py:643
  17.2 7.9 %collective-permute-start.6 = (f32[392,128]{1,0:T(8,128)S(1)}, f32[392,128]{1,0:T(8,128)S(1)}, u32[]{:S(2)}, u32[]{:S(2)}) collective-permute-start(f32[392,128]{1,0:T(8,128)S(1)} %get-tuple-element.37.refs_9_), channel_id=1, source_target_pairs={{0,16},{8,24},{16,0},{24,8},{1,17},{9,25},{17,1},{25,9},{2,18},{10... | collective-permute-start | bytes 602120 | tf_op jit(solution)/shard_map/ppermute | solution.py:643
  17.7 7.5 %collective-permute-start.5 = (f32[392,128]{1,0:T(8,128)S(1)}, f32[392,128]{1,0:T(8,128)S(1)}, u32[]{:S(2)}, u32[]{:S(2)}) collective-permute-start(f32[392,128]{1,0:T(8,128)S(1)} %get-tuple-element.37.refs_9_), channel_id=1, source_target_pairs={{0,8},{8,0},{16,24},{24,16},{1,9},{9,1},{17,25},{25,17},{2,10},{10... | collective-permute-start | bytes 602120 | tf_op jit(solution)/shard_map/ppermute | solution.py:643
  18.2 1.4 %collective-permute-start.4 = (f32[280,128]{1,0:T(8,128)S(1)}, f32[280,128]{1,0:T(8,128)S(1)}, u32[]{:S(2)}, u32[]{:S(2)}) collective-permute-start(f32[280,128]{1,0:T(8,128)S(1)} %get-tuple-element.36.refs_1_), channel_id=1, source_target_pairs={{0,1},{1,0},{2,3},{3,2},{4,5},{5,4},{6,7},{7,6},{8,9},{9,8},{10,11... | collective-permute-start | bytes 430088 | tf_op jit(solution)/shard_map/ppermute | solution.py:643
  23.3 2.3 %collective-permute-start.10 = (f32[392,128]{1,0:T(8,128)S(1)}, f32[392,128]{1,0:T(8,128)S(1)}, u32[]{:S(2)}, u32[]{:S(2)}) collective-permute-start(f32[392,128]{1,0:T(8,128)S(1)} %collective-permute-done.7.refs_12_), channel_id=1, source_target_pairs={{0,1},{1,0},{2,3},{3,2},{4,5},{5,4},{6,7},{7,6},{8,9},{9,8},{10,11... | collective-permute-start | bytes 602120 | tf_op jit(solution)/shard_map/ppermute | solution.py:643
  25.0 1.4 %collective-permute-start.9 = (f32[392,128]{1,0:T(8,128)S(1)}, f32[392,128]{1,0:T(8,128)S(1)}, u32[]{:S(2)}, u32[]{:S(2)}) collective-permute-start(f32[392,128]{1,0:T(8,128)S(1)} %collective-permute-done.6.refs_11_), channel_id=1, source_target_pairs={{0,1},{1,0},{2,3},{3,2},{4,5},{5,4},{6,7},{7,6},{8,9},{9,8},{10,11... | collective-permute-start | bytes 602120 | tf_op jit(solution)/shard_map/ppermute | solution.py:643
  25.1 1.6 %collective-permute-start.8 = (f32[392,128]{1,0:T(8,128)S(1)}, f32[392,128]{1,0:T(8,128)S(1)}, u32[]{:S(2)}, u32[]{:S(2)}) collective-permute-start(f32[392,128]{1,0:T(8,128)S(1)} %collective-permute-done.5.refs_10_), channel_id=1, source_target_pairs={{0,1},{1,0},{2,3},{3,2},{4,5},{5,4},{6,7},{7,6},{8,9},{9,8},{10,11... | collective-permute-start | bytes 602120 | tf_op jit(solution)/shard_map/ppermute | solution.py:643

commit v6 on v5

--- a/solution.py
+++ b/solution.py
@@ -180,9 +180,8 @@
 
 
 def band_kernel(tiles_x, wide, *refs):
-    parts, (rows_ref, z_even, z_odd) = refs[:tiles_x], refs[tiles_x : tiles_x + 3]
-    even_ref, odd_ref, both_ref, held = refs[-4:]
-    both_ref[BAND_ROWS : BAND_ROWS + rows_ref.shape[0], :LANES] = rows_ref[...]
+    parts, (z_even, z_odd) = refs[:tiles_x], refs[tiles_x : tiles_x + 2]
+    even_ref, odd_ref, held = refs[-3:]
     fields, cells_y = z_even.shape[:2]
     for f in range(fields):
         span = slice(BAND_ROWS + f * cells_y, BAND_ROWS + (f + 1) * cells_y)
@@ -205,7 +204,7 @@
                     x = pltpu.roll(x, shift, 1)
                 x = jnp.where((lane >= EW * f) & (lane < EW * f + NW), x, 0.0)
                 total = x if total is None else total + x
-            for ref in (even_ref, odd_ref, both_ref):
+            for ref in (even_ref, odd_ref):
                 ref[at : at + NH] = total
             at += NH
 
@@ -327,9 +326,7 @@
     parts, wall_ref, held = refs[:tiles_y], refs[tiles_y], refs[tiles_y + 1]
     fy = lax.axis_index("fy")
     for k, part in enumerate(parts):
-        count = held.shape[1]
-        rows = part[BAND_ROWS : BAND_ROWS + count, :LANES]
-        held[fy ^ k] = rows + (fy ^ k).astype(jnp.float32) * (ROWS * LANES)
+        held[fy ^ k] = part[...] + (fy ^ k).astype(jnp.float32) * (ROWS * LANES)
     rows = jnp.concatenate([held[j] for j in range(tiles_y)], axis=0)
     row = rows.astype(jnp.int32)
     high, low = spread(
@@ -741,14 +738,22 @@
     if tiles_y > 2:
         y_ghosts.append(pair_swap(y_odd, "fy", 1))
 
+    wall = call(
+        lambda *refs: face_kernel(tiles_y, *refs),
+        [face_of_row.reshape(-1, LANES), rows] + [swap(rows, "fy", j) for j in range(1, tiles_y)],
+        [VMEM] * (1 + tiles_y),
+        [ints(cells_z, LANES)],
+        [VMEM],
+        [pltpu.VMEM((tiles_y,) + rows.shape, f32)],
+        cost_estimate=cost(0.5),
+    )[0]
     ghosts = list(y_ghosts)
-    even, odd, both = call(
+    even, odd = call(
         lambda *refs: band_kernel(tiles_x, wide, *refs),
-        pays + [rows, z_even, z_odd] + ghosts,
-        [VMEM] * (tiles_x + 3) + [ANY] * len(ghosts),
-        [shape(BAND_ROWS + fields * cells_y, wide)] * 2
-        + [shape(BAND_ROWS + 2 * SUBS, wide)],
-        [VMEM] * 3,
+        pays + [z_even, z_odd, wall] + ghosts,
+        [VMEM] * (tiles_x + 2) + [ANY] * (1 + len(ghosts)),
+        [shape(BAND_ROWS + fields * cells_y, wide)] * 2,
+        [VMEM] * 2,
         [pltpu.VMEM((tiles_x, 3 * ROWS, LANES), f32)],
         cost_estimate=cost(0.3),
     )
@@ -756,19 +761,8 @@
     own_bands = [even] + [
         swap(odd if k in z_odds else even, "sec", k) for k in range(1, tiles_s)
     ]
-    boths = [both] + [swap(both, "fy", j) for j in range(1, tiles_y)]
-    wall = call(
-        lambda *refs: face_kernel(tiles_y, *refs),
-        [face_of_row.reshape(-1, LANES)] + boths,
-        [VMEM] * (1 + tiles_y),
-        [ints(cells_z, LANES)],
-        [VMEM],
-        [pltpu.VMEM((tiles_y,) + rows.shape, f32)],
-        cost_estimate=cost(0.5),
-    )[0]
-
     ghosts += [pays[1]] + [pays[m] for m in odds]
-    others = [wall] + [pays[k] for k in range(2, tiles_x) if k not in odds]
+    others = [pays[k] for k in range(2, tiles_x) if k not in odds]
     air_next, edge, gain, ends, weight = call(
         lambda *refs: air_kernel(tiles_x, tiles_y, len(others), *refs),
         [air] + ghosts + others,
@@ -793,7 +787,7 @@
     edge, gain, ends = marks
     all_bands = list(own_bands)
     for j in range(1, tiles_y):
-        all_bands += [boths[j]] + [swap(b, "fy", j) for b in own_bands[1:]]
+        all_bands += [swap(b, "fy", j) for b in own_bands]
 
     grid = (wide // LANES, NT * NH * bands, LANES)
     solid, air_next = call(

time: 31.8 us -> 31.8 us (level)
  waiting for transfers between devices: 9.9 us -> 9.36 us
  starting transfers between devices: 9.66 us -> 10.2 us
    ppermute x10 -> x11, waiting for transfers between devices: 9.9 us -> 9.36 us  [swap(): return lax.ppermute(x, axis, [(i, i ^ mask) for i in range(count)])]
    ppermute x10 -> x11, starting transfers between devices: 9.66 us -> 10.2 us  [swap(): return lax.ppermute(x, axis, [(i, i ^ mask) for i in range(count)])]
  transfers between devices with their start and end apart: 11 -> 12, of which waited for: 7 -> 7; matrix products, arithmetic and copies ran while one was open for 0% -> 0% of each run, Pallas kernels for 13% -> 13%
where the time goes in v6:
time: 31.8 us; the launch traced here: 31.6 us
  Pallas kernels  11.4 us (36%)
  starting transfers between devices  10.2 us (32%)
  waiting for transfers between devices  9.36 us (29%)
  between operations  0.7 us (2%)
    pallas_call x6, Pallas kernels, call(): pl.pallas_call(kernel, in_specs=specs, out_specs=out_specs, out_shape=out...  11.4 us
    ppermute x11, starting transfers between devices, swap(): return lax.ppermute(x, axis, [(i, i ^ mask) for i in range(count)])  10.2 us
    ppermute x11, waiting for transfers between devices, swap(): return lax.ppermute(x, axis, [(i, i ^ mask) for i in range(count)])  9.36 us
  transfers between devices with their start and end apart: 12, of which 7 were waited for; matrix products, arithmetic and copies ran while one was open for 0% of the time, Pallas kernels for 13%

profile of v6, /device:TPU:0, one launch (start us, length us, event | category | flops | bytes accessed | tf_op | source)
XLA Modules:
  0.0 31.6 jit_solution(10346767757938293898)
XLA Ops:
  0.7 2.2 %shard_map.104 = (f32[96,128]{1,0:T(8,128)S(1)}, f32[96,128]{1,0:T(8,128)S(1)}, s32[24,128]{1,0:T(8,128)S(1)}, f32[4,24,32,128]{3,2,1,0:T(8,128)S(1)}) custom-call(s32[8,2139]{1,0:T(8,128)} %bitcast.9, s32[1,2139]{1,0:T(1,128)} %bitcast.12, f32[24,128]{1,0:T(8,128)} %bitcast.10, f32[24,128]{1,0:T(8,128)} %bitcast.11, f32[4,24,32,128]{3,2,1,0:T(8,128)} %air_hbm.1), custom_call_target="tpu_custom_call" | custom-call | tf_op jit(solution)/shard_map/pallas_call | solution.py:673
  2.8 4.1 %collective-permute-start.2 = (f32[96,128]{1,0:T(8,128)S(1)}, f32[96,128]{1,0:T(8,128)S(1)}, u32[]{:S(2)}, u32[]{:S(2)}) collective-permute-start(f32[96,128]{1,0:T(8,128)S(1)} %get-tuple-element.30.refs_0_), channel_id=1, source_target_pairs={{0,4},{2,6},{4,0},{6,2},{1,5},{3,7},{5,1},{7,3},{8,12},{10,14},{12... | collective-permute-start | bytes 147464 | tf_op jit(solution)/shard_map/ppermute | solution.py:640
  7.0 1.6 %collective-permute-start.1 = (f32[96,128]{1,0:T(8,128)S(1)}, f32[96,128]{1,0:T(8,128)S(1)}, u32[]{:S(2)}, u32[]{:S(2)}) collective-permute-start(f32[96,128]{1,0:T(8,128)S(1)} %get-tuple-element.30.refs_0_), channel_id=1, source_target_pairs={{0,2},{2,0},{4,6},{6,4},{1,3},{3,1},{5,7},{7,5},{8,10},{10,8},{12,... | collective-permute-start | bytes 147464 | tf_op jit(solution)/shard_map/ppermute | solution.py:640
  8.5 0.0 collective-permute-start.3
  8.5 1.2 %shard_map.105 = (s32[24,128]{1,0:T(8,128)S(1)}, f32[12,128]{1,0:T(8,128)S(1)}, f32[4,24,128]{2,1,0:T(8,128)S(1)}, f32[4,24,128]{2,1,0:T(8,128)}, f32[4,32,128]{2,1,0:T(8,128)S(1)}, /*index=5*/f32[4,32,128]{2,1,0:T(8,128)S(1)}) custom-call(s32[24,128]{1,0:T(8,128)S(1)} %get-tuple-element.26.nodes_ref, s32[1,1536]{1,0:T(1,128)S(1)} %bitcast.8, ...), custom_call_target="tpu_custom_call" | custom-call | bytes 2220000 | tf_op jit(solution)/shard_map/pallas_call | solution.py:673
  9.7 0.0 collective-permute-start.4
  9.7 0.5 %collective-permute-start = (f32[12,128]{1,0:T(8,128)S(1)}, f32[12,128]{1,0:T(8,128)S(1)}, u32[]{:S(2)}, u32[]{:S(2)}) collective-permute-start(f32[12,128]{1,0:T(8,128)S(1)} %get-tuple-element.29.refs_1_), channel_id=1, source_target_pairs={{0,1},{1,0},{2,3},{3,2},{4,5},{5,4},{6,7},{7,6},{8,9},{9,8},{10,11... | collective-permute-start | bytes 18440 | tf_op jit(solution)/shard_map/ppermute | solution.py:640
  10.2 0.8 %collective-permute-done.refs_2_ = f32[12,128]{1,0:T(8,128)S(1)} collective-permute-done((f32[12,128]{1,0:T(8,128)S(1)}, f32[12,128]{1,0:T(8,128)S(1)}, u32[]{:S(2)}, u32[]{:S(2)}) %collective-permute-start) | collective-permute-done | bytes 6176 | tf_op jit(solution)/shard_map/ppermute | solution.py:640
  11.1 0.4 %shard_map.106.refs_6_.refs_3_ = s32[24,128]{1,0:T(8,128)S(1)} custom-call(s32[24,128]{1,0:T(8,128)S(1)} %bitcast.7, f32[12,128]{1,0:T(8,128)S(1)} %get-tuple-element.29.refs_1_, f32[12,128]{1,0:T(8,128)S(1)} %collective-permute-done.refs_2_), custom_call_target="tpu_custom_call" | custom-call | bytes 1850000 | tf_op jit(solution)/shard_map/pallas_call | solution.py:673
  11.5 3.0 %collective-permute-done.3.refs_3_ = f32[96,128]{1,0:T(8,128)S(1)} collective-permute-done((f32[96,128]{1,0:T(8,128)S(1)}, f32[96,128]{1,0:T(8,128)S(1)}, u32[]{:S(2)}, u32[]{:S(2)}) %collective-permute-start.3) | collective-permute-done | bytes 49184 | tf_op jit(solution)/shard_map/ppermute | solution.py:640
  14.4 0.0 collective-permute-done.2.refs_2_.refs_4_
  14.4 0.0 collective-permute-done.1.refs_1_.refs_2_
  14.4 0.2 shard_map.107
  14.7 2.5 %collective-permute-start.7 = (f32[392,128]{1,0:T(8,128)S(1)}, f32[392,128]{1,0:T(8,128)S(1)}, u32[]{:S(2)}, u32[]{:S(2)}) collective-permute-start(f32[392,128]{1,0:T(8,128)S(1)} %get-tuple-element.40), channel_id=1, source_target_pairs={{0,24},{8,16},{16,8},{24,0},{1,25},{9,17},{17,9},{25,1},{2,26},{10... | collective-permute-start | bytes 602120 | tf_op jit(solution)/shard_map/ppermute | solution.py:640
  17.2 0.5 %collective-permute-start.6 = (f32[392,128]{1,0:T(8,128)S(1)}, f32[392,128]{1,0:T(8,128)S(1)}, u32[]{:S(2)}, u32[]{:S(2)}) collective-permute-start(f32[392,128]{1,0:T(8,128)S(1)} %get-tuple-element.35.refs_9_), channel_id=1, source_target_pairs={{0,16},{8,24},{16,0},{24,8},{1,17},{9,25},{17,1},{25,9},{2,18},{10... | collective-permute-start | bytes 602120 | tf_op jit(solution)/shard_map/ppermute | solution.py:640
  17.7 0.5 %collective-permute-start.5 = (f32[392,128]{1,0:T(8,128)S(1)}, f32[392,128]{1,0:T(8,128)S(1)}, u32[]{:S(2)}, u32[]{:S(2)}) collective-permute-start(f32[392,128]{1,0:T(8,128)S(1)} %get-tuple-element.35.refs_9_), channel_id=1, source_target_pairs={{0,8},{8,0},{16,24},{24,16},{1,9},{9,1},{17,25},{25,17},{2,10},{10... | collective-permute-start | bytes 602120 | tf_op jit(solution)/shard_map/ppermute | solution.py:640
  18.2 2.6 %shard_map.108 = (f32[4,24,32,128]{3,2,1,0:T(8,128)}, f32[24,8,128]{2,1,0:T(8,128)S(1)}, f32[24,128]{1,0:T(8,128)S(1)}, f32[2,4,32,128]{3,2,1,0:T(8,128)S(1)}, f32[2,32,128]{2,1,0:T(8,128)S(1)}) custom-call(f32[4,24,32,128]{3,2,1,0:T(8,128)S(1)} %get-tuple-element.27.air_ref.refs_0_, f32[4,24,128]{2,1,0:T(8,128)S(1)} %collective-permute-done.4.refs_7_.refs_1_, ...), custom_call_target="tpu_custom_call" | custom-call | bytes 14800000 | tf_op jit(solution)/shard_map/pallas_call | solution.py:673
  20.8 2.5 %collective-permute-done.7.refs_12_ = f32[392,128]{1,0:T(8,128)S(1)} collective-permute-done((f32[392,128]{1,0:T(8,128)S(1)}, f32[392,128]{1,0:T(8,128)S(1)}, u32[]{:S(2)}, u32[]{:S(2)}) %collective-permute-start.7) | collective-permute-done | bytes 200736 | tf_op jit(solution)/shard_map/ppermute | solution.py:640
  23.3 1.7 %collective-permute-done.6.refs_11_ = f32[392,128]{1,0:T(8,128)S(1)} collective-permute-done((f32[392,128]{1,0:T(8,128)S(1)}, f32[392,128]{1,0:T(8,128)S(1)}, u32[]{:S(2)}, u32[]{:S(2)}) %collective-permute-start.6) | collective-permute-done | bytes 200736 | tf_op jit(solution)/shard_map/ppermute | solution.py:640
  25.1 0.1 collective-permute-done.5.refs_10_
  25.1 0.4 %collective-permute-start.9 = (f32[392,128]{1,0:T(8,128)S(1)}, f32[392,128]{1,0:T(8,128)S(1)}, u32[]{:S(2)}, u32[]{:S(2)}) collective-permute-start(f32[392,128]{1,0:T(8,128)S(1)} %collective-permute-done.5.refs_10_), channel_id=1, source_target_pairs={{0,1},{1,0},{2,3},{3,2},{4,5},{5,4},{6,7},{7,6},{8,9},{9,8},{10,11... | collective-permute-start | bytes 602120 | tf_op jit(solution)/shard_map/ppermute | solution.py:640
  25.6 0.9 %collective-permute-done.10.refs_15_ = f32[392,128]{1,0:T(8,128)S(1)} collective-permute-done((f32[392,128]{1,0:T(8,128)S(1)}, f32[392,128]{1,0:T(8,128)S(1)}, u32[]{:S(2)}, u32[]{:S(2)}) %collective-permute-start.10) | collective-permute-done | bytes 200736 | tf_op jit(solution)/shard_map/ppermute | solution.py:640
  26.5 0.3 collective-permute-done.9.refs_14_
  26.8 4.8 %shard_map.109 = (f32[24,128]{1,0:T(8,128)}, f32[4,24,32,128]{3,2,1,0:T(8,128)}) custom-call(f32[3]{0:T(128)S(1)} %copy-done.2, f32[3]{0:T(128)S(1)} %copy-done.3, s32[24,128]{1,0:T(8,128)S(1)} %get-tuple-element.28.refs_2_, s32[24,128]{1,0:T(8,128)S(1)} %shard_map.106.refs_6_.refs_3_, ...), custom_call_target="tpu_custom_call", output_to_operand_aliasing={{1}: (8, {})} | custom-call | tf_op jit(solution)/shard_map/pallas_call | solution.py:673
  (14 shorter events, 0.0 us)
Async XLA Ops:
  0.6 7.9 %copy-start.1 = (s32[1,1,1,1536]{3,2,1,0:T(1,128)S(1)}, s32[1,1,1,1536]{3,2,1,0:T(1,128)}, u32[]{:S(2)}) copy-start(s32[1,1,1,1536]{3,2,1,0:T(1,128)} %param.13) | copy-start | bytes 18436
  0.6 10.4 %copy-start = (s32[1,1,3072]{2,1,0:T(1,128)S(1)}, s32[1,1,3072]{2,1,0:T(1,128)}, u32[]{:S(2)}) copy-start(s32[1,1,3072]{2,1,0:T(1,128)} %param.14) | copy-start | bytes 36868
  2.8 11.6 %collective-permute-start.2 = (f32[96,128]{1,0:T(8,128)S(1)}, f32[96,128]{1,0:T(8,128)S(1)}, u32[]{:S(2)}, u32[]{:S(2)}) collective-permute-start(f32[96,128]{1,0:T(8,128)S(1)} %get-tuple-element.30.refs_0_), channel_id=1, source_target_pairs={{0,4},{2,6},{4,0},{6,2},{1,5},{3,7},{5,1},{7,3},{8,12},{10,14},{12... | collective-permute-start | bytes 147464 | tf_op jit(solution)/shard_map/ppermute | solution.py:640
  7.0 7.5 %collective-permute-start.1 = (f32[96,128]{1,0:T(8,128)S(1)}, f32[96,128]{1,0:T(8,128)S(1)}, u32[]{:S(2)}, u32[]{:S(2)}) collective-permute-start(f32[96,128]{1,0:T(8,128)S(1)} %get-tuple-element.30.refs_0_), channel_id=1, source_target_pairs={{0,2},{2,0},{4,6},{6,4},{1,3},{3,1},{5,7},{7,5},{8,10},{10,8},{12,... | collective-permute-start | bytes 147464 | tf_op jit(solution)/shard_map/ppermute | solution.py:640
  8.5 5.9 %collective-permute-start.3 = (f32[96,128]{1,0:T(8,128)S(1)}, f32[96,128]{1,0:T(8,128)S(1)}, u32[]{:S(2)}, u32[]{:S(2)}) collective-permute-start(f32[96,128]{1,0:T(8,128)S(1)} %get-tuple-element.31), channel_id=1, source_target_pairs={{0,6},{2,4},{4,2},{6,0},{1,7},{3,5},{5,3},{7,1},{8,14},{10,12},{12... | collective-permute-start | bytes 147464 | tf_op jit(solution)/shard_map/ppermute | solution.py:640
  8.5 18.3 %copy-start.2 = (f32[3]{0:T(128)S(1)}, f32[3]{0:T(128)}, u32[]{:S(2)}) copy-start(f32[3]{0:T(128)} %refs_0_.1) | copy-start | bytes 40
  8.5 18.3 %copy-start.3 = (f32[3]{0:T(128)S(1)}, f32[3]{0:T(128)}, u32[]{:S(2)}) copy-start(f32[3]{0:T(128)} %refs_1_.1) | copy-start | bytes 40
  9.7 4.7 %collective-permute-start.4 = (f32[4,24,128]{2,1,0:T(8,128)S(1)}, f32[4,24,128]{2,1,0:T(8,128)S(1)}, u32[]{:S(2)}, u32[]{:S(2)}) collective-permute-start(f32[4,24,128]{2,1,0:T(8,128)S(1)} %get-tuple-element.34), channel_id=1, source_target_pairs={{0,1},{1,0},{2,3},{3,2},{4,5},{5,4},{6,7},{7,6},{8,9},{9,8},{10,11... | collective-permute-start | bytes 147464 | tf_op jit(solution)/shard_map/ppermute | solution.py:648
  9.7 1.3 %collective-permute-start = (f32[12,128]{1,0:T(8,128)S(1)}, f32[12,128]{1,0:T(8,128)S(1)}, u32[]{:S(2)}, u32[]{:S(2)}) collective-permute-start(f32[12,128]{1,0:T(8,128)S(1)} %get-tuple-element.29.refs_1_), channel_id=1, source_target_pairs={{0,1},{1,0},{2,3},{3,2},{4,5},{5,4},{6,7},{7,6},{8,9},{9,8},{10,11... | collective-permute-start | bytes 18440 | tf_op jit(solution)/shard_map/ppermute | solution.py:640
  14.7 8.6 %collective-permute-start.7 = (f32[392,128]{1,0:T(8,128)S(1)}, f32[392,128]{1,0:T(8,128)S(1)}, u32[]{:S(2)}, u32[]{:S(2)}) collective-permute-start(f32[392,128]{1,0:T(8,128)S(1)} %get-tuple-element.40), channel_id=1, source_target_pairs={{0,24},{8,16},{16,8},{24,0},{1,25},{9,17},{17,9},{25,1},{2,26},{10... | collective-permute-start | bytes 602120 | tf_op jit(solution)/shard_map/ppermute | solution.py:640
  17.2 7.9 %collective-permute-start.6 = (f32[392,128]{1,0:T(8,128)S(1)}, f32[392,128]{1,0:T(8,128)S(1)}, u32[]{:S(2)}, u32[]{:S(2)}) collective-permute-start(f32[392,128]{1,0:T(8,128)S(1)} %get-tuple-element.35.refs_9_), channel_id=1, source_target_pairs={{0,16},{8,24},{16,0},{24,8},{1,17},{9,25},{17,1},{25,9},{2,18},{10... | collective-permute-start | bytes 602120 | tf_op jit(solution)/shard_map/ppermute | solution.py:640
  17.7 7.5 %collective-permute-start.5 = (f32[392,128]{1,0:T(8,128)S(1)}, f32[392,128]{1,0:T(8,128)S(1)}, u32[]{:S(2)}, u32[]{:S(2)}) collective-permute-start(f32[392,128]{1,0:T(8,128)S(1)} %get-tuple-element.35.refs_9_), channel_id=1, source_target_pairs={{0,8},{8,0},{16,24},{24,16},{1,9},{9,1},{17,25},{25,17},{2,10},{10... | collective-permute-start | bytes 602120 | tf_op jit(solution)/shard_map/ppermute | solution.py:640
  18.2 7.4 %collective-permute-start.8 = (f32[392,128]{1,0:T(8,128)S(1)}, f32[392,128]{1,0:T(8,128)S(1)}, u32[]{:S(2)}, u32[]{:S(2)}) collective-permute-start(f32[392,128]{1,0:T(8,128)S(1)} %get-tuple-element.35.refs_9_), channel_id=1, source_target_pairs={{0,1},{1,0},{2,3},{3,2},{4,5},{5,4},{6,7},{7,6},{8,9},{9,8},{10,11... | collective-permute-start | bytes 602120 | tf_op jit(solution)/shard_map/ppermute | solution.py:640
  23.3 2.3 %collective-permute-start.11 = (f32[392,128]{1,0:T(8,128)S(1)}, f32[392,128]{1,0:T(8,128)S(1)}, u32[]{:S(2)}, u32[]{:S(2)}) collective-permute-start(f32[392,128]{1,0:T(8,128)S(1)} %collective-permute-done.7.refs_12_), channel_id=1, source_target_pairs={{0,1},{1,0},{2,3},{3,2},{4,5},{5,4},{6,7},{7,6},{8,9},{9,8},{10,11... | collective-permute-start | bytes 602120 | tf_op jit(solution)/shard_map/ppermute | solution.py:640
  25.0 1.4 %collective-permute-start.10 = (f32[392,128]{1,0:T(8,128)S(1)}, f32[392,128]{1,0:T(8,128)S(1)}, u32[]{:S(2)}, u32[]{:S(2)}) collective-permute-start(f32[392,128]{1,0:T(8,128)S(1)} %collective-permute-done.6.refs_11_), channel_id=1, source_target_pairs={{0,1},{1,0},{2,3},{3,2},{4,5},{5,4},{6,7},{7,6},{8,9},{9,8},{10,11... | collective-permute-start | bytes 602120 | tf_op jit(solution)/shard_map/ppermute | solution.py:640
  25.1 1.6 %collective-permute-start.9 = (f32[392,128]{1,0:T(8,128)S(1)}, f32[392,128]{1,0:T(8,128)S(1)}, u32[]{:S(2)}, u32[]{:S(2)}) collective-permute-start(f32[392,128]{1,0:T(8,128)S(1)} %collective-permute-done.5.refs_10_), channel_id=1, source_target_pairs={{0,1},{1,0},{2,3},{3,2},{4,5},{5,4},{6,7},{7,6},{8,9},{9,8},{10,11... | collective-permute-start | bytes 602120 | tf_op jit(solution)/shard_map/ppermute | solution.py:640
